TPU v7x, 128 devices: a whole 4x4x4 slice. The times are simulated.
128 devices in a mesh: cp: 64 (over z, y_lo, x, core), hd: 2 (over y_hi).
Axes of the slice: x: 4, y: 4 (y_hi: 2, y_lo: 2; y = y_hi * 2 + y_lo), z: 4, core: 2. Of those that a mesh axis runs over, the one named last changes fastest.
Arguments:
- query: bfloat16 [32768, 512], P('cp', 'hd'), may hold values from -6 to 6
- keys: bfloat16 [32768, 128], P('cp'), may hold values from -4 to 4
- values: bfloat16 [32768, 128], P('cp'), may hold values from -4 to 6
- grad_out: bfloat16 [32768, 512], P('cp', 'hd'), may hold values from -6 to 6
- doc_start: int32 [32768], P('cp'), may hold values from 0 to 32767, as said below
Outputs:
- grad_query: bfloat16 [32768, 512], P('cp', 'hd')
- grad_keys: bfloat16 [32768, 128], P('cp')
- grad_values: bfloat16 [32768, 128], P('cp')
Inputs may be any that keep to these rules, and one draw needn't show every extreme that they name: `doc_start`: documents are contiguous runs of tokens of at most 4096 tokens; no document crosses a multiple of 4096 tokens; the first 4096 tokens form one document; the last token forms a document of its own.
All inputs are finite; a program needn't handle non-finite values.
Results may differ from a plain program's by a relative error of at most 0.0075.
Values may be sent and summed in bfloat16 or wider, within the bound.
No kernel may reach another device: no remote copies, remote signals or barrier semaphores. Data moves between devices by JAX's collectives and lax.ppermute only.
A program may use at most 64 MiB of HBM per device.

v0:
```python
import math

import jax
import jax.numpy as jnp
from jax import lax
from jax.sharding import PartitionSpec as P

HDIM = 128
SPAN = 8


masked_score = -1e30


def passed_along(array, axis, by):
    length = lax.axis_size(axis)
    pairs = [(i, i + by) for i in range(length) if 0 <= i + by < length]
    return lax.ppermute(array, axis, pairs)


def shifted(array, axis, by):
    length = lax.axis_size(axis)
    return lax.ppermute(array, axis, [(i, (i + by) % length) for i in range(length)])


def key_mask(start_rows, query_base, key_base, row_count, key_width):
    query_pos = query_base + lax.iota(jnp.int32, row_count)
    key_pos = key_base + lax.iota(jnp.int32, key_width)
    inside = (key_pos[None, :] >= start_rows[:, None]) & (key_pos[None, :] <= query_pos[:, None])
    return inside & True


def stat_block(
    statistics, query_heads, grad_heads, start_rows, query_base, key_block, value_block, key_base
):
    row_count = query_heads.shape[0]
    key_width = min(512, key_block.shape[0])
    scaling = 1.0 / math.sqrt(query_heads.shape[2])
    running_max, running_sum, weighted = statistics
    allowed = key_mask(start_rows, query_base, key_base + 0, row_count, key_width)
    scores = (
        jnp.einsum("thd,kd->htk", query_heads, key_block, preferred_element_type=jnp.float32)
        * scaling
    )
    scores = jnp.where(allowed[None], scores, masked_score)
    new_max = jnp.maximum(running_max, jnp.max(scores, axis=-1))
    unnormed = jnp.where(allowed[None], jnp.exp(scores - new_max[..., None]), 0.0)
    grad_prob = jnp.einsum(
        "thd,kd->htk", grad_heads, value_block, preferred_element_type=jnp.float32
    )
    factor = jnp.exp(running_max - new_max)
    running_sum = running_sum * factor + jnp.sum(unnormed, axis=-1)
    weighted = weighted * factor + jnp.sum(unnormed * grad_prob, axis=-1)
    return (new_max, running_sum, weighted)


def grad_block(
    query_heads,
    grad_heads,
    log_norm,
    row_delta,
    start_rows,
    query_base,
    key_block,
    value_block,
    key_base,
):
    row_count = query_heads.shape[0]
    key_width = min(512, key_block.shape[0])
    scaling = 1.0 / math.sqrt(query_heads.shape[2])
    allowed = key_mask(start_rows, query_base, key_base + 0, row_count, key_width)
    scores = (
        jnp.einsum("thd,kd->htk", query_heads, key_block, preferred_element_type=jnp.float32)
        * scaling
    )
    probs = jnp.where(allowed[None], jnp.exp(scores - log_norm[..., None]), 0.0)
    grad_prob = jnp.einsum(
        "thd,kd->htk", grad_heads, value_block, preferred_element_type=jnp.float32
    )
    grad_score = (probs * (grad_prob - row_delta[..., None])).astype(jnp.bfloat16)
    probs_low = probs.astype(jnp.bfloat16)
    grad_query = jnp.einsum(
        "htk,kd->thd", grad_score, key_block, preferred_element_type=jnp.float32
    )
    key_terms = jnp.einsum(
        "htk,thd->kd", grad_score, query_heads, preferred_element_type=jnp.float32
    )
    value_terms = jnp.einsum(
        "htk,thd->kd", probs_low, grad_heads, preferred_element_type=jnp.float32
    )
    return (grad_query, key_terms, value_terms)


def body(query, keys, values, grad_out, doc_start):
    row_count = query.shape[0]
    head_count = query.shape[1] // HDIM
    scaling = 1.0 / math.sqrt(HDIM)
    position = lax.axis_index("cp")
    query_heads = query.reshape(row_count, head_count, HDIM)
    grad_heads = grad_out.reshape(row_count, head_count, HDIM)
    own_base = position * row_count
    row_zeros = jnp.zeros((head_count, row_count), jnp.float32)
    statistics = (
        jnp.full((head_count, row_count), masked_score, jnp.float32),
        row_zeros,
        row_zeros,
    )
    key_acc = jnp.zeros((row_count, HDIM), jnp.float32)
    value_acc = jnp.zeros((row_count, HDIM), jnp.float32)
    key_cur, value_cur = (keys, values)
    held_blocks = []
    for offset in range(SPAN):
        held_blocks.append((key_cur, value_cur))
        statistics = stat_block(
            statistics,
            query_heads,
            grad_heads,
            doc_start,
            own_base,
            key_cur,
            value_cur,
            (position - offset) * row_count,
        )
        if offset + 1 < SPAN:
            key_cur, value_cur = passed_along((key_cur, value_cur), "cp", 1)
    running_max, running_sum, weighted = statistics
    log_norm = running_max + jnp.log(running_sum)
    row_delta = weighted / running_sum
    grad_query = jnp.zeros((row_count, head_count, HDIM), jnp.float32)
    key_cur, value_cur = (keys, values)
    for offset in range(SPAN):
        part_query, part_key, part_value = grad_block(
            query_heads,
            grad_heads,
            log_norm,
            row_delta,
            doc_start,
            own_base,
            key_cur,
            value_cur,
            (position - offset) * row_count,
        )
        grad_query = grad_query + part_query
        key_acc = key_acc + part_key
        value_acc = value_acc + part_value
        if offset + 1 < SPAN:
            key_cur, value_cur = passed_along((key_cur, value_cur), "cp", 1)
            key_acc, value_acc = shifted((key_acc, value_acc), "cp", 1)
    key_acc, value_acc = shifted((key_acc, value_acc), "cp", 1 - SPAN)
    key_sum, value_sum = lax.psum((key_acc, value_acc), "hd")
    grad_query_out = (
        (grad_query * scaling).astype(jnp.bfloat16).reshape(row_count, head_count * HDIM)
    )
    return (
        grad_query_out,
        (key_sum * scaling).astype(jnp.bfloat16),
        value_sum.astype(jnp.bfloat16),
    )


def solution(mesh):
    in_specs = (P("cp", "hd"), P("cp", None), P("cp", None), P("cp", "hd"), P("cp"))
    out_specs = (P("cp", "hd"), P("cp", None), P("cp", None))
    return jax.shard_map(body, mesh=mesh, in_specs=in_specs, out_specs=out_specs, check_vma=False)
```

profile of v0, /device:TPU:0, one launch (start us, length us, event | category | flops | bytes accessed | tf_op | source)
XLA Modules:
  0.0 208.0 jit_solution(8209712694214799812)
XLA Ops:
  7.2 1.4 collective-permute-start
  8.7 4.2 %collective-permute-start.7 = (bf16[512,128]{1,0:T(8,128)(2,1)}, bf16[512,128]{1,0:T(8,128)(2,1)S(1)}, u32[]{:S(2)}, u32[]{:S(2)}) collective-permute-start(bf16[512,128]{1,0:T(8,128)(2,1)} %param.7), channel_id=1, source_target_pairs={{0,2},{2,4},{4,6},{6,8},{8,10},{10,12},{12,14},{14,16},{16,18},{18... | collective-permute-start | bytes 393224 | tf_op jit(solution)/shard_map/ppermute | solution.py:18
  13.0 2.7 %compare_and_fusion.7 = (pred[512,512]{0,1:T(8,128)(4,1)S(1)}, pred[512,512]{0,1:T(8,128)(4,1)S(1)}, pred[512,512]{0,1:T(8,128)(4,1)S(1)}, pred[512,512]{0,1:T(8...) fusion(s32[512]{0:T(512)S(1)} %get-tuple-element.79, ...), kind=kLoop, calls=%fused_computation.162 | loop fusion | flops 6291456 | bytes 2115584 | tf_op jit(solution)/shard_map/and | solution.py:29
  15.7 0.6 fusion.40
  16.3 1.9 collective-permute-start.1
  18.2 0.6 fusion.41
  18.8 3.5 %collective-permute-start.8 = (bf16[512,128]{1,0:T(8,128)(2,1)S(1)}, bf16[512,128]{1,0:T(8,128)(2,1)S(1)}, u32[]{:S(2)}, u32[]{:S(2)}) collective-permute-start(bf16[512,128]{1,0:T(8,128)(2,1)S(1)} %collective-permute-done.7), channel_id=1, source_target_pairs={{0,2},{2,4},{4,6},{6,8},{8,10},{10,12},{12,14},{14,16},{16,18},{18... | collective-permute-start | bytes 393224 | tf_op jit(solution)/shard_map/ppermute | solution.py:18
  22.3 1.9 collective-permute-start.2
  24.2 0.6 fusion.42
  24.8 3.8 %collective-permute-start.9 = (bf16[512,128]{1,0:T(8,128)(2,1)S(1)}, bf16[512,128]{1,0:T(8,128)(2,1)S(1)}, u32[]{:S(2)}, u32[]{:S(2)}) collective-permute-start(bf16[512,128]{1,0:T(8,128)(2,1)S(1)} %collective-permute-done.8), channel_id=1, source_target_pairs={{0,2},{2,4},{4,6},{6,8},{8,10},{10,12},{12,14},{14,16},{16,18},{18... | collective-permute-start | bytes 393224 | tf_op jit(solution)/shard_map/ppermute | solution.py:18
  28.6 1.9 collective-permute-start.3
  30.5 0.6 fusion.43
  31.1 3.7 %collective-permute-start.10 = (bf16[512,128]{1,0:T(8,128)(2,1)S(1)}, bf16[512,128]{1,0:T(8,128)(2,1)S(1)}, u32[]{:S(2)}, u32[]{:S(2)}) collective-permute-start(bf16[512,128]{1,0:T(8,128)(2,1)S(1)} %collective-permute-done.9), channel_id=1, source_target_pairs={{0,2},{2,4},{4,6},{6,8},{8,10},{10,12},{12,14},{14,16},{16,18},{18... | collective-permute-start | bytes 393224 | tf_op jit(solution)/shard_map/ppermute | solution.py:18
  34.9 1.9 collective-permute-start.4
  36.8 0.6 fusion.44
  37.4 3.8 %collective-permute-start.11 = (bf16[512,128]{1,0:T(8,128)(2,1)S(1)}, bf16[512,128]{1,0:T(8,128)(2,1)S(1)}, u32[]{:S(2)}, u32[]{:S(2)}) collective-permute-start(bf16[512,128]{1,0:T(8,128)(2,1)S(1)} %collective-permute-done.10), channel_id=1, source_target_pairs={{0,2},{2,4},{4,6},{6,8},{8,10},{10,12},{12,14},{14,16},{16,18},{18... | collective-permute-start | bytes 393224 | tf_op jit(solution)/shard_map/ppermute | solution.py:18
  41.2 1.9 collective-permute-start.5
  43.1 0.6 fusion.45
  43.7 4.8 %collective-permute-start.12 = (bf16[512,128]{1,0:T(8,128)(2,1)S(1)}, bf16[512,128]{1,0:T(8,128)(2,1)S(1)}, u32[]{:S(2)}, u32[]{:S(2)}) collective-permute-start(bf16[512,128]{1,0:T(8,128)(2,1)S(1)} %collective-permute-done.11), channel_id=1, source_target_pairs={{0,2},{2,4},{4,6},{6,8},{8,10},{10,12},{12,14},{14,16},{16,18},{18... | collective-permute-start | bytes 393224 | tf_op jit(solution)/shard_map/ppermute | solution.py:18
  48.5 1.9 collective-permute-start.6
  50.4 0.6 fusion.46
  51.0 6.2 %collective-permute-start.13 = (bf16[512,128]{1,0:T(8,128)(2,1)S(1)}, bf16[512,128]{1,0:T(8,128)(2,1)S(1)}, u32[]{:S(2)}, u32[]{:S(2)}) collective-permute-start(bf16[512,128]{1,0:T(8,128)(2,1)S(1)} %collective-permute-done.12), channel_id=1, source_target_pairs={{0,2},{2,4},{4,6},{6,8},{8,10},{10,12},{12,14},{14,16},{16,18},{18... | collective-permute-start | bytes 393224 | tf_op jit(solution)/shard_map/ppermute | solution.py:18
  57.2 0.6 fusion.47
  57.8 0.9 fusion.21
  58.7 0.9 fusion.3
  59.7 0.9 fusion.6
  60.6 0.9 fusion.9
  61.6 2.1 %fusion.12 = (f32[2,512]{1,0:T(2,128)S(1)}, f32[2,512]{1,0:T(2,128)S(1)}, f32[512,512,2]{1,0,2:T(8,128)}) fusion(f32[512,512,2]{1,0,2:T(8,128)S(1)} %get-tuple-element.57, f32[2,512]{1,0:T(2,128)S(1)} %get-tuple-element.28, pred[512,512]{0,1:T(8,128)(4,1)S(1)} %get-tuple-element.42, bf16[512,128]{1,0:T(8,128)(2,1)S(1)} %collective-permute-done.9, ...), kind=kOutput, calls=%fused_computation.22 | convolution fusion | flops 137885696 | bytes 4861952 | tf_op jit(solution)/shard_map/thd,kd->htk/dot_general | solution.py:48
  63.7 2.1 %fusion.15 = (f32[2,512]{1,0:T(2,128)S(1)}, f32[2,512]{1,0:T(2,128)S(1)}, f32[512,512,2]{1,0,2:T(8,128)}) fusion(f32[512,512,2]{1,0,2:T(8,128)S(1)} %get-tuple-element.59, f32[2,512]{1,0:T(2,128)S(1)} %get-tuple-element.29, pred[512,512]{0,1:T(8,128)(4,1)S(1)} %get-tuple-element.41, bf16[512,128]{1,0:T(8,128)(2,1)S(1)} %collective-permute-done.8, ...), kind=kOutput, calls=%fused_computation.27 | convolution fusion | flops 137885696 | bytes 4861952 | tf_op jit(solution)/shard_map/thd,kd->htk/dot_general | solution.py:48
  65.8 2.2 %fusion.18 = (f32[2,512]{1,0:T(2,128)S(1)}, f32[2,512]{1,0:T(2,128)S(1)}, f32[512,512,2]{1,0,2:T(8,128)}) fusion(f32[512,512,2]{1,0,2:T(8,128)S(1)} %get-tuple-element.61, f32[2,512]{1,0:T(2,128)S(1)} %get-tuple-element.30, pred[512,512]{0,1:T(8,128)(4,1)S(1)} %get-tuple-element.47, bf16[512,128]{1,0:T(8,128)(2,1)S(1)} %collective-permute-done.7, ...), kind=kOutput, calls=%fused_computation.32 | convolution fusion | flops 137885696 | bytes 4861952 | tf_op jit(solution)/shard_map/thd,kd->htk/dot_general | solution.py:48
  68.0 2.1 %fusion = (f32[2,512]{1,0:T(2,128)S(1)}, f32[2,512]{1,0:T(2,128)S(1)}, f32[512,512,2]{1,0,2:T(8,128)}) fusion(f32[512,512,2]{1,0,2:T(8,128)S(1)} %get-tuple-element.49, f32[2,512]{1,0:T(2,128)S(1)} %get-tuple-element.24, pred[512,512]{0,1:T(8,128)(4,1)S(1)} %get-tuple-element.46, bf16[512,128]{1,0:T(8,128)(2,1)S(1)} %collective-permute-done.13, ...), kind=kOutput, calls=%fused_computation.2 | convolution fusion | flops 137885696 | bytes 4861952 | tf_op jit(solution)/shard_map/thd,kd->htk/dot_general | solution.py:48
  70.2 2.0 fusion.5
  72.6 1.1 convolution_bitcast_fusion.15
  73.8 1.2 convolution_bitcast_fusion.7
  75.0 5.5 %fusion.2 = (bf16[2,512,512]{1,2,0:T(8,128)(2,1)S(1)}, bf16[2,512,512]{1,2,0:T(8,128)(2,1)S(1)}, bf16[2,512,512]{1,2,0:T(8,128)(2,1)S(1)}, bf16[2,512,512]{1,2,0:T(8,128)(2,1)S(1)}, bf16[2,512,512]{1,2,0:T(8,128)(2,1)S(1)}) fusion(f32[512,512,2]{1,0,2:T(8,128)} %get-tuple-element.64, f32[512,512,2]{1,0,2:T(8,128)S(1)} %get-tuple-element.49, ...), kind=kLoop, calls=%fused_computation.4 | loop fusion | flops 15728640 | bytes 27533312 | tf_op jit(solution)/shard_map/convert_element_type | solution.py:80
  83.2 4.0 %collective-permute-start.22 = (f32[512,128]{1,0:T(8,128)S(1)}, f32[512,128]{1,0:T(8,128)S(1)}, u32[]{:S(2)}, u32[]{:S(2)}) collective-permute-start(f32[512,128]{1,0:T(8,128)S(1)} %copy-done.27), channel_id=1, source_target_pairs={{0,2},{2,4},{4,6},{6,8},{8,10},{10,12},{12,14},{14,16},{16,18},{18... | collective-permute-start | bytes 786440 | tf_op jit(solution)/shard_map/ppermute | solution.py:23
  89.8 1.4 fusion.66
  91.3 2.0 collective-permute-done.22
  93.3 0.6 fusion.67
  93.9 2.0 collective-permute-start.23
  96.5 4.8 %collective-permute-done.15 = f32[512,128]{1,0:T(8,128)S(1)} collective-permute-done((f32[512,128]{1,0:T(8,128)S(1)}, f32[512,128]{1,0:T(8,128)S(1)}, u32[]{:S(2)}, u32[]{:S(2)}) %collective-permute-start.15) | collective-permute-done | bytes 262176 | tf_op jit(solution)/shard_map/ppermute | solution.py:23
  101.4 2.7 %collective-permute-done.23 = f32[512,128]{1,0:T(8,128)S(1)} collective-permute-done((f32[512,128]{1,0:T(8,128)S(1)}, f32[512,128]{1,0:T(8,128)S(1)}, u32[]{:S(2)}, u32[]{:S(2)}) %collective-permute-start.23) | collective-permute-done | bytes 262176 | tf_op jit(solution)/shard_map/ppermute | solution.py:23
  104.2 0.5 convolution_bitcast_fusion.4
  104.8 6.6 %collective-permute-done.16 = f32[512,128]{1,0:T(8,128)S(1)} collective-permute-done((f32[512,128]{1,0:T(8,128)S(1)}, f32[512,128]{1,0:T(8,128)S(1)}, u32[]{:S(2)}, u32[]{:S(2)}) %collective-permute-start.16) | collective-permute-done | bytes 262176 | tf_op jit(solution)/shard_map/ppermute | solution.py:23
  111.5 2.7 %collective-permute-done.24 = f32[512,128]{1,0:T(8,128)S(1)} collective-permute-done((f32[512,128]{1,0:T(8,128)S(1)}, f32[512,128]{1,0:T(8,128)S(1)}, u32[]{:S(2)}, u32[]{:S(2)}) %collective-permute-start.24) | collective-permute-done | bytes 262176 | tf_op jit(solution)/shard_map/ppermute | solution.py:23
  114.4 0.5 convolution_bitcast_fusion.3
  114.9 6.6 %collective-permute-done.17 = f32[512,128]{1,0:T(8,128)S(1)} collective-permute-done((f32[512,128]{1,0:T(8,128)S(1)}, f32[512,128]{1,0:T(8,128)S(1)}, u32[]{:S(2)}, u32[]{:S(2)}) %collective-permute-start.17) | collective-permute-done | bytes 262176 | tf_op jit(solution)/shard_map/ppermute | solution.py:23
  121.6 2.7 %collective-permute-done.25 = f32[512,128]{1,0:T(8,128)S(1)} collective-permute-done((f32[512,128]{1,0:T(8,128)S(1)}, f32[512,128]{1,0:T(8,128)S(1)}, u32[]{:S(2)}, u32[]{:S(2)}) %collective-permute-start.25) | collective-permute-done | bytes 262176 | tf_op jit(solution)/shard_map/ppermute | solution.py:23
  124.5 0.5 convolution_bitcast_fusion.2
  125.0 6.6 %collective-permute-done.18 = f32[512,128]{1,0:T(8,128)S(1)} collective-permute-done((f32[512,128]{1,0:T(8,128)S(1)}, f32[512,128]{1,0:T(8,128)S(1)}, u32[]{:S(2)}, u32[]{:S(2)}) %collective-permute-start.18) | collective-permute-done | bytes 262176 | tf_op jit(solution)/shard_map/ppermute | solution.py:23
  131.8 2.7 %collective-permute-done.26 = f32[512,128]{1,0:T(8,128)S(1)} collective-permute-done((f32[512,128]{1,0:T(8,128)S(1)}, f32[512,128]{1,0:T(8,128)S(1)}, u32[]{:S(2)}, u32[]{:S(2)}) %collective-permute-start.26) | collective-permute-done | bytes 262176 | tf_op jit(solution)/shard_map/ppermute | solution.py:23
  134.9 0.5 convolution_bitcast_fusion.1
  135.4 6.4 %collective-permute-done.19 = f32[512,128]{1,0:T(8,128)S(1)} collective-permute-done((f32[512,128]{1,0:T(8,128)S(1)}, f32[512,128]{1,0:T(8,128)S(1)}, u32[]{:S(2)}, u32[]{:S(2)}) %collective-permute-start.19) | collective-permute-done | bytes 262176 | tf_op jit(solution)/shard_map/ppermute | solution.py:23
  141.9 3.0 %collective-permute-done.27 = f32[512,128]{1,0:T(8,128)S(1)} collective-permute-done((f32[512,128]{1,0:T(8,128)S(1)}, f32[512,128]{1,0:T(8,128)S(1)}, u32[]{:S(2)}, u32[]{:S(2)}) %collective-permute-start.27) | collective-permute-done | bytes 262176 | tf_op jit(solution)/shard_map/ppermute | solution.py:23
  145.0 0.5 convolution_bitcast_fusion
  145.5 6.4 %collective-permute-done.20 = f32[512,128]{1,0:T(8,128)S(1)} collective-permute-done((f32[512,128]{1,0:T(8,128)S(1)}, f32[512,128]{1,0:T(8,128)S(1)}, u32[]{:S(2)}, u32[]{:S(2)}) %collective-permute-start.20) | collective-permute-done | bytes 262176 | tf_op jit(solution)/shard_map/ppermute | solution.py:23
  152.0 3.0 %collective-permute-done.28 = f32[512,128]{1,0:T(8,128)S(1)} collective-permute-done((f32[512,128]{1,0:T(8,128)S(1)}, f32[512,128]{1,0:T(8,128)S(1)}, u32[]{:S(2)}, u32[]{:S(2)}) %collective-permute-start.28) | collective-permute-done | bytes 262176 | tf_op jit(solution)/shard_map/ppermute | solution.py:23
  155.5 0.8 copy.56
  156.3 2.7 %collective-permute-done.21 = f32[512,128]{1,0:T(8,128)S(1)} collective-permute-done((f32[512,128]{1,0:T(8,128)S(1)}, f32[512,128]{1,0:T(8,128)S(1)}, u32[]{:S(2)}, u32[]{:S(2)}) %collective-permute-start.21) | collective-permute-done | bytes 262176 | tf_op jit(solution)/shard_map/ppermute | solution.py:23
  159.0 0.7 copy-done.14
  159.7 2.4 %collective-permute-done.29 = f32[512,128]{1,0:T(8,128)S(1)} collective-permute-done((f32[512,128]{1,0:T(8,128)S(1)}, f32[512,128]{1,0:T(8,128)S(1)}, u32[]{:S(2)}, u32[]{:S(2)}) %collective-permute-start.29) | collective-permute-done | bytes 262176 | tf_op jit(solution)/shard_map/ppermute | solution.py:23
  162.1 14.8 %all-reduce.4 = bf16[512,128]{1,0:T(8,128)(2,1)} all-reduce(f32[512,128]{1,0:T(8,128)S(1)} %collective-permute-done.29), channel_id=1, replica_groups=mesh['cp'=64,'hd'=2] {'hd'}, use_global_device_ids=true, to_apply=%region_25.26 | all-reduce | flops 65536 | bytes 393216 | tf_op jit(solution)/shard_map/psum | solution.py:150
  176.9 22.6 %all-reduce.3.cloned.1.call-done = f32[512,128]{1,0:T(8,128)} async-done(((f32[512,128]{1,0:T(8,128)}), f32[512,128]{1,0:T(8,128)}) %all-reduce.3.cloned.1.call-update) | async-done | bytes 262160 | tf_op jit(solution)/shard_map/psum | solution.py:150
  199.6 1.6 multiply_convert_fusion
  (122 shorter events, 8.3 us)
Async XLA Ops:
  7.2 50.7 %copy-start = (bf16[512,256]{1,0:T(8,128)(2,1)S(1)}, bf16[512,256]{1,0:T(8,128)(2,1)}, u32[]{:S(2)}) copy-start(bf16[512,256]{1,0:T(8,128)(2,1)} %param.8) | copy-start | bytes 786436
  7.2 8.5 %copy-start.23 = (bf16[512,128]{1,0:T(8,128)(2,1)S(1)}, bf16[512,128]{1,0:T(8,128)(2,1)}, u32[]{:S(2)}) copy-start(bf16[512,128]{1,0:T(8,128)(2,1)} %param.6) | copy-start | bytes 393220
  7.2 8.5 %copy-start.1 = (bf16[512,256]{1,0:T(8,128)(2,1)S(1)}, bf16[512,256]{1,0:T(8,128)(2,1)}, u32[]{:S(2)}) copy-start(bf16[512,256]{1,0:T(8,128)(2,1)} %param.5) | copy-start | bytes 786436
  7.2 192.3 %all-reduce.3.cloned.1.call-start = ((), (), s32[]{:S(2)}) async-start(), calls=%async_computation | async-start | bytes 524288 | tf_op jit(solution)/shard_map/psum | solution.py:150
  7.2 9.0 %collective-permute-start = (bf16[512,128]{1,0:T(8,128)(2,1)}, bf16[512,128]{1,0:T(8,128)(2,1)S(1)}, u32[]{:S(2)}, u32[]{:S(2)}) collective-permute-start(bf16[512,128]{1,0:T(8,128)(2,1)} %param.6), channel_id=1, source_target_pairs={{0,2},{2,4},{4,6},{6,8},{8,10},{10,12},{12,14},{14,16},{16,18},{18... | collective-permute-start | bytes 393224 | tf_op jit(solution)/shard_map/ppermute | solution.py:18
  8.7 10.1 %collective-permute-start.7 = (bf16[512,128]{1,0:T(8,128)(2,1)}, bf16[512,128]{1,0:T(8,128)(2,1)S(1)}, u32[]{:S(2)}, u32[]{:S(2)}) collective-permute-start(bf16[512,128]{1,0:T(8,128)(2,1)} %param.7), channel_id=1, source_target_pairs={{0,2},{2,4},{4,6},{6,8},{8,10},{10,12},{12,14},{14,16},{16,18},{18... | collective-permute-start | bytes 393224 | tf_op jit(solution)/shard_map/ppermute | solution.py:18
  15.6 45.0 %copy-start.6 = (pred[512,512]{0,1:T(8,128)(4,1)}, pred[512,512]{0,1:T(8,128)(4,1)S(1)}, u32[]{:S(2)}) copy-start(pred[512,512]{0,1:T(8,128)(4,1)S(1)} %get-tuple-element.43) | copy-start | bytes 786436
  15.7 45.9 %copy-start.8 = (pred[512,512]{0,1:T(8,128)(4,1)}, pred[512,512]{0,1:T(8,128)(4,1)S(1)}, u32[]{:S(2)}) copy-start(pred[512,512]{0,1:T(8,128)(4,1)S(1)} %get-tuple-element.42) | copy-start | bytes 786436
  15.7 48.0 %copy-start.10 = (pred[512,512]{0,1:T(8,128)(4,1)}, pred[512,512]{0,1:T(8,128)(4,1)S(1)}, u32[]{:S(2)}) copy-start(pred[512,512]{0,1:T(8,128)(4,1)S(1)} %get-tuple-element.41) | copy-start | bytes 786436
  15.7 50.1 %copy-start.12 = (pred[512,512]{0,1:T(8,128)(4,1)}, pred[512,512]{0,1:T(8,128)(4,1)S(1)}, u32[]{:S(2)}) copy-start(pred[512,512]{0,1:T(8,128)(4,1)S(1)} %get-tuple-element.47) | copy-start | bytes 786436
  15.7 54.5 %copy-start.2 = (pred[512,512]{0,1:T(8,128)(4,1)}, pred[512,512]{0,1:T(8,128)(4,1)S(1)}, u32[]{:S(2)}) copy-start(pred[512,512]{0,1:T(8,128)(4,1)S(1)} %get-tuple-element.45) | copy-start | bytes 786436
  15.7 54.5 %copy-start.4 = (pred[512,512]{0,1:T(8,128)(4,1)}, pred[512,512]{0,1:T(8,128)(4,1)S(1)}, u32[]{:S(2)}) copy-start(pred[512,512]{0,1:T(8,128)(4,1)S(1)} %get-tuple-element.44) | copy-start | bytes 786436
  16.3 6.0 %collective-permute-start.1 = (bf16[512,128]{1,0:T(8,128)(2,1)S(1)}, bf16[512,128]{1,0:T(8,128)(2,1)S(1)}, u32[]{:S(2)}, u32[]{:S(2)}) collective-permute-start(bf16[512,128]{1,0:T(8,128)(2,1)S(1)} %collective-permute-done), channel_id=1, source_target_pairs={{0,2},{2,4},{4,6},{6,8},{8,10},{10,12},{12,14},{14,16},{16,18},{18... | collective-permute-start | bytes 393224 | tf_op jit(solution)/shard_map/ppermute | solution.py:18
  18.8 6.0 %collective-permute-start.8 = (bf16[512,128]{1,0:T(8,128)(2,1)S(1)}, bf16[512,128]{1,0:T(8,128)(2,1)S(1)}, u32[]{:S(2)}, u32[]{:S(2)}) collective-permute-start(bf16[512,128]{1,0:T(8,128)(2,1)S(1)} %collective-permute-done.7), channel_id=1, source_target_pairs={{0,2},{2,4},{4,6},{6,8},{8,10},{10,12},{12,14},{14,16},{16,18},{18... | collective-permute-start | bytes 393224 | tf_op jit(solution)/shard_map/ppermute | solution.py:18
  22.3 6.3 %collective-permute-start.2 = (bf16[512,128]{1,0:T(8,128)(2,1)S(1)}, bf16[512,128]{1,0:T(8,128)(2,1)S(1)}, u32[]{:S(2)}, u32[]{:S(2)}) collective-permute-start(bf16[512,128]{1,0:T(8,128)(2,1)S(1)} %collective-permute-done.1), channel_id=1, source_target_pairs={{0,2},{2,4},{4,6},{6,8},{8,10},{10,12},{12,14},{14,16},{16,18},{18... | collective-permute-start | bytes 393224 | tf_op jit(solution)/shard_map/ppermute | solution.py:18
  24.8 6.3 %collective-permute-start.9 = (bf16[512,128]{1,0:T(8,128)(2,1)S(1)}, bf16[512,128]{1,0:T(8,128)(2,1)S(1)}, u32[]{:S(2)}, u32[]{:S(2)}) collective-permute-start(bf16[512,128]{1,0:T(8,128)(2,1)S(1)} %collective-permute-done.8), channel_id=1, source_target_pairs={{0,2},{2,4},{4,6},{6,8},{8,10},{10,12},{12,14},{14,16},{16,18},{18... | collective-permute-start | bytes 393224 | tf_op jit(solution)/shard_map/ppermute | solution.py:18
  28.6 8.8 %copy-start.15 = (bf16[512,128]{1,0:T(8,128)(2,1)}, bf16[512,128]{1,0:T(8,128)(2,1)S(1)}, u32[]{:S(2)}) copy-start(bf16[512,128]{1,0:T(8,128)(2,1)S(1)} %collective-permute-done.2) | copy-start | bytes 393220
  28.6 6.3 %collective-permute-start.3 = (bf16[512,128]{1,0:T(8,128)(2,1)S(1)}, bf16[512,128]{1,0:T(8,128)(2,1)S(1)}, u32[]{:S(2)}, u32[]{:S(2)}) collective-permute-start(bf16[512,128]{1,0:T(8,128)(2,1)S(1)} %collective-permute-done.2), channel_id=1, source_target_pairs={{0,2},{2,4},{4,6},{6,8},{8,10},{10,12},{12,14},{14,16},{16,18},{18... | collective-permute-start | bytes 393224 | tf_op jit(solution)/shard_map/ppermute | solution.py:18
  31.1 6.3 %collective-permute-start.10 = (bf16[512,128]{1,0:T(8,128)(2,1)S(1)}, bf16[512,128]{1,0:T(8,128)(2,1)S(1)}, u32[]{:S(2)}, u32[]{:S(2)}) collective-permute-start(bf16[512,128]{1,0:T(8,128)(2,1)S(1)} %collective-permute-done.9), channel_id=1, source_target_pairs={{0,2},{2,4},{4,6},{6,8},{8,10},{10,12},{12,14},{14,16},{16,18},{18... | collective-permute-start | bytes 393224 | tf_op jit(solution)/shard_map/ppermute | solution.py:18
  34.9 8.8 %copy-start.17 = (bf16[512,128]{1,0:T(8,128)(2,1)}, bf16[512,128]{1,0:T(8,128)(2,1)S(1)}, u32[]{:S(2)}) copy-start(bf16[512,128]{1,0:T(8,128)(2,1)S(1)} %collective-permute-done.3) | copy-start | bytes 393220
  34.9 6.3 %collective-permute-start.4 = (bf16[512,128]{1,0:T(8,128)(2,1)S(1)}, bf16[512,128]{1,0:T(8,128)(2,1)S(1)}, u32[]{:S(2)}, u32[]{:S(2)}) collective-permute-start(bf16[512,128]{1,0:T(8,128)(2,1)S(1)} %collective-permute-done.3), channel_id=1, source_target_pairs={{0,2},{2,4},{4,6},{6,8},{8,10},{10,12},{12,14},{14,16},{16,18},{18... | collective-permute-start | bytes 393224 | tf_op jit(solution)/shard_map/ppermute | solution.py:18
  37.4 6.3 %collective-permute-start.11 = (bf16[512,128]{1,0:T(8,128)(2,1)S(1)}, bf16[512,128]{1,0:T(8,128)(2,1)S(1)}, u32[]{:S(2)}, u32[]{:S(2)}) collective-permute-start(bf16[512,128]{1,0:T(8,128)(2,1)S(1)} %collective-permute-done.10), channel_id=1, source_target_pairs={{0,2},{2,4},{4,6},{6,8},{8,10},{10,12},{12,14},{14,16},{16,18},{18... | collective-permute-start | bytes 393224 | tf_op jit(solution)/shard_map/ppermute | solution.py:18
  41.2 9.8 %copy-start.19 = (bf16[512,128]{1,0:T(8,128)(2,1)}, bf16[512,128]{1,0:T(8,128)(2,1)S(1)}, u32[]{:S(2)}) copy-start(bf16[512,128]{1,0:T(8,128)(2,1)S(1)} %collective-permute-done.4) | copy-start | bytes 393220
  41.2 7.3 %collective-permute-start.5 = (bf16[512,128]{1,0:T(8,128)(2,1)S(1)}, bf16[512,128]{1,0:T(8,128)(2,1)S(1)}, u32[]{:S(2)}, u32[]{:S(2)}) collective-permute-start(bf16[512,128]{1,0:T(8,128)(2,1)S(1)} %collective-permute-done.4), channel_id=1, source_target_pairs={{0,2},{2,4},{4,6},{6,8},{8,10},{10,12},{12,14},{14,16},{16,18},{18... | collective-permute-start | bytes 393224 | tf_op jit(solution)/shard_map/ppermute | solution.py:18
  43.7 7.4 %collective-permute-start.12 = (bf16[512,128]{1,0:T(8,128)(2,1)S(1)}, bf16[512,128]{1,0:T(8,128)(2,1)S(1)}, u32[]{:S(2)}, u32[]{:S(2)}) collective-permute-start(bf16[512,128]{1,0:T(8,128)(2,1)S(1)} %collective-permute-done.11), channel_id=1, source_target_pairs={{0,2},{2,4},{4,6},{6,8},{8,10},{10,12},{12,14},{14,16},{16,18},{18... | collective-permute-start | bytes 393224 | tf_op jit(solution)/shard_map/ppermute | solution.py:18
  48.5 9.3 %copy-start.21 = (bf16[512,128]{1,0:T(8,128)(2,1)}, bf16[512,128]{1,0:T(8,128)(2,1)S(1)}, u32[]{:S(2)}) copy-start(bf16[512,128]{1,0:T(8,128)(2,1)S(1)} %collective-permute-done.5) | copy-start | bytes 393220
  48.5 8.7 %collective-permute-start.6 = (bf16[512,128]{1,0:T(8,128)(2,1)S(1)}, bf16[512,128]{1,0:T(8,128)(2,1)S(1)}, u32[]{:S(2)}, u32[]{:S(2)}) collective-permute-start(bf16[512,128]{1,0:T(8,128)(2,1)S(1)} %collective-permute-done.5), channel_id=1, source_target_pairs={{0,2},{2,4},{4,6},{6,8},{8,10},{10,12},{12,14},{14,16},{16,18},{18... | collective-permute-start | bytes 393224 | tf_op jit(solution)/shard_map/ppermute | solution.py:18
  51.0 6.8 %copy-start.28 = (bf16[512,128]{1,0:T(8,128)(2,1)S(1)}, bf16[512,128]{1,0:T(8,128)(2,1)}, u32[]{:S(2)}) copy-start(bf16[512,128]{1,0:T(8,128)(2,1)} %param.7) | copy-start | bytes 393220
  51.0 16.9 %collective-permute-start.13 = (bf16[512,128]{1,0:T(8,128)(2,1)S(1)}, bf16[512,128]{1,0:T(8,128)(2,1)S(1)}, u32[]{:S(2)}, u32[]{:S(2)}) collective-permute-start(bf16[512,128]{1,0:T(8,128)(2,1)S(1)} %collective-permute-done.12), channel_id=1, source_target_pairs={{0,2},{2,4},{4,6},{6,8},{8,10},{10,12},{12,14},{14,16},{16,18},{18... | collective-permute-start | bytes 393224 | tf_op jit(solution)/shard_map/ppermute | solution.py:18
  57.2 1.5 copy-start.25
  70.2 2.0 copy-start.24
  75.0 14.8 %collective-permute-start.14 = (f32[512,128]{1,0:T(8,128)}, f32[512,128]{1,0:T(8,128)}, u32[]{:S(2)}, u32[]{:S(2)}) collective-permute-start(f32[512,128]{1,0:T(8,128)} %convolution_bitcast_fusion.15), channel_id=1, source_target_pairs={{0,2},{2,4},{4,6},{6,8},{8,10},{10,12},{12,14},{14,16},{16,18},{18... | collective-permute-start | bytes 786440 | tf_op jit(solution)/shard_map/ppermute | solution.py:23
  81.9 1.3 copy-start.27
  83.2 10.1 %collective-permute-start.22 = (f32[512,128]{1,0:T(8,128)S(1)}, f32[512,128]{1,0:T(8,128)S(1)}, u32[]{:S(2)}, u32[]{:S(2)}) collective-permute-start(f32[512,128]{1,0:T(8,128)S(1)} %copy-done.27), channel_id=1, source_target_pairs={{0,2},{2,4},{4,6},{6,8},{8,10},{10,12},{12,14},{14,16},{16,18},{18... | collective-permute-start | bytes 786440 | tf_op jit(solution)/shard_map/ppermute | solution.py:23
  87.2 0.9 copy-start.16
  87.6 0.9 copy-start.18
  88.1 0.9 copy-start.20
  88.5 0.9 copy-start.22
  89.4 3.9 %copy-start.13 = (pred[512,512]{0,1:T(8,128)(4,1)S(1)}, pred[512,512]{0,1:T(8,128)(4,1)}, u32[]{:S(2)}) copy-start(pred[512,512]{0,1:T(8,128)(4,1)} %copy-done.12) | copy-start | bytes 786436
  91.2 4.8 %copy-start.11 = (pred[512,512]{0,1:T(8,128)(4,1)S(1)}, pred[512,512]{0,1:T(8,128)(4,1)}, u32[]{:S(2)}) copy-start(pred[512,512]{0,1:T(8,128)(4,1)} %copy-done.10) | copy-start | bytes 786436
  91.2 10.1 %collective-permute-start.15 = (f32[512,128]{1,0:T(8,128)S(1)}, f32[512,128]{1,0:T(8,128)S(1)}, u32[]{:S(2)}, u32[]{:S(2)}) collective-permute-start(f32[512,128]{1,0:T(8,128)S(1)} %fusion.66), channel_id=1, source_target_pairs={{0,2},{2,4},{4,6},{6,8},{8,10},{10,12},{12,14},{14,16},{16,18},{18... | collective-permute-start | bytes 786440 | tf_op jit(solution)/shard_map/ppermute | solution.py:23
  93.9 10.3 %copy-start.9 = (pred[512,512]{0,1:T(8,128)(4,1)S(1)}, pred[512,512]{0,1:T(8,128)(4,1)}, u32[]{:S(2)}) copy-start(pred[512,512]{0,1:T(8,128)(4,1)} %copy-done.8) | copy-start | bytes 786436
  93.9 10.2 %collective-permute-start.23 = (f32[512,128]{1,0:T(8,128)S(1)}, f32[512,128]{1,0:T(8,128)S(1)}, u32[]{:S(2)}, u32[]{:S(2)}) collective-permute-start(f32[512,128]{1,0:T(8,128)S(1)} %fusion.67), channel_id=1, source_target_pairs={{0,2},{2,4},{4,6},{6,8},{8,10},{10,12},{12,14},{14,16},{16,18},{18... | collective-permute-start | bytes 786440 | tf_op jit(solution)/shard_map/ppermute | solution.py:23
  101.3 10.1 %collective-permute-start.16 = (f32[512,128]{1,0:T(8,128)S(1)}, f32[512,128]{1,0:T(8,128)S(1)}, u32[]{:S(2)}, u32[]{:S(2)}) collective-permute-start(f32[512,128]{1,0:T(8,128)S(1)} %add.397), channel_id=1, source_target_pairs={{0,2},{2,4},{4,6},{6,8},{8,10},{10,12},{12,14},{14,16},{16,18},{18... | collective-permute-start | bytes 786440 | tf_op jit(solution)/shard_map/ppermute | solution.py:23
  104.1 10.2 %copy-start.7 = (pred[512,512]{0,1:T(8,128)(4,1)S(1)}, pred[512,512]{0,1:T(8,128)(4,1)}, u32[]{:S(2)}) copy-start(pred[512,512]{0,1:T(8,128)(4,1)} %copy-done.6) | copy-start | bytes 786436
  104.1 10.1 %collective-permute-start.24 = (f32[512,128]{1,0:T(8,128)S(1)}, f32[512,128]{1,0:T(8,128)S(1)}, u32[]{:S(2)}, u32[]{:S(2)}) collective-permute-start(f32[512,128]{1,0:T(8,128)S(1)} %add.404), channel_id=1, source_target_pairs={{0,2},{2,4},{4,6},{6,8},{8,10},{10,12},{12,14},{14,16},{16,18},{18... | collective-permute-start | bytes 786440 | tf_op jit(solution)/shard_map/ppermute | solution.py:23
  111.4 10.1 %collective-permute-start.17 = (f32[512,128]{1,0:T(8,128)S(1)}, f32[512,128]{1,0:T(8,128)S(1)}, u32[]{:S(2)}, u32[]{:S(2)}) collective-permute-start(f32[512,128]{1,0:T(8,128)S(1)} %add.398), channel_id=1, source_target_pairs={{0,2},{2,4},{4,6},{6,8},{8,10},{10,12},{12,14},{14,16},{16,18},{18... | collective-permute-start | bytes 786440 | tf_op jit(solution)/shard_map/ppermute | solution.py:23
  114.3 10.2 %copy-start.5 = (pred[512,512]{0,1:T(8,128)(4,1)S(1)}, pred[512,512]{0,1:T(8,128)(4,1)}, u32[]{:S(2)}) copy-start(pred[512,512]{0,1:T(8,128)(4,1)} %copy-done.4) | copy-start | bytes 786436
  114.3 10.1 %collective-permute-start.25 = (f32[512,128]{1,0:T(8,128)S(1)}, f32[512,128]{1,0:T(8,128)S(1)}, u32[]{:S(2)}, u32[]{:S(2)}) collective-permute-start(f32[512,128]{1,0:T(8,128)S(1)} %add.405), channel_id=1, source_target_pairs={{0,2},{2,4},{4,6},{6,8},{8,10},{10,12},{12,14},{14,16},{16,18},{18... | collective-permute-start | bytes 786440 | tf_op jit(solution)/shard_map/ppermute | solution.py:23
  121.6 10.1 %collective-permute-start.18 = (f32[512,128]{1,0:T(8,128)S(1)}, f32[512,128]{1,0:T(8,128)S(1)}, u32[]{:S(2)}, u32[]{:S(2)}) collective-permute-start(f32[512,128]{1,0:T(8,128)S(1)} %add.399), channel_id=1, source_target_pairs={{0,2},{2,4},{4,6},{6,8},{8,10},{10,12},{12,14},{14,16},{16,18},{18... | collective-permute-start | bytes 786440 | tf_op jit(solution)/shard_map/ppermute | solution.py:23
  124.4 10.5 %copy-start.3 = (pred[512,512]{0,1:T(8,128)(4,1)S(1)}, pred[512,512]{0,1:T(8,128)(4,1)}, u32[]{:S(2)}) copy-start(pred[512,512]{0,1:T(8,128)(4,1)} %copy-done.2) | copy-start | bytes 786436
  124.4 10.1 %collective-permute-start.26 = (f32[512,128]{1,0:T(8,128)S(1)}, f32[512,128]{1,0:T(8,128)S(1)}, u32[]{:S(2)}, u32[]{:S(2)}) collective-permute-start(f32[512,128]{1,0:T(8,128)S(1)} %add.406), channel_id=1, source_target_pairs={{0,2},{2,4},{4,6},{6,8},{8,10},{10,12},{12,14},{14,16},{16,18},{18... | collective-permute-start | bytes 786440 | tf_op jit(solution)/shard_map/ppermute | solution.py:23
  131.7 10.1 %collective-permute-start.19 = (f32[512,128]{1,0:T(8,128)S(1)}, f32[512,128]{1,0:T(8,128)S(1)}, u32[]{:S(2)}, u32[]{:S(2)}) collective-permute-start(f32[512,128]{1,0:T(8,128)S(1)} %add.400), channel_id=1, source_target_pairs={{0,2},{2,4},{4,6},{6,8},{8,10},{10,12},{12,14},{14,16},{16,18},{18... | collective-permute-start | bytes 786440 | tf_op jit(solution)/shard_map/ppermute | solution.py:23
  134.5 10.3 %collective-permute-start.27 = (f32[512,128]{1,0:T(8,128)S(1)}, f32[512,128]{1,0:T(8,128)S(1)}, u32[]{:S(2)}, u32[]{:S(2)}) collective-permute-start(f32[512,128]{1,0:T(8,128)S(1)} %add.407), channel_id=1, source_target_pairs={{0,2},{2,4},{4,6},{6,8},{8,10},{10,12},{12,14},{14,16},{16,18},{18... | collective-permute-start | bytes 786440 | tf_op jit(solution)/shard_map/ppermute | solution.py:23
  141.8 10.1 %collective-permute-start.20 = (f32[512,128]{1,0:T(8,128)S(1)}, f32[512,128]{1,0:T(8,128)S(1)}, u32[]{:S(2)}, u32[]{:S(2)}) collective-permute-start(f32[512,128]{1,0:T(8,128)S(1)} %add.401), channel_id=1, source_target_pairs={{0,2},{2,4},{4,6},{6,8},{8,10},{10,12},{12,14},{14,16},{16,18},{18... | collective-permute-start | bytes 786440 | tf_op jit(solution)/shard_map/ppermute | solution.py:23
  144.9 10.2 %copy-start.26 = (bf16[512,128]{1,0:T(8,128)(2,1)S(1)}, bf16[512,128]{1,0:T(8,128)(2,1)}, u32[]{:S(2)}) copy-start(bf16[512,128]{1,0:T(8,128)(2,1)} %copy-done.25) | copy-start | bytes 393220
  144.9 10.1 %collective-permute-start.28 = (f32[512,128]{1,0:T(8,128)S(1)}, f32[512,128]{1,0:T(8,128)S(1)}, u32[]{:S(2)}, u32[]{:S(2)}) collective-permute-start(f32[512,128]{1,0:T(8,128)S(1)} %add.408), channel_id=1, source_target_pairs={{0,2},{2,4},{4,6},{6,8},{8,10},{10,12},{12,14},{14,16},{16,18},{18... | collective-permute-start | bytes 786440 | tf_op jit(solution)/shard_map/ppermute | solution.py:23
  151.9 7.1 %collective-permute-start.21 = (f32[512,128]{1,0:T(8,128)S(1)}, f32[512,128]{1,0:T(8,128)S(1)}, u32[]{:S(2)}, u32[]{:S(2)}) collective-permute-start(f32[512,128]{1,0:T(8,128)S(1)} %add.402), channel_id=1, source_target_pairs={{0,114},{2,116},{4,118},{6,120},{8,122},{10,124},{12,126},{14,0},{... | collective-permute-start | bytes 786440 | tf_op jit(solution)/shard_map/ppermute | solution.py:23
  155.0 7.1 %collective-permute-start.29 = (f32[512,128]{1,0:T(8,128)S(1)}, f32[512,128]{1,0:T(8,128)S(1)}, u32[]{:S(2)}, u32[]{:S(2)}) collective-permute-start(f32[512,128]{1,0:T(8,128)S(1)} %add.409), channel_id=1, source_target_pairs={{0,114},{2,116},{4,118},{6,120},{8,122},{10,124},{12,126},{14,0},{... | collective-permute-start | bytes 786440 | tf_op jit(solution)/shard_map/ppermute | solution.py:23
  159.0 0.7 copy-start.14
Sparse Core Ops, SparseCore 0:
  159.8 39.6 all-reduce.2
where the time goes:
time: 209 us; the launch traced here: 208 us
  waiting for transfers between devices  84 us (40%)
  starting transfers between devices  50.3 us (24%)
  matrix products  29.6 us (14%)
  between operations  15 us (7%)
  blocking collectives  14.8 us (7%)
  other arithmetic  12.3 us (6%)
    ppermute x16, waiting for transfers between devices, shifted(): lax.ppermute(array, axis, [(i, (i + by) % length) for i in range(length)])  61.3 us
    ppermute x14, starting transfers between devices, passed_along(): return lax.ppermute(array, axis, pairs)  42.9 us
    psum x1, waiting for transfers between devices, body(): key_sum, value_sum = lax.psum((key_acc, value_acc), 'hd')  22.6 us
    psum x1, blocking collectives, body(): key_sum, value_sum = lax.psum((key_acc, value_acc), 'hd')  14.8 us
    dot_general x7, matrix products, stat_block(): jnp.einsum('thd,kd->htk', grad_heads, value_block, preferred_element_type...  11.3 us
    convert_element_type x2, other arithmetic, grad_block(): (probs * (grad_prob - row_delta[..., None])).astype(jnp.bfloat16)  7.54 us
    ppermute x16, starting transfers between devices, shifted(): lax.ppermute(array, axis, [(i, (i + by) % length) for i in range(length)])  7.29 us
    dot_general x8, matrix products, grad_block(): jnp.einsum('htk,thd->kd', grad_score, query_heads, preferred_element_type...  5.13 us
  transfers between devices with their start and end apart: 31, of which 16 were waited for; matrix products, arithmetic and copies ran while one was open for 16% of the time, Pallas kernels for 0%

commit v1 on v0

v1 whole, which is shorter than its diff:
```python
import functools
import math

import jax
import jax.numpy as jnp
from jax import lax
from jax.experimental import pallas as pl
from jax.experimental.pallas import tpu as pltpu
from jax.sharding import PartitionSpec as P

HDIM = 128
GROUP = 8
SCALE = 1.0 / math.sqrt(HDIM)
EXP_SCALE = SCALE * math.log2(math.e)
MASKED = -1e30
FLOOR = -1e29

NT = (((1,), (1,)), ((), ()))
NN = (((1,), (0,)), ((), ()))
TN = (((0,), (0,)), ((), ()))


def dot(a, b, dims):
    return lax.dot_general(a, b, dims, preferred_element_type=jnp.float32)


def chip_shift(array, by):
    n = lax.axis_size("cp")
    pairs = [(i, i - i % GROUP + (i % GROUP + 2 * by) % GROUP) for i in range(n)]
    return lax.ppermute(array, "cp", pairs)


def core_swap(array):
    n = lax.axis_size("cp")
    return lax.ppermute(array, "cp", [(i, i ^ 1) for i in range(n)])


def hd_swap(array):
    return lax.ppermute(array, "hd", [(0, 1), (1, 0)])


def masked_scores(k, q, starts, row_base, key_base, diagonal):
    s = dot(k, q, NT)
    key_pos = key_base + lax.broadcasted_iota(jnp.int32, s.shape, 0)
    allowed = key_pos >= starts
    if diagonal:
        row_pos = row_base + lax.broadcasted_iota(jnp.int32, s.shape, 1)
        allowed = allowed & (key_pos <= row_pos)
    return jnp.where(allowed, s, MASKED)


def stats_kernel(shifts, pos_ref, stats_in, *refs):
    kv_refs, (q_own, q_sib, g_own, g_sib, st_own, st_sib, stats) = refs[: len(shifts)], refs[len(shifts) :]
    cp = pos_ref[0]
    in_group = lax.rem(cp, GROUP)
    size = q_own.shape[0]
    stats[...] = stats_in[...]
    for kv, shift in zip(kv_refs, shifts):
        key_block = cp - 2 * shift
        for group, (q, g, st) in enumerate(((q_own, g_own, st_own), (q_sib, g_sib, st_sib))):
            row_block = cp if group == 0 else cp + 1 - 2 * lax.rem(cp, 2)

            def work(kv=kv, q=q, g=g, st=st, group=group, shift=shift, key_block=key_block, row_block=row_block):
                for head in range(2):
                    cols = pl.ds(head * HDIM, HDIM)
                    s = masked_scores(
                        kv[:, 0:HDIM], q[:, cols], st[...], row_block * size, key_block * size, shift == 0 and group == 0
                    )
                    dp = dot(kv[:, HDIM:], g[:, cols], NT)
                    at = 3 * (2 * group + head)
                    m = stats[at : at + 1, :]
                    new = jnp.maximum(m, jnp.max(s, axis=0, keepdims=True))
                    p = jnp.exp2((s - new) * EXP_SCALE)
                    f = jnp.exp2((m - new) * EXP_SCALE)
                    stats[at : at + 1, :] = new
                    stats[at + 1 : at + 2, :] = stats[at + 1 : at + 2, :] * f + jnp.sum(p, axis=0, keepdims=True)
                    stats[at + 2 : at + 3, :] = stats[at + 2 : at + 3, :] * f + jnp.sum(p * dp, axis=0, keepdims=True)

            if shift == 0 and group == 0:
                work()
            elif shift == 0:
                pl.when(lax.rem(cp, 2) == 0)(work)
            else:
                pl.when(in_group >= 2 * shift)(work)


def grads_kernel(shift, first, pos_ref, *refs):
    if first:
        kv, q_own, q_sib, g_own, g_sib, st_own, st_sib, fin, dq, dkv, acc = refs
        dq_in = None
    else:
        dq_in, kv, q_own, q_sib, g_own, g_sib, st_own, st_sib, fin, dq, dkv, acc = refs
    cp = pos_ref[0]
    in_group = lax.rem(cp, GROUP)
    size = q_own.shape[0]
    acc[...] = jnp.zeros_like(acc)
    if first:
        dq[...] = jnp.zeros_like(dq)
    else:
        dq[...] = dq_in[...]
    key_block = cp - 2 * shift
    for group, (q, g, st) in enumerate(((q_own, g_own, st_own), (q_sib, g_sib, st_sib))):
        row_block = cp if group == 0 else cp + 1 - 2 * lax.rem(cp, 2)

        def work(q=q, g=g, st=st, group=group, row_block=row_block):
            for head in range(2):
                cols = pl.ds(head * HDIM, HDIM)
                k = kv[:, 0:HDIM]
                s = masked_scores(k, q[:, cols], st[...], row_block * size, key_block * size, shift == 0 and group == 0)
                dp = dot(kv[:, HDIM:], g[:, cols], NT)
                at = 2 * (2 * group + head)
                p = jnp.exp2(s * EXP_SCALE - fin[at : at + 1, :])
                ds = (p * (dp - fin[at + 1 : at + 2, :])).astype(jnp.bfloat16)
                acc[:, 0:HDIM] += dot(ds, q[:, cols], NN)
                acc[:, HDIM:] += dot(p.astype(jnp.bfloat16), g[:, cols], NN)
                dq[group * size : (group + 1) * size, cols] += dot(ds, k, TN)

        if shift == 0 and group == 0:
            work()
        elif shift == 0:
            pl.when(lax.rem(cp, 2) == 0)(work)
        else:
            pl.when(in_group >= 2 * shift)(work)
    dkv[...] = acc[...].astype(dkv.dtype)


VM = pl.BlockSpec(memory_space=pltpu.VMEM)
SM = pl.BlockSpec(memory_space=pltpu.SMEM)


def call_stats(shifts, cp, stats, blocks, rows):
    units = 4 * len(shifts)
    return pl.pallas_call(
        functools.partial(stats_kernel, shifts),
        out_shape=jax.ShapeDtypeStruct(stats.shape, jnp.float32),
        in_specs=[SM] + [VM] * (1 + len(shifts) + len(rows)),
        out_specs=VM,
        compiler_params=pltpu.CompilerParams(vmem_limit_bytes=32 * 2**20),
        cost_estimate=pl.CostEstimate(flops=units * 4 * 512 * 512 * 128, bytes_accessed=2**20, transcendentals=units * 512 * 512),
        name="stats",
    )(cp, stats, *blocks, *rows)


def call_grads(shift, cp, dq, block, rows, fin):
    size = block.shape[0]
    first = dq is None
    out = (
        jax.ShapeDtypeStruct((2 * size, 2 * HDIM), jnp.float32),
        jax.ShapeDtypeStruct((size, 2 * HDIM), jnp.float32 if shift == 0 else jnp.bfloat16),
    )
    return pl.pallas_call(
        functools.partial(grads_kernel, shift, first),
        out_shape=out,
        in_specs=[SM] + [VM] * (2 + len(rows) + (0 if first else 1)),
        out_specs=(VM, VM),
        scratch_shapes=[pltpu.VMEM((size, 2 * HDIM), jnp.float32)],
        compiler_params=pltpu.CompilerParams(vmem_limit_bytes=32 * 2**20),
        cost_estimate=pl.CostEstimate(flops=4 * 10 * 512 * 512 * 128, bytes_accessed=3 * 2**20, transcendentals=4 * 512 * 512),
        name="grads",
    )(cp, *([] if first else [dq]), block, *rows, fin)


def body(query, keys, values, grad_out, doc_start):
    size = query.shape[0]
    position = lax.axis_index("cp").astype(jnp.int32)
    cp = position.reshape(1)
    kv = jnp.concatenate([keys, values], axis=1)
    from1 = chip_shift(kv, 1)
    from3 = chip_shift(kv, 3)
    from2 = chip_shift(kv, 2)
    starts = doc_start.reshape(1, size)
    rows = (query, core_swap(query), grad_out, core_swap(grad_out), starts, core_swap(starts))

    zero = jnp.zeros((4, 1, size), jnp.float32)
    stats = jnp.concatenate([zero + FLOOR, zero, zero], axis=1).reshape(12, size)
    stats = call_stats((0,), cp, stats, (kv,), rows)
    stats = call_stats((1, 3), cp, stats, (from1, from3), rows)
    stats = call_stats((2,), cp, stats, (from2,), rows)

    other = core_swap(stats).reshape(2, 6, size)[::-1].reshape(4, 3, size)
    mine = stats.reshape(4, 3, size)
    top = jnp.maximum(mine[:, 0], other[:, 0])
    f_mine = jnp.exp2((mine[:, 0] - top) * EXP_SCALE)
    f_other = jnp.exp2((other[:, 0] - top) * EXP_SCALE)
    total = mine[:, 1] * f_mine + other[:, 1] * f_other
    weighted = mine[:, 2] * f_mine + other[:, 2] * f_other
    fin = jnp.stack([top * EXP_SCALE + jnp.log2(total), weighted / total], axis=1).reshape(8, size)

    dq, part2 = call_grads(2, cp, None, from2, rows, fin)
    back2 = chip_shift(part2, 2)
    dq, part1 = call_grads(1, cp, dq, from1, rows, fin)
    back1 = chip_shift(part1, 3)
    dq, part3 = call_grads(3, cp, dq, from3, rows, fin)
    back3 = chip_shift(part3, 1)
    dq, own = call_grads(0, cp, dq, kv, rows, fin)

    dq_other = core_swap(dq[size:])
    grad_query = ((dq[:size] + dq_other) * SCALE).astype(jnp.bfloat16)

    f32 = jnp.float32
    half = (own + back1.astype(f32) + back3.astype(f32) + back2.astype(f32)).astype(jnp.bfloat16)
    dkv = half.astype(f32) + hd_swap(half).astype(f32)
    return (
        grad_query,
        (dkv[:, :HDIM] * SCALE).astype(jnp.bfloat16),
        dkv[:, HDIM:].astype(jnp.bfloat16),
    )


def solution(mesh):
    in_specs = (P("cp", "hd"), P("cp", None), P("cp", None), P("cp", "hd"), P("cp"))
    out_specs = (P("cp", "hd"), P("cp", None), P("cp", None))
    return jax.shard_map(body, mesh=mesh, in_specs=in_specs, out_specs=out_specs, check_vma=False)
```

time: 209 us -> 62.8 us (0.30)
  waiting for transfers between devices: 84 us -> 24.2 us
  matrix products: 29.6 us -> 0 us
  starting transfers between devices: 50.3 us -> 25.4 us
  blocking collectives: 14.8 us -> 0 us
  between operations: 15 us -> 0.82 us
  other arithmetic: 12.3 us -> 1.72 us
  Pallas kernels: 0 us -> 6.33 us
    ppermute x30 -> x12, waiting for transfers between devices: 61.3 us -> 24.2 us  [the longest x6 16 us: chip_shift(): return lax.ppermute(array, 'cp', pairs)]
    dot_general x40 -> x0, matrix products: 29.6 us -> none  [the longest x7 11.3 us: stat_block(): jnp.einsum('thd,kd->htk', grad_heads, value_block, preferred_element_type...]
    ppermute x30 -> x12, starting transfers between devices: 50.2 us -> 25.4 us  [the longest x6 21.4 us: chip_shift(): return lax.ppermute(array, 'cp', pairs)]
    psum x1 -> x0, waiting for transfers between devices: 22.6 us -> none  [body(): key_sum, value_sum = lax.psum((key_acc, value_acc), 'hd')]
    psum x1 -> x0, blocking collectives: 14.8 us -> none  [body(): key_sum, value_sum = lax.psum((key_acc, value_acc), 'hd')]
    convert_element_type x3, other arithmetic: 9.16 us -> 1.62 us  [the longest x1 0.82 us: body(): grad_query = ((dq[:size] + dq_other) * SCALE).astype(jnp.bfloat16)]
    pallas_call x0 -> x7, Pallas kernels: none -> 6.33 us  [the longest x4 4.28 us: call_grads(): pl.pallas_call(functools.partial(grads_kernel, shift, first), out_shape=o...]
    and x1 -> x0, other arithmetic: 2.67 us -> none  [key_mask(): (key_pos[None, :] >= start_rows[:, None]) & (key_pos[None, :] <= query_po...]
  transfers between devices with their start and end apart: 31 -> 12, of which waited for: 16 -> 8; matrix products, arithmetic and copies ran while one was open for 16% -> 5% of each run, Pallas kernels for 0% -> 9%
where the time goes in v1:
time: 62.8 us; the launch traced here: 62.6 us
  starting transfers between devices  25.4 us (40%)
  waiting for transfers between devices  24.2 us (39%)
  Pallas kernels  6.33 us (10%)
  local copies, waits for them, and re-layouts  4.1 us (7%)
  other arithmetic  1.72 us (3%)
  between operations  0.82 us (1%)
    ppermute x6, starting transfers between devices, chip_shift(): return lax.ppermute(array, 'cp', pairs)  21.4 us
    ppermute x6, waiting for transfers between devices, chip_shift(): return lax.ppermute(array, 'cp', pairs)  16 us
    ppermute x1, waiting for transfers between devices, hd_swap(): return lax.ppermute(array, 'hd', [(0, 1), (1, 0)])  5.72 us
    pallas_call x4, Pallas kernels, call_grads(): pl.pallas_call(functools.partial(grads_kernel, shift, first), out_shape=o...  4.28 us
    ppermute x1, starting transfers between devices, hd_swap(): return lax.ppermute(array, 'hd', [(0, 1), (1, 0)])  3.28 us
    ppermute x5, waiting for transfers between devices, core_swap(): return lax.ppermute(array, 'cp', [(i, i ^ 1) for i in range(n)])  2.54 us
    unnamed x9, local copies, waits for them, and re-layouts  2.34 us
    pallas_call x3, Pallas kernels, call_stats(): pl.pallas_call(functools.partial(stats_kernel, shifts), out_shape=jax.Sha...  2.06 us
  transfers between devices with their start and end apart: 12, of which 8 were waited for; matrix products, arithmetic and copies ran while one was open for 5% of the time, Pallas kernels for 9%

profile of v1, /device:TPU:0, one launch (start us, length us, event | category | flops | bytes accessed | tf_op | source)
XLA Modules:
  0.0 62.6 jit_solution(1289034706788862695)
XLA Ops:
  0.6 0.0 copy-start
  0.6 0.0 copy-start.1
  0.7 0.1 collective-permute-start.1
  0.7 0.5 collective-permute-start.2
  1.2 0.9 %constant_dynamic-update-slice_fusion.1 = bf16[512,256]{1,0:T(8,128)(2,1)S(1)} fusion(bf16[512,128]{1,0:T(8,128)(2,1)} %param.6), kind=kLoop, calls=%fused_computation.19 | loop fusion | bytes 262144
  2.2 0.9 %constant_dynamic-update-slice_fusion.refs_0_.refs_1_ = bf16[512,256]{1,0:T(8,128)(2,1)S(1)} fusion(bf16[512,256]{1,0:T(8,128)(2,1)S(1)} %constant_dynamic-update-slice_fusion.1, bf16[512,128]{1,0:T(8,128)(2,1)} %param.7), kind=kLoop, calls=%fused_computation.18 | loop fusion | bytes 262144 | tf_op jit(solution)/shard_map/concatenate | solution.py:167
  3.1 2.9 %collective-permute-start.5 = (bf16[512,256]{1,0:T(8,128)(2,1)S(1)}, bf16[512,256]{1,0:T(8,128)(2,1)S(1)}, u32[]{:S(2)}, u32[]{:S(2)}) collective-permute-start(bf16[512,256]{1,0:T(8,128)(2,1)S(1)} %constant_dynamic-update-slice_fusion.refs_0_.refs_1_), channel_id=1, source_target_pairs={{0,12},{2,14},{4,0},{6,2},{8,4},{10,6},{12,8},{14,10},{16,28},{18,... | collective-permute-start | bytes 786440 | tf_op jit(solution)/shard_map/ppermute | solution.py:30
  6.0 0.0 collective-permute-start.4
  6.0 0.0 collective-permute-start.3
  6.0 1.4 %collective-permute-done.3.refs_6_.refs_7_ = s32[1,512]{1,0:T(1,128)S(1)} collective-permute-done((s32[1,512]{1,0:T(1,128)}, s32[1,512]{1,0:T(1,128)S(1)}, u32[]{:S(2)}, u32[]{:S(2)}) %collective-permute-start.3) | collective-permute-done | bytes 2080 | tf_op jit(solution)/shard_map/ppermute | solution.py:35
  7.4 2.3 %collective-permute-start = (bf16[512,256]{1,0:T(8,128)(2,1)S(1)}, bf16[512,256]{1,0:T(8,128)(2,1)S(1)}, u32[]{:S(2)}, u32[]{:S(2)}) collective-permute-start(bf16[512,256]{1,0:T(8,128)(2,1)S(1)} %constant_dynamic-update-slice_fusion.refs_0_.refs_1_), channel_id=1, source_target_pairs={{0,8},{2,10},{4,12},{6,14},{8,0},{10,2},{12,4},{14,6},{16,24},{18,... | collective-permute-start | bytes 786440 | tf_op jit(solution)/shard_map/ppermute | solution.py:30
  9.7 0.0 copy-start.2
  9.7 0.0 collective-permute-done.1.refs_2_.refs_3_
  9.7 0.0 collective-permute-done.2.refs_4_.refs_5_
  9.7 0.0 copy-done
  9.7 0.0 copy-done.1
  9.7 0.7 %copy-done.2 = s32[512]{0:T(512)S(1)} copy-done((s32[512]{0:T(512)S(1)}, s32[512]{0:T(512)}, u32[]{:S(2)}) %copy-start.2) | copy-done | bytes 2072
  10.4 0.0 copy-start.3
  10.4 0.8 %copy-done.3 = f32[12,512]{1,0:T(8,128)S(1)} copy-done((f32[12,512]{1,0:T(8,128)S(1)}, f32[12,512]{1,0:T(8,128)}, u32[]{:S(2)}) %copy-start.3) | copy-done | bytes 24600
  11.1 2.0 %stats.3.stats_in = f32[12,512]{1,0:T(8,128)S(1)} custom-call(s32[1]{0:T(128)} %bitcast.pos_ref, f32[12,512]{1,0:T(8,128)S(1)} %copy-done.3, bf16[512,256]{1,0:T(8,128)(2,1)S(1)} %constant_dynamic-update-slice_fusion.refs_0_.refs_1_, bf16[512,256]{1,0:T(8,128)(2,1)S(1)} %copy-done, bf16[512,256]{1,0:T(8,128)(2,1)S(1)} %collective-permute-done.1.refs_2_.refs_3_, ...), custom_call_target="tpu_custom_call" | custom-call | flops 536870912 | bytes 1048576 | tf_op jit(solution)/shard_map/stats/pallas_call | solution.py:133
  13.2 4.3 %collective-permute-done.5.refs_1_ = bf16[512,256]{1,0:T(8,128)(2,1)S(1)} collective-permute-done((bf16[512,256]{1,0:T(8,128)(2,1)S(1)}, bf16[512,256]{1,0:T(8,128)(2,1)S(1)}, u32[]{:S(2)}, u32[]{:S(2)}) %collective-permute-start.5) | collective-permute-done | bytes 262176 | tf_op jit(solution)/shard_map/ppermute | solution.py:30
  17.5 3.4 %collective-permute-done.4.refs_0_.refs_1_ = bf16[512,256]{1,0:T(8,128)(2,1)S(1)} collective-permute-done((bf16[512,256]{1,0:T(8,128)(2,1)S(1)}, bf16[512,256]{1,0:T(8,128)(2,1)S(1)}, u32[]{:S(2)}, u32[]{:S(2)}) %collective-permute-start.4) | collective-permute-done | bytes 262176 | tf_op jit(solution)/shard_map/ppermute | solution.py:30
  20.9 0.0 collective-permute-done.refs_0_
  20.9 0.1 collective-permute-start.6
  21.0 1.2 %collective-permute-done.6 = f32[12,512]{1,0:T(8,128)S(1)} collective-permute-done((f32[12,512]{1,0:T(8,128)S(1)}, f32[12,512]{1,0:T(8,128)S(1)}, u32[]{:S(2)}, u32[]{:S(2)}) %collective-permute-start.6) | collective-permute-done | bytes 24608 | tf_op jit(solution)/shard_map/ppermute | solution.py:35
  22.4 0.3 grads.4
  22.7 0.1 grads.5
  22.8 0.1 grads.6
  23.0 1.9 %collective-permute-start.9 = (bf16[512,256]{1,0:T(8,128)(2,1)S(1)}, bf16[512,256]{1,0:T(8,128)(2,1)S(1)}, u32[]{:S(2)}, u32[]{:S(2)}) collective-permute-start(bf16[512,256]{1,0:T(8,128)(2,1)S(1)} %get-tuple-element.17), channel_id=1, source_target_pairs={{0,4},{2,6},{4,8},{6,10},{8,12},{10,14},{12,0},{14,2},{16,20},{18,... | collective-permute-start | bytes 786440 | tf_op jit(solution)/shard_map/ppermute | solution.py:30
  24.9 12.9 %collective-permute-start.8 = (bf16[512,256]{1,0:T(8,128)(2,1)S(1)}, bf16[512,256]{1,0:T(8,128)(2,1)S(1)}, u32[]{:S(2)}, u32[]{:S(2)}) collective-permute-start(bf16[512,256]{1,0:T(8,128)(2,1)S(1)} %get-tuple-element.16), channel_id=1, source_target_pairs={{0,12},{2,14},{4,0},{6,2},{8,4},{10,6},{12,8},{14,10},{16,28},{18,... | collective-permute-start | bytes 786440 | tf_op jit(solution)/shard_map/ppermute | solution.py:30
  37.7 1.4 %collective-permute-start.10 = (bf16[512,256]{1,0:T(8,128)(2,1)S(1)}, bf16[512,256]{1,0:T(8,128)(2,1)S(1)}, u32[]{:S(2)}, u32[]{:S(2)}) collective-permute-start(bf16[512,256]{1,0:T(8,128)(2,1)S(1)} %get-tuple-element.18), channel_id=1, source_target_pairs={{0,8},{2,10},{4,12},{6,14},{8,0},{10,2},{12,4},{14,6},{16,24},{18,... | collective-permute-start | bytes 786440 | tf_op jit(solution)/shard_map/ppermute | solution.py:30
  39.1 3.7 %grads.7 = (f32[1024,256]{1,0:T(8,128)S(1)}, f32[512,256]{1,0:T(8,128)S(1)}) custom-call(s32[1]{0:T(128)} %bitcast.pos_ref, f32[1024,256]{1,0:T(8,128)S(1)} %get-tuple-element.13.refs_0_, bf16[512,256]{1,0:T(8,128)(2,1)S(1)} %constant_dynamic-update-slice_fusion.refs_0_.refs_1_, bf16[512,256]{1,0:T(8,128)(2,1)S(1)} %copy-done, ...), custom_call_target="tpu_custom_call" | custom-call | flops 1342177280 | bytes 3145728 | tf_op jit(solution)/shard_map/grads/pallas_call | solution.py:151
  42.8 1.5 %collective-permute-done.9 = bf16[512,256]{1,0:T(8,128)(2,1)S(1)} collective-permute-done((bf16[512,256]{1,0:T(8,128)(2,1)S(1)}, bf16[512,256]{1,0:T(8,128)(2,1)S(1)}, u32[]{:S(2)}, u32[]{:S(2)}) %collective-permute-start.9) | collective-permute-done | bytes 262176 | tf_op jit(solution)/shard_map/ppermute | solution.py:30
  44.3 5.0 %collective-permute-done.8 = bf16[512,256]{1,0:T(8,128)(2,1)S(1)} collective-permute-done((bf16[512,256]{1,0:T(8,128)(2,1)S(1)}, bf16[512,256]{1,0:T(8,128)(2,1)S(1)}, u32[]{:S(2)}, u32[]{:S(2)}) %collective-permute-start.8) | collective-permute-done | bytes 262176 | tf_op jit(solution)/shard_map/ppermute | solution.py:30
  49.3 1.8 %collective-permute-done.10 = bf16[512,256]{1,0:T(8,128)(2,1)S(1)} collective-permute-done((bf16[512,256]{1,0:T(8,128)(2,1)S(1)}, bf16[512,256]{1,0:T(8,128)(2,1)S(1)}, u32[]{:S(2)}, u32[]{:S(2)}) %collective-permute-start.10) | collective-permute-done | bytes 262176 | tf_op jit(solution)/shard_map/ppermute | solution.py:30
  51.1 0.1 add_convert_fusion
  51.2 3.3 %collective-permute-start.11 = (bf16[512,256]{1,0:T(8,128)(2,1)S(1)}, bf16[512,256]{1,0:T(8,128)(2,1)S(1)}, u32[]{:S(2)}, u32[]{:S(2)}) collective-permute-start(bf16[512,256]{1,0:T(8,128)(2,1)S(1)} %add_convert_fusion), channel_id=1, source_target_pairs={{0,1},{1,0},{2,3},{3,2},{4,5},{5,4},{6,7},{7,6},{8,9},{9,8},{10,11... | collective-permute-start | bytes 786440 | tf_op jit(solution)/shard_map/ppermute | solution.py:39
  54.5 0.1 collective-permute-start.7
  54.6 5.7 %collective-permute-done.11 = bf16[512,256]{1,0:T(8,128)(2,1)S(1)} collective-permute-done((bf16[512,256]{1,0:T(8,128)(2,1)S(1)}, bf16[512,256]{1,0:T(8,128)(2,1)S(1)}, u32[]{:S(2)}, u32[]{:S(2)}) %collective-permute-start.11) | collective-permute-done | bytes 262176 | tf_op jit(solution)/shard_map/ppermute | solution.py:39
  60.4 0.1 convert_add_fusion
  60.4 0.7 %slice.56 = bf16[512,128]{1,0:T(8,128)(2,1)} slice(f32[512,256]{1,0:T(8,128)S(1)} %convert_add_fusion), slice={[0:512], [128:256]} | slice | bytes 262144 | tf_op jit(solution)/shard_map/slice | solution.py:206
  61.1 0.7 %fusion = bf16[512,128]{1,0:T(8,128)(2,1)} fusion(f32[512,256]{1,0:T(8,128)S(1)} %convert_add_fusion), kind=kLoop, calls=%fused_computation.5 | loop fusion | flops 131072 | bytes 393216 | tf_op jit(solution)/shard_map/convert_element_type | solution.py:205
  61.8 0.0 collective-permute-done.7
  61.8 0.8 %multiply_convert_fusion = bf16[512,256]{1,0:T(8,128)(2,1)} fusion(f32[512,256]{1,0:T(8,128)S(1)} %collective-permute-done.7, f32[1024,256]{1,0:T(8,128)S(1)} %get-tuple-element.14), kind=kLoop, calls=%fused_computation.2 | loop fusion | flops 393216 | bytes 1310720 | tf_op jit(solution)/shard_map/convert_element_type | solution.py:198
  (13 shorter events, 0.2 us)
Async XLA Ops:
  0.6 9.1 %copy-start = (bf16[512,256]{1,0:T(8,128)(2,1)S(1)}, bf16[512,256]{1,0:T(8,128)(2,1)}, u32[]{:S(2)}) copy-start(bf16[512,256]{1,0:T(8,128)(2,1)} %refs_2_.7) | copy-start | bytes 786436
  0.6 9.1 %copy-start.1 = (bf16[512,256]{1,0:T(8,128)(2,1)S(1)}, bf16[512,256]{1,0:T(8,128)(2,1)}, u32[]{:S(2)}) copy-start(bf16[512,256]{1,0:T(8,128)(2,1)} %refs_4_.7) | copy-start | bytes 786436
  0.7 9.0 %collective-permute-start.1 = (bf16[512,256]{1,0:T(8,128)(2,1)}, bf16[512,256]{1,0:T(8,128)(2,1)S(1)}, u32[]{:S(2)}, u32[]{:S(2)}) collective-permute-start(bf16[512,256]{1,0:T(8,128)(2,1)} %refs_2_.7), channel_id=1, source_target_pairs={{0,2},{2,0},{4,6},{6,4},{8,10},{10,8},{12,14},{14,12},{16,18},{18,... | collective-permute-start | bytes 786440 | tf_op jit(solution)/shard_map/ppermute | solution.py:35
  0.7 8.9 %collective-permute-start.2 = (bf16[512,256]{1,0:T(8,128)(2,1)}, bf16[512,256]{1,0:T(8,128)(2,1)S(1)}, u32[]{:S(2)}, u32[]{:S(2)}) collective-permute-start(bf16[512,256]{1,0:T(8,128)(2,1)} %refs_4_.7), channel_id=1, source_target_pairs={{0,2},{2,0},{4,6},{6,4},{8,10},{10,8},{12,14},{14,12},{16,18},{18,... | collective-permute-start | bytes 786440 | tf_op jit(solution)/shard_map/ppermute | solution.py:35
  3.1 14.4 %collective-permute-start.5 = (bf16[512,256]{1,0:T(8,128)(2,1)S(1)}, bf16[512,256]{1,0:T(8,128)(2,1)S(1)}, u32[]{:S(2)}, u32[]{:S(2)}) collective-permute-start(bf16[512,256]{1,0:T(8,128)(2,1)S(1)} %constant_dynamic-update-slice_fusion.refs_0_.refs_1_), channel_id=1, source_target_pairs={{0,12},{2,14},{4,0},{6,2},{8,4},{10,6},{12,8},{14,10},{16,28},{18,... | collective-permute-start | bytes 786440 | tf_op jit(solution)/shard_map/ppermute | solution.py:30
  6.0 14.9 %collective-permute-start.4 = (bf16[512,256]{1,0:T(8,128)(2,1)S(1)}, bf16[512,256]{1,0:T(8,128)(2,1)S(1)}, u32[]{:S(2)}, u32[]{:S(2)}) collective-permute-start(bf16[512,256]{1,0:T(8,128)(2,1)S(1)} %constant_dynamic-update-slice_fusion.refs_0_.refs_1_), channel_id=1, source_target_pairs={{0,4},{2,6},{4,8},{6,10},{8,12},{10,14},{12,0},{14,2},{16,20},{18,... | collective-permute-start | bytes 786440 | tf_op jit(solution)/shard_map/ppermute | solution.py:30
  6.0 1.4 %collective-permute-start.3 = (s32[1,512]{1,0:T(1,128)}, s32[1,512]{1,0:T(1,128)S(1)}, u32[]{:S(2)}, u32[]{:S(2)}) collective-permute-start(s32[1,512]{1,0:T(1,128)} %bitcast.2), channel_id=1, source_target_pairs={{0,2},{2,0},{4,6},{6,4},{8,10},{10,8},{12,14},{14,12},{16,18},{18,... | collective-permute-start | bytes 6152 | tf_op jit(solution)/shard_map/ppermute | solution.py:35
  7.4 13.5 %collective-permute-start = (bf16[512,256]{1,0:T(8,128)(2,1)S(1)}, bf16[512,256]{1,0:T(8,128)(2,1)S(1)}, u32[]{:S(2)}, u32[]{:S(2)}) collective-permute-start(bf16[512,256]{1,0:T(8,128)(2,1)S(1)} %constant_dynamic-update-slice_fusion.refs_0_.refs_1_), channel_id=1, source_target_pairs={{0,8},{2,10},{4,12},{6,14},{8,0},{10,2},{12,4},{14,6},{16,24},{18,... | collective-permute-start | bytes 786440 | tf_op jit(solution)/shard_map/ppermute | solution.py:30
  9.7 0.7 %copy-start.2 = (s32[512]{0:T(512)S(1)}, s32[512]{0:T(512)}, u32[]{:S(2)}) copy-start(s32[512]{0:T(512)} %param.9) | copy-start | bytes 6148
  10.4 0.8 %copy-start.3 = (f32[12,512]{1,0:T(8,128)S(1)}, f32[12,512]{1,0:T(8,128)}, u32[]{:S(2)}) copy-start(f32[12,512]{1,0:T(8,128)} %constant.4.clone.1.stats_in) | copy-start | bytes 73732
  20.9 1.3 %collective-permute-start.6 = (f32[12,512]{1,0:T(8,128)S(1)}, f32[12,512]{1,0:T(8,128)S(1)}, u32[]{:S(2)}, u32[]{:S(2)}) collective-permute-start(f32[12,512]{1,0:T(8,128)S(1)} %stats.5), channel_id=1, source_target_pairs={{0,2},{2,0},{4,6},{6,4},{8,10},{10,8},{12,14},{14,12},{16,18},{18,... | collective-permute-start | bytes 73736 | tf_op jit(solution)/shard_map/ppermute | solution.py:35
  23.0 21.3 %collective-permute-start.9 = (bf16[512,256]{1,0:T(8,128)(2,1)S(1)}, bf16[512,256]{1,0:T(8,128)(2,1)S(1)}, u32[]{:S(2)}, u32[]{:S(2)}) collective-permute-start(bf16[512,256]{1,0:T(8,128)(2,1)S(1)} %get-tuple-element.17), channel_id=1, source_target_pairs={{0,4},{2,6},{4,8},{6,10},{8,12},{10,14},{12,0},{14,2},{16,20},{18,... | collective-permute-start | bytes 786440 | tf_op jit(solution)/shard_map/ppermute | solution.py:30
  24.9 24.4 %collective-permute-start.8 = (bf16[512,256]{1,0:T(8,128)(2,1)S(1)}, bf16[512,256]{1,0:T(8,128)(2,1)S(1)}, u32[]{:S(2)}, u32[]{:S(2)}) collective-permute-start(bf16[512,256]{1,0:T(8,128)(2,1)S(1)} %get-tuple-element.16), channel_id=1, source_target_pairs={{0,12},{2,14},{4,0},{6,2},{8,4},{10,6},{12,8},{14,10},{16,28},{18,... | collective-permute-start | bytes 786440 | tf_op jit(solution)/shard_map/ppermute | solution.py:30
  37.7 13.3 %collective-permute-start.10 = (bf16[512,256]{1,0:T(8,128)(2,1)S(1)}, bf16[512,256]{1,0:T(8,128)(2,1)S(1)}, u32[]{:S(2)}, u32[]{:S(2)}) collective-permute-start(bf16[512,256]{1,0:T(8,128)(2,1)S(1)} %get-tuple-element.18), channel_id=1, source_target_pairs={{0,8},{2,10},{4,12},{6,14},{8,0},{10,2},{12,4},{14,6},{16,24},{18,... | collective-permute-start | bytes 786440 | tf_op jit(solution)/shard_map/ppermute | solution.py:30
  51.2 9.1 %collective-permute-start.11 = (bf16[512,256]{1,0:T(8,128)(2,1)S(1)}, bf16[512,256]{1,0:T(8,128)(2,1)S(1)}, u32[]{:S(2)}, u32[]{:S(2)}) collective-permute-start(bf16[512,256]{1,0:T(8,128)(2,1)S(1)} %add_convert_fusion), channel_id=1, source_target_pairs={{0,1},{1,0},{2,3},{3,2},{4,5},{5,4},{6,7},{7,6},{8,9},{9,8},{10,11... | collective-permute-start | bytes 786440 | tf_op jit(solution)/shard_map/ppermute | solution.py:39
  54.5 7.2 %collective-permute-start.7 = (f32[512,256]{1,0:T(8,128)S(1)}, f32[512,256]{1,0:T(8,128)S(1)}, u32[]{:S(2)}, u32[]{:S(2)}) collective-permute-start(f32[512,256]{1,0:T(8,128)S(1)} %slice.40), channel_id=1, source_target_pairs={{0,2},{2,0},{4,6},{6,4},{8,10},{10,8},{12,14},{14,12},{16,18},{18,... | collective-permute-start | bytes 1572872 | tf_op jit(solution)/shard_map/ppermute | solution.py:35

commit v2 on v1

--- a/solution.py
+++ b/solution.py
@@ -84,21 +84,32 @@
                 pl.when(in_group >= 2 * shift)(work)
 
 
+def merged(stats, other, at, other_at):
+    m, m2 = stats[at : at + 1, :], other[other_at : other_at + 1, :]
+    top = jnp.maximum(m, m2)
+    f, f2 = jnp.exp2((m - top) * EXP_SCALE), jnp.exp2((m2 - top) * EXP_SCALE)
+    total = stats[at + 1 : at + 2, :] * f + other[other_at + 1 : other_at + 2, :] * f2
+    weighted = stats[at + 2 : at + 3, :] * f + other[other_at + 2 : other_at + 3, :] * f2
+    return top * EXP_SCALE + jnp.log2(total), weighted / total
+
+
 def grads_kernel(shift, first, pos_ref, *refs):
     if first:
-        kv, q_own, q_sib, g_own, g_sib, st_own, st_sib, fin, dq, dkv, acc = refs
-        dq_in = None
+        stats, other, kv, q_own, q_sib, g_own, g_sib, st_own, st_sib, dq, dkv, fin, acc = refs
+        for s in range(4):
+            log_sum, delta = merged(stats, other, 3 * s, 3 * (s ^ 2))
+            fin[2 * s : 2 * s + 1, :] = log_sum
+            fin[2 * s + 1 : 2 * s + 2, :] = delta
+        dq[...] = jnp.zeros_like(dq)
     else:
-        dq_in, kv, q_own, q_sib, g_own, g_sib, st_own, st_sib, fin, dq, dkv, acc = refs
+        dq_in, fin, kv, q_own, q_sib, g_own, g_sib, st_own, st_sib, dq, dkv, acc = refs
+        dq[...] = dq_in[...]
     cp = pos_ref[0]
     in_group = lax.rem(cp, GROUP)
     size = q_own.shape[0]
     acc[...] = jnp.zeros_like(acc)
-    if first:
-        dq[...] = jnp.zeros_like(dq)
-    else:
-        dq[...] = dq_in[...]
     key_block = cp - 2 * shift
+    k_t = kv[:, 0:HDIM].T
     for group, (q, g, st) in enumerate(((q_own, g_own, st_own), (q_sib, g_sib, st_sib))):
         row_block = cp if group == 0 else cp + 1 - 2 * lax.rem(cp, 2)
 
@@ -113,7 +124,7 @@
                 ds = (p * (dp - fin[at + 1 : at + 2, :])).astype(jnp.bfloat16)
                 acc[:, 0:HDIM] += dot(ds, q[:, cols], NN)
                 acc[:, HDIM:] += dot(p.astype(jnp.bfloat16), g[:, cols], NN)
-                dq[group * size : (group + 1) * size, cols] += dot(ds, k, TN)
+                dq[group, cols, :] += dot(k_t, ds, NN)
 
         if shift == 0 and group == 0:
             work()
@@ -124,47 +135,82 @@
     dkv[...] = acc[...].astype(dkv.dtype)
 
 
+def pack_kernel(keys, values, kv):
+    kv[:, 0:HDIM] = keys[...]
+    kv[:, HDIM:] = values[...]
+
+
+def query_kernel(mine, other, out):
+    out[...] = ((mine[0] + other[...]) * SCALE).T.astype(out.dtype)
+
+
+def add_kernel(total, part, out):
+    out[...] = (total[...] + part[...].astype(jnp.float32)).astype(out.dtype)
+
+
+def last_kernel(mine, other, grad_keys, grad_values):
+    total = mine[...].astype(jnp.float32) + other[...].astype(jnp.float32)
+    grad_keys[...] = (total[:, 0:HDIM] * SCALE).astype(grad_keys.dtype)
+    grad_values[...] = total[:, HDIM:].astype(grad_values.dtype)
+
+
 VM = pl.BlockSpec(memory_space=pltpu.VMEM)
 SM = pl.BlockSpec(memory_space=pltpu.SMEM)
 
 
+BLOCK_COST = pl.CostEstimate(flops=4 * 10 * 512 * 512 * 128, bytes_accessed=2**20, transcendentals=0)
+NO_COST = pl.CostEstimate(flops=0, bytes_accessed=2**10, transcendentals=0)
+
+
+def simple(kernel, out, *args, cost=NO_COST):
+    return pl.pallas_call(
+        kernel,
+        out_shape=out,
+        in_specs=[VM] * len(args),
+        out_specs=jax.tree.map(lambda _: VM, out),
+        cost_estimate=cost,
+    )(*args)
+
+
 def call_stats(shifts, cp, stats, blocks, rows):
-    units = 4 * len(shifts)
     return pl.pallas_call(
         functools.partial(stats_kernel, shifts),
         out_shape=jax.ShapeDtypeStruct(stats.shape, jnp.float32),
         in_specs=[SM] + [VM] * (1 + len(shifts) + len(rows)),
         out_specs=VM,
         compiler_params=pltpu.CompilerParams(vmem_limit_bytes=32 * 2**20),
-        cost_estimate=pl.CostEstimate(flops=units * 4 * 512 * 512 * 128, bytes_accessed=2**20, transcendentals=units * 512 * 512),
+        cost_estimate=BLOCK_COST,
         name="stats",
     )(cp, stats, *blocks, *rows)
 
 
-def call_grads(shift, cp, dq, block, rows, fin):
+def call_grads(shift, cp, before, block, rows):
     size = block.shape[0]
-    first = dq is None
-    out = (
-        jax.ShapeDtypeStruct((2 * size, 2 * HDIM), jnp.float32),
+    first = shift == 2
+    out = [
+        jax.ShapeDtypeStruct((2, 2 * HDIM, size), jnp.float32),
         jax.ShapeDtypeStruct((size, 2 * HDIM), jnp.float32 if shift == 0 else jnp.bfloat16),
-    )
+    ]
+    if first:
+        out.append(jax.ShapeDtypeStruct((8, size), jnp.float32))
     return pl.pallas_call(
         functools.partial(grads_kernel, shift, first),
         out_shape=out,
-        in_specs=[SM] + [VM] * (2 + len(rows) + (0 if first else 1)),
-        out_specs=(VM, VM),
+        in_specs=[SM] + [VM] * (3 + len(rows)),
+        out_specs=[VM] * len(out),
         scratch_shapes=[pltpu.VMEM((size, 2 * HDIM), jnp.float32)],
         compiler_params=pltpu.CompilerParams(vmem_limit_bytes=32 * 2**20),
-        cost_estimate=pl.CostEstimate(flops=4 * 10 * 512 * 512 * 128, bytes_accessed=3 * 2**20, transcendentals=4 * 512 * 512),
+        cost_estimate=NO_COST if shift == 0 else BLOCK_COST,
         name="grads",
-    )(cp, *([] if first else [dq]), block, *rows, fin)
+    )(cp, *before, block, *rows)
 
 
 def body(query, keys, values, grad_out, doc_start):
     size = query.shape[0]
     position = lax.axis_index("cp").astype(jnp.int32)
     cp = position.reshape(1)
-    kv = jnp.concatenate([keys, values], axis=1)
+    packed = jax.ShapeDtypeStruct((size, 2 * HDIM), jnp.bfloat16)
+    kv = simple(pack_kernel, packed, keys, values)
     from1 = chip_shift(kv, 1)
     from3 = chip_shift(kv, 3)
     from2 = chip_shift(kv, 2)
@@ -177,34 +223,23 @@
     stats = call_stats((1, 3), cp, stats, (from1, from3), rows)
     stats = call_stats((2,), cp, stats, (from2,), rows)
 
-    other = core_swap(stats).reshape(2, 6, size)[::-1].reshape(4, 3, size)
-    mine = stats.reshape(4, 3, size)
-    top = jnp.maximum(mine[:, 0], other[:, 0])
-    f_mine = jnp.exp2((mine[:, 0] - top) * EXP_SCALE)
-    f_other = jnp.exp2((other[:, 0] - top) * EXP_SCALE)
-    total = mine[:, 1] * f_mine + other[:, 1] * f_other
-    weighted = mine[:, 2] * f_mine + other[:, 2] * f_other
-    fin = jnp.stack([top * EXP_SCALE + jnp.log2(total), weighted / total], axis=1).reshape(8, size)
-
-    dq, part2 = call_grads(2, cp, None, from2, rows, fin)
+    dq, part2, fin = call_grads(2, cp, (stats, core_swap(stats)), from2, rows)
     back2 = chip_shift(part2, 2)
-    dq, part1 = call_grads(1, cp, dq, from1, rows, fin)
+    dq, part1 = call_grads(1, cp, (dq, fin), from1, rows)
     back1 = chip_shift(part1, 3)
-    dq, part3 = call_grads(3, cp, dq, from3, rows, fin)
+    dq, part3 = call_grads(3, cp, (dq, fin), from3, rows)
     back3 = chip_shift(part3, 1)
-    dq, own = call_grads(0, cp, dq, kv, rows, fin)
-
-    dq_other = core_swap(dq[size:])
-    grad_query = ((dq[:size] + dq_other) * SCALE).astype(jnp.bfloat16)
-
-    f32 = jnp.float32
-    half = (own + back1.astype(f32) + back3.astype(f32) + back2.astype(f32)).astype(jnp.bfloat16)
-    dkv = half.astype(f32) + hd_swap(half).astype(f32)
-    return (
-        grad_query,
-        (dkv[:, :HDIM] * SCALE).astype(jnp.bfloat16),
-        dkv[:, HDIM:].astype(jnp.bfloat16),
-    )
+    dq, own = call_grads(0, cp, (dq, fin), kv, rows)
+
+    dq_other = core_swap(dq[1])
+    grad_query = simple(query_kernel, jax.ShapeDtypeStruct(query.shape, query.dtype), dq, dq_other)
+    total = jax.ShapeDtypeStruct(own.shape, own.dtype)
+    half = simple(add_kernel, total, own, back2, cost=BLOCK_COST)
+    half = simple(add_kernel, total, half, back1, cost=BLOCK_COST)
+    half = simple(add_kernel, packed, half, back3)
+    other = hd_swap(half)
+    grad_keys, grad_values = simple(last_kernel, [jax.ShapeDtypeStruct(keys.shape, keys.dtype)] * 2, half, other)
+    return grad_query, grad_keys, grad_values
 
 
 def solution(mesh):

time: 62.8 us -> 65.7 us (1.046)
  Pallas kernels: 6.33 us -> 17.2 us
  waiting for transfers between devices: 24.2 us -> 16.6 us
  local copies, waits for them, and re-layouts: 4.1 us -> 6.97 us
  starting transfers between devices: 25.4 us -> 23.3 us
  other arithmetic: 1.72 us -> 0 us
    pallas_call x0 -> x6, Pallas kernels: none -> 11.5 us  [simple(): pl.pallas_call(kernel, out_shape=out, in_specs=[VM] * len(args), out_spec...]
    ppermute x6, waiting for transfers between devices: 16 us -> 6.96 us  [chip_shift(): return lax.ppermute(array, 'cp', pairs)]
    unnamed x9 -> x26, local copies, waits for them, and re-layouts: 2.34 us -> 6.94 us
    ppermute x6, starting transfers between devices: 21.4 us -> 19.4 us  [chip_shift(): return lax.ppermute(array, 'cp', pairs)]
    convert_element_type x3 -> x0, other arithmetic: 1.62 us -> none  [the longest x1 0.82 us: body(): grad_query = ((dq[:size] + dq_other) * SCALE).astype(jnp.bfloat16)]
    ppermute x1, waiting for transfers between devices: 5.72 us -> 7.06 us  [hd_swap(): return lax.ppermute(array, 'hd', [(0, 1), (1, 0)])]
    concatenate x1 -> x0, local copies, waits for them, and re-layouts: 0.94 us -> none  [body(): kv = jnp.concatenate([keys, values], axis=1)]
    slice x4 -> x0, local copies, waits for them, and re-layouts: 0.75 us -> none  [the longest x1 0.67 us: body(): dkv[:, HDIM:].astype(jnp.bfloat16)]
  transfers between devices with their start and end apart: 12 -> 12, of which waited for: 8 -> 5; matrix products, arithmetic and copies ran while one was open for 5% -> 0% of each run, Pallas kernels for 9% -> 23%
where the time goes in v2:
time: 65.7 us; the launch traced here: 64.9 us
  starting transfers between devices  23.3 us (35%)
  Pallas kernels  17.2 us (26%)
  waiting for transfers between devices  16.6 us (25%)
  local copies, waits for them, and re-layouts  6.97 us (11%)
  between operations  0.79 us (1%)
    ppermute x6, starting transfers between devices, chip_shift(): return lax.ppermute(array, 'cp', pairs)  19.4 us
    pallas_call x6, Pallas kernels, simple(): pl.pallas_call(kernel, out_shape=out, in_specs=[VM] * len(args), out_spec...  11.5 us
    ppermute x1, waiting for transfers between devices, hd_swap(): return lax.ppermute(array, 'hd', [(0, 1), (1, 0)])  7.06 us
    ppermute x6, waiting for transfers between devices, chip_shift(): return lax.ppermute(array, 'cp', pairs)  6.96 us
    unnamed x26, local copies, waits for them, and re-layouts  6.94 us
    pallas_call x4, Pallas kernels, call_grads(): pl.pallas_call(functools.partial(grads_kernel, shift, first), out_shape=o...  3.66 us
    ppermute x1, starting transfers between devices, hd_swap(): return lax.ppermute(array, 'hd', [(0, 1), (1, 0)])  3.2 us
    ppermute x5, waiting for transfers between devices, core_swap(): return lax.ppermute(array, 'cp', [(i, i ^ 1) for i in range(n)])  2.57 us
  transfers between devices with their start and end apart: 12, of which 5 were waited for; matrix products, arithmetic and copies ran while one was open for 0% of the time, Pallas kernels for 23%

profile of v2, /device:TPU:0, one launch (start us, length us, event | category | flops | bytes accessed | tf_op | source)
XLA Modules:
  0.0 64.9 jit_solution(5553159628310328561)
XLA Ops:
  0.6 0.0 copy-start.3
  0.6 0.0 copy-start.4
  0.7 0.1 collective-permute-start
  0.7 0.5 collective-permute-start.1
  1.2 1.7 %shard_map.76.refs_0_.refs_2_ = bf16[512,256]{1,0:T(8,128)(2,1)} custom-call(bf16[512,128]{1,0:T(8,128)(2,1)} %keys.1, bf16[512,128]{1,0:T(8,128)(2,1)} %values.1), custom_call_target="tpu_custom_call" | custom-call | bytes 1024 | tf_op jit(solution)/shard_map/pallas_call | solution.py:166
  3.0 2.8 %collective-permute-start.4 = (bf16[512,256]{1,0:T(8,128)(2,1)}, bf16[512,256]{1,0:T(8,128)(2,1)S(1)}, u32[]{:S(2)}, u32[]{:S(2)}) collective-permute-start(bf16[512,256]{1,0:T(8,128)(2,1)} %shard_map.76.refs_0_.refs_2_), channel_id=1, source_target_pairs={{0,12},{2,14},{4,0},{6,2},{8,4},{10,6},{12,8},{14,10},{16,28},{18,... | collective-permute-start | bytes 786440 | tf_op jit(solution)/shard_map/ppermute | solution.py:30
  5.8 0.0 collective-permute-start.3
  5.8 0.0 collective-permute-start.2
  5.8 1.4 %collective-permute-done.2.refs_6_.refs_7_.refs_8_ = s32[1,512]{1,0:T(1,128)S(1)} collective-permute-done((s32[1,512]{1,0:T(1,128)}, s32[1,512]{1,0:T(1,128)S(1)}, u32[]{:S(2)}, u32[]{:S(2)}) %collective-permute-start.2) | collective-permute-done | bytes 2080 | tf_op jit(solution)/shard_map/ppermute | solution.py:35
  7.2 2.3 %collective-permute-start.5 = (bf16[512,256]{1,0:T(8,128)(2,1)}, bf16[512,256]{1,0:T(8,128)(2,1)S(1)}, u32[]{:S(2)}, u32[]{:S(2)}) collective-permute-start(bf16[512,256]{1,0:T(8,128)(2,1)} %shard_map.76.refs_0_.refs_2_), channel_id=1, source_target_pairs={{0,8},{2,10},{4,12},{6,14},{8,0},{10,2},{12,4},{14,6},{16,24},{18,... | collective-permute-start | bytes 786440 | tf_op jit(solution)/shard_map/ppermute | solution.py:30
  9.5 0.0 copy-start.5
  9.5 0.0 collective-permute-done.refs_2_.refs_3_.refs_4_
  9.5 0.0 collective-permute-done.1.refs_4_.refs_5_.refs_6_
  9.5 0.0 copy-done.3
  9.5 0.0 copy-done.4
  9.5 0.7 %copy-done.5 = s32[512]{0:T(512)S(1)} copy-done((s32[512]{0:T(512)S(1)}, s32[512]{0:T(512)}, u32[]{:S(2)}) %copy-start.5) | copy-done | bytes 2072
  10.1 0.0 copy-start.1
  10.1 0.9 %copy-done.1 = bf16[512,256]{1,0:T(8,128)(2,1)S(1)} copy-done((bf16[512,256]{1,0:T(8,128)(2,1)S(1)}, bf16[512,256]{1,0:T(8,128)(2,1)}, u32[]{:S(2)}) %copy-start.1) | copy-done | bytes 262168
  11.1 0.0 copy-start.7
  11.1 0.8 %copy-done.7 = f32[12,512]{1,0:T(8,128)S(1)} copy-done((f32[12,512]{1,0:T(8,128)S(1)}, f32[12,512]{1,0:T(8,128)}, u32[]{:S(2)}) %copy-start.7) | copy-done | bytes 24600
  11.8 2.1 %stats.3.stats_in = f32[12,512]{1,0:T(8,128)S(1)} custom-call(s32[1]{0:T(128)} %bitcast.pos_ref, f32[12,512]{1,0:T(8,128)S(1)} %copy-done.7, bf16[512,256]{1,0:T(8,128)(2,1)S(1)} %copy-done.1, bf16[512,256]{1,0:T(8,128)(2,1)S(1)} %copy-done.3, bf16[512,256]{1,0:T(8,128)(2,1)S(1)} %collective-permute-done.refs_2_.refs_3_.refs_4_, ...), custom_call_target="tpu_custom_call" | custom-call | flops 1342177280 | bytes 1048576 | tf_op jit(solution)/shard_map/stats/pallas_call | solution.py:176
  13.9 3.7 %collective-permute-done.4.refs_1_.refs_2_ = bf16[512,256]{1,0:T(8,128)(2,1)S(1)} collective-permute-done((bf16[512,256]{1,0:T(8,128)(2,1)}, bf16[512,256]{1,0:T(8,128)(2,1)S(1)}, u32[]{:S(2)}, u32[]{:S(2)}) %collective-permute-start.4) | collective-permute-done | bytes 262176 | tf_op jit(solution)/shard_map/ppermute | solution.py:30
  17.6 3.3 %collective-permute-done.3.refs_0_.refs_2_ = bf16[512,256]{1,0:T(8,128)(2,1)S(1)} collective-permute-done((bf16[512,256]{1,0:T(8,128)(2,1)}, bf16[512,256]{1,0:T(8,128)(2,1)S(1)}, u32[]{:S(2)}, u32[]{:S(2)}) %collective-permute-start.3) | collective-permute-done | bytes 262176 | tf_op jit(solution)/shard_map/ppermute | solution.py:30
  20.9 0.0 collective-permute-done.5.refs_0_.refs_2_
  20.9 0.1 collective-permute-start.6
  21.0 1.2 %collective-permute-done.6.refs_1_ = f32[12,512]{1,0:T(8,128)S(1)} collective-permute-done((f32[12,512]{1,0:T(8,128)S(1)}, f32[12,512]{1,0:T(8,128)S(1)}, u32[]{:S(2)}, u32[]{:S(2)}) %collective-permute-start.6) | collective-permute-done | bytes 24608 | tf_op jit(solution)/shard_map/ppermute | solution.py:35
  22.2 0.1 grads.4
  22.3 5.4 %collective-permute-start.8 = (bf16[512,256]{1,0:T(8,128)(2,1)S(1)}, bf16[512,256]{1,0:T(8,128)(2,1)S(1)}, u32[]{:S(2)}, u32[]{:S(2)}) collective-permute-start(bf16[512,256]{1,0:T(8,128)(2,1)S(1)} %get-tuple-element.20), channel_id=1, source_target_pairs={{0,8},{2,10},{4,12},{6,14},{8,0},{10,2},{12,4},{14,6},{16,24},{18,... | collective-permute-start | bytes 786440 | tf_op jit(solution)/shard_map/ppermute | solution.py:30
  27.7 0.1 grads.5
  27.8 0.0 copy-start.2
  27.9 0.1 grads.6
  28.0 6.8 %collective-permute-start.10 = (bf16[512,256]{1,0:T(8,128)(2,1)S(1)}, bf16[512,256]{1,0:T(8,128)(2,1)S(1)}, u32[]{:S(2)}, u32[]{:S(2)}) collective-permute-start(bf16[512,256]{1,0:T(8,128)(2,1)S(1)} %get-tuple-element.22), channel_id=1, source_target_pairs={{0,4},{2,6},{4,8},{6,10},{8,12},{10,14},{12,0},{14,2},{16,20},{18,... | collective-permute-start | bytes 786440 | tf_op jit(solution)/shard_map/ppermute | solution.py:30
  34.8 2.1 %collective-permute-start.9 = (bf16[512,256]{1,0:T(8,128)(2,1)S(1)}, bf16[512,256]{1,0:T(8,128)(2,1)S(1)}, u32[]{:S(2)}, u32[]{:S(2)}) collective-permute-start(bf16[512,256]{1,0:T(8,128)(2,1)S(1)} %get-tuple-element.21), channel_id=1, source_target_pairs={{0,12},{2,14},{4,0},{6,2},{8,4},{10,6},{12,8},{14,10},{16,28},{18,... | collective-permute-start | bytes 786440 | tf_op jit(solution)/shard_map/ppermute | solution.py:30
  36.9 0.0 copy-done.2
  36.9 3.2 %grads.7 = (f32[2,256,512]{2,1,0:T(8,128)S(1)}, f32[512,256]{1,0:T(8,128)S(1)}) custom-call(s32[1]{0:T(128)} %bitcast.pos_ref, f32[2,256,512]{2,1,0:T(8,128)S(1)} %get-tuple-element.17.refs_0_, f32[8,512]{1,0:T(8,128)S(1)} %get-tuple-element.15.refs_1_, bf16[512,256]{1,0:T(8,128)(2,1)S(1)} %copy-done.2, bf16[512,256]{1,0:T(8,128)(2,1)S(1)} %copy-done.3, ...), custom_call_target="tpu_custom_call" | custom-call | bytes 1024 | tf_op jit(solution)/shard_map/grads/pallas_call | solution.py:196
  40.1 0.0 copy-start.6
  40.2 0.8 %copy-done.6 = f32[512,256]{1,0:T(8,128)} copy-done((f32[512,256]{1,0:T(8,128)}, f32[512,256]{1,0:T(8,128)S(1)}, u32[]{:S(2)}) %copy-start.6) | copy-done | bytes 524312
  40.9 0.0 copy-start
  41.0 0.1 collective-permute-start.7
  41.1 0.0 collective-permute-done.8.part
  41.1 0.0 copy-start.11
  41.1 0.9 %copy-done.11 = bf16[512,256]{1,0:T(8,128)(2,1)} copy-done((bf16[512,256]{1,0:T(8,128)(2,1)}, bf16[512,256]{1,0:T(8,128)(2,1)S(1)}, u32[]{:S(2)}) %copy-start.11) | copy-done | bytes 262168
  42.0 1.9 %shard_map.78.total = f32[512,256]{1,0:T(8,128)} custom-call(f32[512,256]{1,0:T(8,128)} %copy-done.6, bf16[512,256]{1,0:T(8,128)(2,1)} %copy-done.11), custom_call_target="tpu_custom_call" | custom-call | flops 1342177280 | bytes 1048576 | tf_op jit(solution)/shard_map/pallas_call | solution.py:166
  43.9 0.0 copy-done
  43.9 0.0 collective-permute-done.9.part
  43.9 0.0 copy-start.12
  43.9 0.7 %copy-done.12 = bf16[512,256]{1,0:T(8,128)(2,1)} copy-done((bf16[512,256]{1,0:T(8,128)(2,1)}, bf16[512,256]{1,0:T(8,128)(2,1)S(1)}, u32[]{:S(2)}) %copy-start.12) | copy-done | bytes 262168
  44.6 2.0 %shard_map.79.total = f32[512,256]{1,0:T(8,128)} custom-call(f32[512,256]{1,0:T(8,128)} %shard_map.78.total, bf16[512,256]{1,0:T(8,128)(2,1)} %copy-done.12), custom_call_target="tpu_custom_call" | custom-call | flops 1342177280 | bytes 1048576 | tf_op jit(solution)/shard_map/pallas_call | solution.py:166
  46.6 0.0 collective-permute-done.10.part
  46.6 0.0 copy-start.10
  46.6 0.7 %copy-done.10 = bf16[512,256]{1,0:T(8,128)(2,1)} copy-done((bf16[512,256]{1,0:T(8,128)(2,1)}, bf16[512,256]{1,0:T(8,128)(2,1)S(1)}, u32[]{:S(2)}) %copy-start.10) | copy-done | bytes 262168
  47.3 1.9 %shard_map.80.mine = bf16[512,256]{1,0:T(8,128)(2,1)} custom-call(f32[512,256]{1,0:T(8,128)} %shard_map.79.total, bf16[512,256]{1,0:T(8,128)(2,1)} %copy-done.10), custom_call_target="tpu_custom_call" | custom-call | bytes 1024 | tf_op jit(solution)/shard_map/pallas_call | solution.py:166
  49.2 3.2 %collective-permute-start.11 = (bf16[512,256]{1,0:T(8,128)(2,1)}, bf16[512,256]{1,0:T(8,128)(2,1)S(1)}, u32[]{:S(2)}, u32[]{:S(2)}) collective-permute-start(bf16[512,256]{1,0:T(8,128)(2,1)} %shard_map.80.mine), channel_id=1, source_target_pairs={{0,1},{1,0},{2,3},{3,2},{4,5},{5,4},{6,7},{7,6},{8,9},{9,8},{10,11... | collective-permute-start | bytes 786440 | tf_op jit(solution)/shard_map/ppermute | solution.py:39
  52.3 7.1 %collective-permute-done.11.other = bf16[512,256]{1,0:T(8,128)(2,1)S(1)} collective-permute-done((bf16[512,256]{1,0:T(8,128)(2,1)}, bf16[512,256]{1,0:T(8,128)(2,1)S(1)}, u32[]{:S(2)}, u32[]{:S(2)}) %collective-permute-start.11) | collective-permute-done | bytes 262176 | tf_op jit(solution)/shard_map/ppermute | solution.py:39
  59.4 0.0 copy-start.9
  59.4 0.7 %copy-done.9 = bf16[512,256]{1,0:T(8,128)(2,1)} copy-done((bf16[512,256]{1,0:T(8,128)(2,1)}, bf16[512,256]{1,0:T(8,128)(2,1)S(1)}, u32[]{:S(2)}) %copy-start.9) | copy-done | bytes 262168
  60.1 1.8 %shard_map.81 = (bf16[512,128]{1,0:T(8,128)(2,1)}, bf16[512,128]{1,0:T(8,128)(2,1)}) custom-call(bf16[512,256]{1,0:T(8,128)(2,1)} %shard_map.80.mine, bf16[512,256]{1,0:T(8,128)(2,1)} %copy-done.9), custom_call_target="tpu_custom_call" | custom-call | bytes 1024 | tf_op jit(solution)/shard_map/pallas_call | solution.py:166
  61.9 0.0 collective-permute-done.7.other
  61.9 0.0 copy-start.8
  61.9 0.8 %copy-done.8 = f32[256,512]{1,0:T(8,128)} copy-done((f32[256,512]{1,0:T(8,128)}, f32[256,512]{1,0:T(8,128)S(1)}, u32[]{:S(2)}) %copy-start.8) | copy-done | bytes 524312
  62.7 2.2 %shard_map.77 = bf16[512,256]{1,0:T(8,128)(2,1)} custom-call(f32[2,256,512]{2,1,0:T(8,128)} %copy-done, f32[256,512]{1,0:T(8,128)} %copy-done.8), custom_call_target="tpu_custom_call" | custom-call | bytes 1024 | tf_op jit(solution)/shard_map/pallas_call | solution.py:166
  (3 shorter events, 0.0 us)
Async XLA Ops:
  0.6 8.8 %copy-start.3 = (bf16[512,256]{1,0:T(8,128)(2,1)S(1)}, bf16[512,256]{1,0:T(8,128)(2,1)}, u32[]{:S(2)}) copy-start(bf16[512,256]{1,0:T(8,128)(2,1)} %refs_3_.11) | copy-start | bytes 786436
  0.6 8.8 %copy-start.4 = (bf16[512,256]{1,0:T(8,128)(2,1)S(1)}, bf16[512,256]{1,0:T(8,128)(2,1)}, u32[]{:S(2)}) copy-start(bf16[512,256]{1,0:T(8,128)(2,1)} %refs_5_.7) | copy-start | bytes 786436
  0.7 8.8 %collective-permute-start = (bf16[512,256]{1,0:T(8,128)(2,1)}, bf16[512,256]{1,0:T(8,128)(2,1)S(1)}, u32[]{:S(2)}, u32[]{:S(2)}) collective-permute-start(bf16[512,256]{1,0:T(8,128)(2,1)} %refs_3_.11), channel_id=1, source_target_pairs={{0,2},{2,0},{4,6},{6,4},{8,10},{10,8},{12,14},{14,12},{16,18},{18,... | collective-permute-start | bytes 786440 | tf_op jit(solution)/shard_map/ppermute | solution.py:35
  0.7 8.7 %collective-permute-start.1 = (bf16[512,256]{1,0:T(8,128)(2,1)}, bf16[512,256]{1,0:T(8,128)(2,1)S(1)}, u32[]{:S(2)}, u32[]{:S(2)}) collective-permute-start(bf16[512,256]{1,0:T(8,128)(2,1)} %refs_5_.7), channel_id=1, source_target_pairs={{0,2},{2,0},{4,6},{6,4},{8,10},{10,8},{12,14},{14,12},{16,18},{18,... | collective-permute-start | bytes 786440 | tf_op jit(solution)/shard_map/ppermute | solution.py:35
  3.0 14.6 %collective-permute-start.4 = (bf16[512,256]{1,0:T(8,128)(2,1)}, bf16[512,256]{1,0:T(8,128)(2,1)S(1)}, u32[]{:S(2)}, u32[]{:S(2)}) collective-permute-start(bf16[512,256]{1,0:T(8,128)(2,1)} %shard_map.76.refs_0_.refs_2_), channel_id=1, source_target_pairs={{0,12},{2,14},{4,0},{6,2},{8,4},{10,6},{12,8},{14,10},{16,28},{18,... | collective-permute-start | bytes 786440 | tf_op jit(solution)/shard_map/ppermute | solution.py:30
  5.8 15.1 %collective-permute-start.3 = (bf16[512,256]{1,0:T(8,128)(2,1)}, bf16[512,256]{1,0:T(8,128)(2,1)S(1)}, u32[]{:S(2)}, u32[]{:S(2)}) collective-permute-start(bf16[512,256]{1,0:T(8,128)(2,1)} %shard_map.76.refs_0_.refs_2_), channel_id=1, source_target_pairs={{0,4},{2,6},{4,8},{6,10},{8,12},{10,14},{12,0},{14,2},{16,20},{18,... | collective-permute-start | bytes 786440 | tf_op jit(solution)/shard_map/ppermute | solution.py:30
  5.8 1.4 %collective-permute-start.2 = (s32[1,512]{1,0:T(1,128)}, s32[1,512]{1,0:T(1,128)S(1)}, u32[]{:S(2)}, u32[]{:S(2)}) collective-permute-start(s32[1,512]{1,0:T(1,128)} %bitcast.4), channel_id=1, source_target_pairs={{0,2},{2,0},{4,6},{6,4},{8,10},{10,8},{12,14},{14,12},{16,18},{18,... | collective-permute-start | bytes 6152 | tf_op jit(solution)/shard_map/ppermute | solution.py:35
  7.2 13.7 %collective-permute-start.5 = (bf16[512,256]{1,0:T(8,128)(2,1)}, bf16[512,256]{1,0:T(8,128)(2,1)S(1)}, u32[]{:S(2)}, u32[]{:S(2)}) collective-permute-start(bf16[512,256]{1,0:T(8,128)(2,1)} %shard_map.76.refs_0_.refs_2_), channel_id=1, source_target_pairs={{0,8},{2,10},{4,12},{6,14},{8,0},{10,2},{12,4},{14,6},{16,24},{18,... | collective-permute-start | bytes 786440 | tf_op jit(solution)/shard_map/ppermute | solution.py:30
  9.5 0.7 %copy-start.5 = (s32[512]{0:T(512)S(1)}, s32[512]{0:T(512)}, u32[]{:S(2)}) copy-start(s32[512]{0:T(512)} %param.9) | copy-start | bytes 6148
  10.1 0.9 %copy-start.1 = (bf16[512,256]{1,0:T(8,128)(2,1)S(1)}, bf16[512,256]{1,0:T(8,128)(2,1)}, u32[]{:S(2)}) copy-start(bf16[512,256]{1,0:T(8,128)(2,1)} %shard_map.76.refs_0_.refs_2_) | copy-start | bytes 786436
  11.1 0.8 %copy-start.7 = (f32[12,512]{1,0:T(8,128)S(1)}, f32[12,512]{1,0:T(8,128)}, u32[]{:S(2)}) copy-start(f32[12,512]{1,0:T(8,128)} %constant.7.clone.1.stats_in) | copy-start | bytes 73732
  20.9 1.3 %collective-permute-start.6 = (f32[12,512]{1,0:T(8,128)S(1)}, f32[12,512]{1,0:T(8,128)S(1)}, u32[]{:S(2)}, u32[]{:S(2)}) collective-permute-start(f32[12,512]{1,0:T(8,128)S(1)} %stats.5.refs_0_), channel_id=1, source_target_pairs={{0,2},{2,0},{4,6},{6,4},{8,10},{10,8},{12,14},{14,12},{16,18},{18,... | collective-permute-start | bytes 73736 | tf_op jit(solution)/shard_map/ppermute | solution.py:35
  22.3 18.8 %collective-permute-start.8 = (bf16[512,256]{1,0:T(8,128)(2,1)S(1)}, bf16[512,256]{1,0:T(8,128)(2,1)S(1)}, u32[]{:S(2)}, u32[]{:S(2)}) collective-permute-start(bf16[512,256]{1,0:T(8,128)(2,1)S(1)} %get-tuple-element.20), channel_id=1, source_target_pairs={{0,8},{2,10},{4,12},{6,14},{8,0},{10,2},{12,4},{14,6},{16,24},{18,... | collective-permute-start | bytes 786440 | tf_op jit(solution)/shard_map/ppermute | solution.py:30
  27.8 9.0 %copy-start.2 = (bf16[512,256]{1,0:T(8,128)(2,1)S(1)}, bf16[512,256]{1,0:T(8,128)(2,1)}, u32[]{:S(2)}) copy-start(bf16[512,256]{1,0:T(8,128)(2,1)} %shard_map.76.refs_0_.refs_2_) | copy-start | bytes 786436
  28.0 18.6 %collective-permute-start.10 = (bf16[512,256]{1,0:T(8,128)(2,1)S(1)}, bf16[512,256]{1,0:T(8,128)(2,1)S(1)}, u32[]{:S(2)}, u32[]{:S(2)}) collective-permute-start(bf16[512,256]{1,0:T(8,128)(2,1)S(1)} %get-tuple-element.22), channel_id=1, source_target_pairs={{0,4},{2,6},{4,8},{6,10},{8,12},{10,14},{12,0},{14,2},{16,20},{18,... | collective-permute-start | bytes 786440 | tf_op jit(solution)/shard_map/ppermute | solution.py:30
  34.8 9.1 %collective-permute-start.9 = (bf16[512,256]{1,0:T(8,128)(2,1)S(1)}, bf16[512,256]{1,0:T(8,128)(2,1)S(1)}, u32[]{:S(2)}, u32[]{:S(2)}) collective-permute-start(bf16[512,256]{1,0:T(8,128)(2,1)S(1)} %get-tuple-element.21), channel_id=1, source_target_pairs={{0,12},{2,14},{4,0},{6,2},{8,4},{10,6},{12,8},{14,10},{16,28},{18,... | collective-permute-start | bytes 786440 | tf_op jit(solution)/shard_map/ppermute | solution.py:30
  40.1 0.8 %copy-start.6 = (f32[512,256]{1,0:T(8,128)}, f32[512,256]{1,0:T(8,128)S(1)}, u32[]{:S(2)}) copy-start(f32[512,256]{1,0:T(8,128)S(1)} %get-tuple-element.19.total) | copy-start | bytes 1572868
  40.9 3.0 %copy-start = (f32[2,256,512]{2,1,0:T(8,128)}, f32[2,256,512]{2,1,0:T(8,128)S(1)}, u32[]{:S(2)}) copy-start(f32[2,256,512]{2,1,0:T(8,128)S(1)} %get-tuple-element.18.mine) | copy-start | bytes 3145732
  41.0 20.9 %collective-permute-start.7 = (f32[256,512]{1,0:T(8,128)S(1)}, f32[256,512]{1,0:T(8,128)S(1)}, u32[]{:S(2)}, u32[]{:S(2)}) collective-permute-start(f32[256,512]{1,0:T(8,128)S(1)} %slice_bitcast_fusion), channel_id=1, source_target_pairs={{0,2},{2,0},{4,6},{6,4},{8,10},{10,8},{12,14},{14,12},{16,18},{18,... | collective-permute-start | bytes 1572872 | tf_op jit(solution)/shard_map/ppermute | solution.py:35
  41.1 0.9 %copy-start.11 = (bf16[512,256]{1,0:T(8,128)(2,1)}, bf16[512,256]{1,0:T(8,128)(2,1)S(1)}, u32[]{:S(2)}) copy-start(bf16[512,256]{1,0:T(8,128)(2,1)S(1)} %collective-permute-done.8.part) | copy-start | bytes 786436
  43.9 0.7 %copy-start.12 = (bf16[512,256]{1,0:T(8,128)(2,1)}, bf16[512,256]{1,0:T(8,128)(2,1)S(1)}, u32[]{:S(2)}) copy-start(bf16[512,256]{1,0:T(8,128)(2,1)S(1)} %collective-permute-done.9.part) | copy-start | bytes 786436
  46.6 0.7 %copy-start.10 = (bf16[512,256]{1,0:T(8,128)(2,1)}, bf16[512,256]{1,0:T(8,128)(2,1)S(1)}, u32[]{:S(2)}) copy-start(bf16[512,256]{1,0:T(8,128)(2,1)S(1)} %collective-permute-done.10.part) | copy-start | bytes 786436
  49.2 10.3 %collective-permute-start.11 = (bf16[512,256]{1,0:T(8,128)(2,1)}, bf16[512,256]{1,0:T(8,128)(2,1)S(1)}, u32[]{:S(2)}, u32[]{:S(2)}) collective-permute-start(bf16[512,256]{1,0:T(8,128)(2,1)} %shard_map.80.mine), channel_id=1, source_target_pairs={{0,1},{1,0},{2,3},{3,2},{4,5},{5,4},{6,7},{7,6},{8,9},{9,8},{10,11... | collective-permute-start | bytes 786440 | tf_op jit(solution)/shard_map/ppermute | solution.py:39
  59.4 0.7 %copy-start.9 = (bf16[512,256]{1,0:T(8,128)(2,1)}, bf16[512,256]{1,0:T(8,128)(2,1)S(1)}, u32[]{:S(2)}) copy-start(bf16[512,256]{1,0:T(8,128)(2,1)S(1)} %collective-permute-done.11.other) | copy-start | bytes 786436
  61.9 0.8 %copy-start.8 = (f32[256,512]{1,0:T(8,128)}, f32[256,512]{1,0:T(8,128)S(1)}, u32[]{:S(2)}) copy-start(f32[256,512]{1,0:T(8,128)S(1)} %collective-permute-done.7.other) | copy-start | bytes 1572868

commit v3 on v2

v3 whole, which is shorter than its diff:
```python
import functools
import math

import jax
import jax.numpy as jnp
from jax import lax
from jax.experimental import pallas as pl
from jax.experimental.pallas import tpu as pltpu
from jax.sharding import PartitionSpec as P

HDIM = 128
GROUP = 8
SCALE = 1.0 / math.sqrt(HDIM)
EXP_SCALE = SCALE * math.log2(math.e)
MASKED = -1e30
FLOOR = -1e29
KERNEL_VMEM = 16 * 2**20

NT = (((1,), (1,)), ((), ()))
NN = (((1,), (0,)), ((), ()))
TN = (((0,), (0,)), ((), ()))


def dot(a, b, dims):
    return lax.dot_general(a, b, dims, preferred_element_type=jnp.float32)


def chip_shift(array, even, odd):
    n = lax.axis_size("cp")
    pairs = [(i, i - i % GROUP + (i % GROUP + 2 * (odd if i % 2 else even)) % GROUP) for i in range(n)]
    return lax.ppermute(array, "cp", pairs)


def core_swap(array):
    n = lax.axis_size("cp")
    return lax.ppermute(array, "cp", [(i, i ^ 1) for i in range(n)])


def hd_swap(array):
    return lax.ppermute(array, "hd", [(0, 1), (1, 0)])


def masked_scores(k, q, starts, row_base, key_base, diagonal):
    s = dot(k, q, NT)
    key_pos = key_base + lax.broadcasted_iota(jnp.int32, s.shape, 0)
    allowed = key_pos >= starts
    if diagonal:
        row_pos = row_base + lax.broadcasted_iota(jnp.int32, s.shape, 1)
        allowed = allowed & (key_pos <= row_pos)
    return jnp.where(allowed, s, MASKED)


def distance(slot, cp):
    return slot if slot < 2 else slot + lax.rem(cp, 2) * (5 - 2 * slot)


def stats_kernel(shifts, pos_ref, *refs):
    n = len(shifts)
    first = shifts[0] == 0
    if not first:
        stats_in, *refs = refs
    blocks, (q_own, q_sib, g_own, g_sib, st_own, st_sib), outs = refs[:n], refs[n : n + 6], refs[n + 6 :]
    stats, kept = outs[0], outs[1:]
    cp = pos_ref[0]
    in_group = lax.rem(cp, GROUP)
    size = q_own.shape[0]
    if first:
        for at in range(0, 12, 3):
            stats[at : at + 1, :] = jnp.full((1, size), FLOOR)
            stats[at + 1 : at + 3, :] = jnp.zeros((2, size))
    else:
        stats[...] = stats_in[...]
    for i, (kv, shift) in enumerate(zip(blocks, shifts)):
        chips = distance(shift, cp)
        key_block = cp - 2 * chips
        for group, (q, g, st) in enumerate(((q_own, g_own, st_own), (q_sib, g_sib, st_sib))):
            row_block = cp if group == 0 else cp + 1 - 2 * lax.rem(cp, 2)

            def work(i=i, kv=kv, q=q, g=g, st=st, group=group, shift=shift, key_block=key_block, row_block=row_block):
                for head in range(2):
                    cols = pl.ds(head * HDIM, HDIM)
                    s = masked_scores(
                        kv[0], q[:, cols], st[...], row_block * size, key_block * size, shift == 0 and group == 0
                    )
                    dp = dot(kv[1], g[:, cols], NT)
                    if shift:
                        kept[2 * i][2 * group + head] = s
                        kept[2 * i + 1][2 * group + head] = dp
                    at = 3 * (2 * group + head)
                    m = stats[at : at + 1, :]
                    new = jnp.maximum(m, jnp.max(s, axis=0, keepdims=True))
                    p = jnp.exp2((s - new) * EXP_SCALE)
                    f = jnp.exp2((m - new) * EXP_SCALE)
                    stats[at : at + 1, :] = new
                    stats[at + 1 : at + 2, :] = stats[at + 1 : at + 2, :] * f + jnp.sum(p, axis=0, keepdims=True)
                    stats[at + 2 : at + 3, :] = stats[at + 2 : at + 3, :] * f + jnp.sum(p * dp, axis=0, keepdims=True)

            if shift == 0 and group == 0:
                work()
            elif shift == 0:
                pl.when(lax.rem(cp, 2) == 0)(work)
            else:
                pl.when(in_group >= 2 * chips)(work)


def merged(stats, other, at, other_at):
    m, m2 = stats[at : at + 1, :], other[other_at : other_at + 1, :]
    top = jnp.maximum(m, m2)
    f, f2 = jnp.exp2((m - top) * EXP_SCALE), jnp.exp2((m2 - top) * EXP_SCALE)
    total = stats[at + 1 : at + 2, :] * f + other[other_at + 1 : other_at + 2, :] * f2
    weighted = stats[at + 2 : at + 3, :] * f + other[other_at + 2 : other_at + 3, :] * f2
    return top * EXP_SCALE + jnp.log2(total), weighted / total


def grads_kernel(shift, first, pos_ref, *refs):
    if first:
        stats, other, kv, q_own, q_sib, g_own, g_sib, *refs = refs
        kept, (dq, dkv, fin, acc) = refs[:2], refs[2:]
        for s in range(4):
            log_sum, delta = merged(stats, other, 3 * s, 3 * (s ^ 2))
            fin[2 * s : 2 * s + 1, :] = log_sum
            fin[2 * s + 1 : 2 * s + 2, :] = delta
        dq[...] = jnp.zeros_like(dq)
    else:
        dq_in, fin, kv, q_own, q_sib, g_own, g_sib, *refs = refs
        kept, (dq, dkv, acc) = refs[:2], refs[2:]
        dq[...] = dq_in[...]
    cp = pos_ref[0]
    in_group = lax.rem(cp, GROUP)
    size = q_own.shape[0]
    acc[...] = jnp.zeros_like(acc)
    chips = distance(shift, cp)
    key_block = cp - 2 * chips
    k_t = kv[0].T
    for group, (q, g) in enumerate(((q_own, g_own), (q_sib, g_sib))):
        row_block = cp if group == 0 else cp + 1 - 2 * lax.rem(cp, 2)

        def work(q=q, g=g, group=group, row_block=row_block):
            for head in range(2):
                cols = pl.ds(head * HDIM, HDIM)
                if shift:
                    s = kept[0][2 * group + head]
                    dp = kept[1][2 * group + head]
                else:
                    s = masked_scores(kv[0], q[:, cols], kept[group][...], row_block * size, key_block * size, group == 0)
                    dp = dot(kv[1], g[:, cols], NT)
                at = 2 * (2 * group + head)
                p = jnp.exp2(s * EXP_SCALE - fin[at : at + 1, :])
                ds = (p * (dp - fin[at + 1 : at + 2, :])).astype(jnp.bfloat16)
                acc[0] += dot(ds, q[:, cols], NN)
                acc[1] += dot(p.astype(jnp.bfloat16), g[:, cols], NN)
                dq[group, cols, :] += dot(k_t, ds, NN)

        if shift == 0 and group == 0:
            work()
        elif shift == 0:
            pl.when(lax.rem(cp, 2) == 0)(work)
        else:
            pl.when(in_group >= 2 * chips)(work)
    dkv[...] = acc[...].astype(dkv.dtype)


def pack_kernel(keys, values, kv, sems):
    copies = [pltpu.make_async_copy(src, kv.at[i], sems.at[i]) for i, src in enumerate((keys, values))]
    for copy in copies:
        copy.start()
    for copy in copies:
        copy.wait()


def query_kernel(mine, other, out, done):
    done[...] = jnp.zeros_like(done)
    out[...] = ((mine[0] + other[...]) * SCALE).T.astype(out.dtype)


def add_kernel(total, part, out):
    out[...] = (total[...] + part[...].astype(jnp.float32)).astype(out.dtype)


def last_kernel(mine, other, _, grad_keys, grad_values):
    total = mine[...].astype(jnp.float32) + other[...].astype(jnp.float32)
    grad_keys[...] = (total[0] * SCALE).astype(grad_keys.dtype)
    grad_values[...] = total[1].astype(grad_values.dtype)


VM = pl.BlockSpec(memory_space=pltpu.VMEM)
SM = pl.BlockSpec(memory_space=pltpu.SMEM)


BLOCK_COST = pl.CostEstimate(flops=4 * 10 * 512 * 512 * 128, bytes_accessed=2**20, transcendentals=0)
LONG_COST = pl.CostEstimate(flops=40 * 10 * 512 * 512 * 128, bytes_accessed=2**20, transcendentals=0)
NO_COST = pl.CostEstimate(flops=0, bytes_accessed=2**10, transcendentals=0)


def simple(kernel, out, *args, cost=NO_COST):
    return pl.pallas_call(
        kernel,
        out_shape=out,
        in_specs=[VM] * len(args),
        out_specs=jax.tree.map(lambda _: VM, out),
        compiler_params=pltpu.CompilerParams(vmem_limit_bytes=8 * 2**20),
        cost_estimate=cost,
    )(*args)


def pack(keys, values):
    return pl.pallas_call(
        pack_kernel,
        out_shape=jax.ShapeDtypeStruct((2, *keys.shape), keys.dtype),
        in_specs=[pl.BlockSpec(memory_space=pltpu.HBM)] * 2,
        out_specs=VM,
        scratch_shapes=[pltpu.SemaphoreType.DMA((2,))],
        compiler_params=pltpu.CompilerParams(vmem_limit_bytes=8 * 2**20),
        cost_estimate=NO_COST,
        name="pack",
    )(keys, values)


def call_stats(shifts, cp, stats, blocks, rows):
    size = blocks[0].shape[1]
    remote = sum(shift > 0 for shift in shifts)
    kept = [jax.ShapeDtypeStruct((4, size, size), jnp.float32)] * (2 * remote)
    return pl.pallas_call(
        functools.partial(stats_kernel, shifts),
        out_shape=[jax.ShapeDtypeStruct((12, size), jnp.float32)] + kept,
        in_specs=[SM] + [VM] * (len(stats) + len(shifts) + len(rows)),
        out_specs=[VM] * (1 + len(kept)),
        compiler_params=pltpu.CompilerParams(vmem_limit_bytes=KERNEL_VMEM),
        cost_estimate=BLOCK_COST,
        name="stats",
    )(cp, *stats, *blocks, *rows)


def call_grads(shift, cp, before, block, rows, kept):
    size = block.shape[1]
    first = shift == 2
    out = [
        jax.ShapeDtypeStruct((2, 2 * HDIM, size), jnp.float32),
        jax.ShapeDtypeStruct((2, size, HDIM), jnp.float32 if shift == 0 else jnp.bfloat16),
    ]
    if first:
        out.append(jax.ShapeDtypeStruct((8, size), jnp.float32))
    return pl.pallas_call(
        functools.partial(grads_kernel, shift, first),
        out_shape=out,
        in_specs=[SM] + [VM] * (3 + 4 + 2),
        out_specs=[VM] * len(out),
        scratch_shapes=[pltpu.VMEM((2, size, HDIM), jnp.float32)],
        compiler_params=pltpu.CompilerParams(vmem_limit_bytes=KERNEL_VMEM),
        cost_estimate=NO_COST if shift == 0 else BLOCK_COST,
        name="grads",
    )(cp, *before, block, *rows[:4], *kept)


def body(query, keys, values, grad_out, doc_start):
    size = query.shape[0]
    position = lax.axis_index("cp").astype(jnp.int32)
    cp = position.reshape(1)
    kv = pack(keys, values)
    from1 = chip_shift(kv, 1, 1)
    from3 = chip_shift(kv, 3, 2)
    from2 = chip_shift(kv, 2, 3)
    starts = doc_start.reshape(1, size)
    rows = (query, core_swap(query), grad_out, core_swap(grad_out), starts, core_swap(starts))

    stats, *_ = call_stats((0,), cp, (), (kv,), rows)
    near = jax.ShapeDtypeStruct(keys.shape, keys.dtype)
    stats, s1, dp1 = call_stats((1,), cp, (stats,), (from1,), rows)
    stats, s2, dp2 = call_stats((2,), cp, (stats,), (from2,), rows)
    stats, s3, dp3 = call_stats((3,), cp, (stats,), (from3,), rows)

    dq, part2, fin = call_grads(2, cp, (stats, core_swap(stats)), from2, rows, (s2, dp2))
    back2 = chip_shift(part2, 2, 1)
    dq, part1 = call_grads(1, cp, (dq, fin), from1, rows, (s1, dp1))
    back1 = chip_shift(part1, 3, 3)
    dq, part3 = call_grads(3, cp, (dq, fin), from3, rows, (s3, dp3))
    back3 = chip_shift(part3, 1, 2)
    dq, own = call_grads(0, cp, (dq, fin), kv, rows, rows[4:])

    dq_other = core_swap(dq[1])
    token = jax.ShapeDtypeStruct((8, HDIM), jnp.float32)
    grad_query, done = simple(query_kernel, [jax.ShapeDtypeStruct(query.shape, query.dtype), token], dq, dq_other)
    total = jax.ShapeDtypeStruct(own.shape, own.dtype)
    half = simple(add_kernel, total, own, back2, cost=BLOCK_COST)
    half = simple(add_kernel, total, half, back1, cost=BLOCK_COST)
    half = simple(add_kernel, jax.ShapeDtypeStruct(kv.shape, kv.dtype), half, back3)
    other = hd_swap(half)
    grad_keys, grad_values = simple(last_kernel, [near] * 2, half, other, done)
    return grad_query, grad_keys, grad_values


def solution(mesh):
    in_specs = (P("cp", "hd"), P("cp", None), P("cp", None), P("cp", "hd"), P("cp"))
    out_specs = (P("cp", "hd"), P("cp", None), P("cp", None))
    return jax.shard_map(body, mesh=mesh, in_specs=in_specs, out_specs=out_specs, check_vma=False)
```

time: 65.7 us -> 51.9 us (0.79)
  the two profiles are of different devices: /device:TPU:0 before, /device:TPU:1 now
where the time goes in v3:
time: 51.9 us; the launch traced here: 51.7 us
  starting transfers between devices  21.6 us (42%)
  waiting for transfers between devices  19.2 us (37%)
  Pallas kernels  5.6 us (11%)
  local copies, waits for them, and re-layouts  4.44 us (9%)
  between operations  0.79 us (2%)
    ppermute x6, starting transfers between devices, chip_shift(): return lax.ppermute(array, 'cp', pairs)  12.7 us
    ppermute x6, waiting for transfers between devices, chip_shift(): return lax.ppermute(array, 'cp', pairs)  11.4 us
    ppermute x1, waiting for transfers between devices, hd_swap(): return lax.ppermute(array, 'hd', [(0, 1), (1, 0)])  5.95 us
    ppermute x5, starting transfers between devices, core_swap(): return lax.ppermute(array, 'cp', [(i, i ^ 1) for i in range(n)])  5.81 us
    unnamed x16, local copies, waits for them, and re-layouts  4.4 us
    ppermute x1, starting transfers between devices, hd_swap(): return lax.ppermute(array, 'hd', [(0, 1), (1, 0)])  3.09 us
    pallas_call x4, Pallas kernels, call_grads(): pl.pallas_call(functools.partial(grads_kernel, shift, first), out_shape=o...  2.35 us
    ppermute x5, waiting for transfers between devices, core_swap(): return lax.ppermute(array, 'cp', [(i, i ^ 1) for i in range(n)])  1.9 us
  transfers between devices with their start and end apart: 12, of which 6 were waited for; matrix products, arithmetic and copies ran while one was open for 0% of the time, Pallas kernels for 9%

profile of v3, /device:TPU:1, one launch (start us, length us, event | category | flops | bytes accessed | tf_op | source)
XLA Modules:
  0.0 51.7 jit_solution(15465612351817725074)
XLA Ops:
  0.6 0.0 copy-start.1
  0.6 0.0 copy-start.3
  0.7 1.5 %collective-permute-start = (bf16[512,256]{1,0:T(8,128)(2,1)}, bf16[512,256]{1,0:T(8,128)(2,1)S(1)}, u32[]{:S(2)}, u32[]{:S(2)}) collective-permute-start(bf16[512,256]{1,0:T(8,128)(2,1)} %refs_3_.9), channel_id=1, source_target_pairs={{0,2},{2,0},{4,6},{6,4},{8,10},{10,8},{12,14},{14,12},{16,18},{18,... | collective-permute-start | bytes 786440 | tf_op jit(solution)/shard_map/ppermute | solution.py:36
  2.2 0.1 collective-permute-start.1
  2.3 0.0 copy-start.4
  2.3 0.9 %copy-done.4 = bf16[512,128]{1,0:T(8,128)(2,1)S(1)} copy-done((bf16[512,128]{1,0:T(8,128)(2,1)S(1)}, bf16[512,128]{1,0:T(8,128)(2,1)}, u32[]{:S(2)}) %copy-start.4) | copy-done | bytes 131096
  3.2 0.0 copy-start.5
  3.2 0.9 %copy-done.5 = bf16[512,128]{1,0:T(8,128)(2,1)S(1)} copy-done((bf16[512,128]{1,0:T(8,128)(2,1)S(1)}, bf16[512,128]{1,0:T(8,128)(2,1)}, u32[]{:S(2)}) %copy-start.5) | copy-done | bytes 131096
  4.1 0.0 copy-start.7
  4.1 0.3 pack.1.refs_0_.refs_2_
  4.4 1.4 %collective-permute-start.3 = (bf16[2,512,128]{2,1,0:T(8,128)(2,1)S(1)}, bf16[2,512,128]{2,1,0:T(8,128)(2,1)S(1)}, u32[]{:S(2)}, u32[]{:S(2)}) collective-permute-start(bf16[2,512,128]{2,1,0:T(8,128)(2,1)S(1)} %pack.1.refs_0_.refs_2_), channel_id=1, source_target_pairs={{0,4},{2,6},{4,8},{6,10},{8,12},{10,14},{12,0},{14,2},{16,20},{18,... | collective-permute-start | bytes 786440 | tf_op jit(solution)/shard_map/ppermute | solution.py:31
  5.8 1.4 %collective-permute-start.4 = (bf16[2,512,128]{2,1,0:T(8,128)(2,1)S(1)}, bf16[2,512,128]{2,1,0:T(8,128)(2,1)S(1)}, u32[]{:S(2)}, u32[]{:S(2)}) collective-permute-start(bf16[2,512,128]{2,1,0:T(8,128)(2,1)S(1)} %pack.1.refs_0_.refs_2_), channel_id=1, source_target_pairs={{0,8},{2,14},{4,12},{6,2},{8,0},{10,6},{12,4},{14,10},{16,24},{18,... | collective-permute-start | bytes 786440 | tf_op jit(solution)/shard_map/ppermute | solution.py:31
  7.1 2.0 %collective-permute-start.2 = (s32[1,512]{1,0:T(1,128)}, s32[1,512]{1,0:T(1,128)S(1)}, u32[]{:S(2)}, u32[]{:S(2)}) collective-permute-start(s32[1,512]{1,0:T(1,128)} %bitcast.4), channel_id=1, source_target_pairs={{0,2},{2,0},{4,6},{6,4},{8,10},{10,8},{12,14},{14,12},{16,18},{18,... | collective-permute-start | bytes 6152 | tf_op jit(solution)/shard_map/ppermute | solution.py:36
  9.2 1.0 %collective-permute-done.2.refs_6_.refs_7_.refs_8_ = s32[1,512]{1,0:T(1,128)S(1)} collective-permute-done((s32[1,512]{1,0:T(1,128)}, s32[1,512]{1,0:T(1,128)S(1)}, u32[]{:S(2)}, u32[]{:S(2)}) %collective-permute-start.2) | collective-permute-done | bytes 2080 | tf_op jit(solution)/shard_map/ppermute | solution.py:36
  10.2 0.5 %collective-permute-start.5 = (bf16[2,512,128]{2,1,0:T(8,128)(2,1)S(1)}, bf16[2,512,128]{2,1,0:T(8,128)(2,1)S(1)}, u32[]{:S(2)}, u32[]{:S(2)}) collective-permute-start(bf16[2,512,128]{2,1,0:T(8,128)(2,1)S(1)} %pack.1.refs_0_.refs_2_), channel_id=1, source_target_pairs={{0,12},{2,10},{4,0},{6,14},{8,4},{10,2},{12,8},{14,6},{16,28},{18,... | collective-permute-start | bytes 786440 | tf_op jit(solution)/shard_map/ppermute | solution.py:31
  10.7 0.0 collective-permute-done.refs_2_.refs_3_.refs_4_
  10.7 0.0 collective-permute-done.1.refs_4_.refs_5_.refs_6_
  10.8 0.0 copy-start
  10.8 0.9 %copy-done = bf16[512,256]{1,0:T(8,128)(2,1)S(1)} copy-done((bf16[512,256]{1,0:T(8,128)(2,1)S(1)}, bf16[512,256]{1,0:T(8,128)(2,1)}, u32[]{:S(2)}) %copy-start) | copy-done | bytes 262168
  11.7 0.0 copy-start.2
  11.7 0.9 %copy-done.2 = bf16[512,256]{1,0:T(8,128)(2,1)S(1)} copy-done((bf16[512,256]{1,0:T(8,128)(2,1)S(1)}, bf16[512,256]{1,0:T(8,128)(2,1)}, u32[]{:S(2)}) %copy-start.2) | copy-done | bytes 262168
  12.7 0.0 copy-start.6
  12.7 0.7 %copy-done.6 = s32[512]{0:T(512)S(1)} copy-done((s32[512]{0:T(512)S(1)}, s32[512]{0:T(512)}, u32[]{:S(2)}) %copy-start.6) | copy-done | bytes 2072
  13.3 1.1 %stats.4.refs_0_ = f32[12,512]{1,0:T(8,128)S(1)} custom-call(s32[1]{0:T(128)} %bitcast.pos_ref, bf16[2,512,128]{2,1,0:T(8,128)(2,1)S(1)} %pack.1.refs_0_.refs_2_, bf16[512,256]{1,0:T(8,128)(2,1)S(1)} %copy-done, bf16[512,256]{1,0:T(8,128)(2,1)S(1)} %collective-permute-done.refs_2_.refs_3_.refs_4_, bf16[512,256]{1,0:T(8,128)(2,1)S(1)} %copy-done.2, ...), custom_call_target="tpu_custom_call" | custom-call | flops 1342177280 | bytes 1048576 | tf_op jit(solution)/shard_map/stats/pallas_call | solution.py:223
  14.5 0.0 collective-permute-done.3.refs_1_.refs_2_
  14.5 0.0 copy-done.1
  14.5 0.0 copy-done.3
  14.5 0.0 copy-done.7
  14.5 0.0 collective-permute-done.4.refs_1_.refs_2_
  14.6 5.5 %collective-permute-done.5.refs_1_.refs_2_ = bf16[2,512,128]{2,1,0:T(8,128)(2,1)S(1)} collective-permute-done((bf16[2,512,128]{2,1,0:T(8,128)(2,1)S(1)}, bf16[2,512,128]{2,1,0:T(8,128)(2,1)S(1)}, u32[]{:S(2)}, u32[]{:S(2)}) %collective-permute-start.5) | collective-permute-done | bytes 262176 | tf_op jit(solution)/shard_map/ppermute | solution.py:31
  20.1 1.1 %collective-permute-start.6 = (f32[12,512]{1,0:T(8,128)S(1)}, f32[12,512]{1,0:T(8,128)S(1)}, u32[]{:S(2)}, u32[]{:S(2)}) collective-permute-start(f32[12,512]{1,0:T(8,128)S(1)} %get-tuple-element.27.refs_0_), channel_id=1, source_target_pairs={{0,2},{2,0},{4,6},{6,4},{8,10},{10,8},{12,14},{14,12},{16,18},{18,... | collective-permute-start | bytes 73736 | tf_op jit(solution)/shard_map/ppermute | solution.py:36
  21.2 0.9 %collective-permute-done.6.refs_1_ = f32[12,512]{1,0:T(8,128)S(1)} collective-permute-done((f32[12,512]{1,0:T(8,128)S(1)}, f32[12,512]{1,0:T(8,128)S(1)}, u32[]{:S(2)}, u32[]{:S(2)}) %collective-permute-start.6) | collective-permute-done | bytes 24608 | tf_op jit(solution)/shard_map/ppermute | solution.py:36
  22.1 0.1 grads.4
  22.2 0.5 %collective-permute-start.8 = (bf16[2,512,128]{2,1,0:T(8,128)(2,1)S(1)}, bf16[2,512,128]{2,1,0:T(8,128)(2,1)S(1)}, u32[]{:S(2)}, u32[]{:S(2)}) collective-permute-start(bf16[2,512,128]{2,1,0:T(8,128)(2,1)S(1)} %get-tuple-element.41), channel_id=1, source_target_pairs={{0,8},{2,6},{4,12},{6,10},{8,0},{10,14},{12,4},{14,2},{16,24},{18,... | collective-permute-start | bytes 786440 | tf_op jit(solution)/shard_map/ppermute | solution.py:31
  22.7 0.3 grads.5
  23.1 0.1 grads.6
  23.2 8.9 %collective-permute-start.10 = (bf16[2,512,128]{2,1,0:T(8,128)(2,1)S(1)}, bf16[2,512,128]{2,1,0:T(8,128)(2,1)S(1)}, u32[]{:S(2)}, u32[]{:S(2)}) collective-permute-start(bf16[2,512,128]{2,1,0:T(8,128)(2,1)S(1)} %get-tuple-element.43), channel_id=1, source_target_pairs={{0,4},{2,10},{4,8},{6,14},{8,12},{10,2},{12,0},{14,6},{16,20},{18,... | collective-permute-start | bytes 786440 | tf_op jit(solution)/shard_map/ppermute | solution.py:31
  32.1 0.0 collective-permute-start.9
  32.1 1.7 %grads.7 = (f32[2,256,512]{2,1,0:T(8,128)S(1)}, f32[2,512,128]{2,1,0:T(8,128)S(1)}) custom-call(s32[1]{0:T(128)} %bitcast.pos_ref, f32[2,256,512]{2,1,0:T(8,128)S(1)} %get-tuple-element.37.refs_0_, f32[8,512]{1,0:T(8,128)S(1)} %get-tuple-element.31.refs_1_, bf16[2,512,128]{2,1,0:T(8,128)(2,1)S(1)} %pack.1.refs_0_.refs_2_, bf16[512,256]{1,0:T(8,128)(2,1)S(1)} %copy-done.1, ...), custom_call_target="tpu_custom_call" | custom-call | bytes 1024 | tf_op jit(solution)/shard_map/grads/pallas_call | solution.py:243
  33.9 1.1 %collective-permute-start.7 = (f32[256,512]{1,0:T(8,128)S(1)}, f32[256,512]{1,0:T(8,128)S(1)}, u32[]{:S(2)}, u32[]{:S(2)}) collective-permute-start(f32[256,512]{1,0:T(8,128)S(1)} %slice_bitcast_fusion), channel_id=1, source_target_pairs={{0,2},{2,0},{4,6},{6,4},{8,10},{10,8},{12,14},{14,12},{16,18},{18,... | collective-permute-start | bytes 1572872 | tf_op jit(solution)/shard_map/ppermute | solution.py:36
  35.0 0.6 %collective-permute-done.8.part = bf16[2,512,128]{2,1,0:T(8,128)(2,1)S(1)} collective-permute-done((bf16[2,512,128]{2,1,0:T(8,128)(2,1)S(1)}, bf16[2,512,128]{2,1,0:T(8,128)(2,1)S(1)}, u32[]{:S(2)}, u32[]{:S(2)}) %collective-permute-start.8) | collective-permute-done | bytes 262176 | tf_op jit(solution)/shard_map/ppermute | solution.py:31
  35.7 5.2 %collective-permute-done.9.part = bf16[2,512,128]{2,1,0:T(8,128)(2,1)S(1)} collective-permute-done((bf16[2,512,128]{2,1,0:T(8,128)(2,1)S(1)}, bf16[2,512,128]{2,1,0:T(8,128)(2,1)S(1)}, u32[]{:S(2)}, u32[]{:S(2)}) %collective-permute-start.9) | collective-permute-done | bytes 262176 | tf_op jit(solution)/shard_map/ppermute | solution.py:31
  40.9 0.1 shard_map.78.total
  41.0 0.0 collective-permute-done.10.part
  41.0 3.1 %collective-permute-start.11 = (bf16[2,512,128]{2,1,0:T(8,128)(2,1)S(1)}, bf16[2,512,128]{2,1,0:T(8,128)(2,1)S(1)}, u32[]{:S(2)}, u32[]{:S(2)}) collective-permute-start(bf16[2,512,128]{2,1,0:T(8,128)(2,1)S(1)} %shard_map.79.mine), channel_id=1, source_target_pairs={{0,1},{1,0},{2,3},{3,2},{4,5},{5,4},{6,7},{7,6},{8,9},{9,8},{10,11... | collective-permute-start | bytes 786440 | tf_op jit(solution)/shard_map/ppermute | solution.py:40
  44.1 0.0 collective-permute-done.7.other
  44.1 0.8 %shard_map.76 = (bf16[512,256]{1,0:T(8,128)(2,1)}, f32[8,128]{1,0:T(8,128)S(1)}) custom-call(f32[2,256,512]{2,1,0:T(8,128)S(1)} %get-tuple-element.38.mine, f32[256,512]{1,0:T(8,128)S(1)} %collective-permute-done.7.other), custom_call_target="tpu_custom_call" | custom-call | bytes 1024 | tf_op jit(solution)/shard_map/pallas_call | solution.py:196
  45.0 6.0 %collective-permute-done.11.other = bf16[2,512,128]{2,1,0:T(8,128)(2,1)S(1)} collective-permute-done((bf16[2,512,128]{2,1,0:T(8,128)(2,1)S(1)}, bf16[2,512,128]{2,1,0:T(8,128)(2,1)S(1)}, u32[]{:S(2)}, u32[]{:S(2)}) %collective-permute-start.11) | collective-permute-done | bytes 262176 | tf_op jit(solution)/shard_map/ppermute | solution.py:40
  50.9 0.7 %shard_map.80 = (bf16[512,128]{1,0:T(8,128)(2,1)}, bf16[512,128]{1,0:T(8,128)(2,1)}) custom-call(bf16[2,512,128]{2,1,0:T(8,128)(2,1)S(1)} %shard_map.79.mine, bf16[2,512,128]{2,1,0:T(8,128)(2,1)S(1)} %collective-permute-done.11.other, f32[8,128]{1,0:T(8,128)S(1)} %get-tuple-element.44._), custom_call_target="tpu_custom_call" | custom-call | bytes 1024 | tf_op jit(solution)/shard_map/pallas_call | solution.py:196
  (6 shorter events, 0.2 us)
Async XLA Ops:
  0.6 13.9 %copy-start.1 = (bf16[512,256]{1,0:T(8,128)(2,1)S(1)}, bf16[512,256]{1,0:T(8,128)(2,1)}, u32[]{:S(2)}) copy-start(bf16[512,256]{1,0:T(8,128)(2,1)} %refs_3_.9) | copy-start | bytes 786436
  0.6 13.9 %copy-start.3 = (bf16[512,256]{1,0:T(8,128)(2,1)S(1)}, bf16[512,256]{1,0:T(8,128)(2,1)}, u32[]{:S(2)}) copy-start(bf16[512,256]{1,0:T(8,128)(2,1)} %refs_5_.7) | copy-start | bytes 786436
  0.7 10.1 %collective-permute-start = (bf16[512,256]{1,0:T(8,128)(2,1)}, bf16[512,256]{1,0:T(8,128)(2,1)S(1)}, u32[]{:S(2)}, u32[]{:S(2)}) collective-permute-start(bf16[512,256]{1,0:T(8,128)(2,1)} %refs_3_.9), channel_id=1, source_target_pairs={{0,2},{2,0},{4,6},{6,4},{8,10},{10,8},{12,14},{14,12},{16,18},{18,... | collective-permute-start | bytes 786440 | tf_op jit(solution)/shard_map/ppermute | solution.py:36
  2.2 8.6 %collective-permute-start.1 = (bf16[512,256]{1,0:T(8,128)(2,1)}, bf16[512,256]{1,0:T(8,128)(2,1)S(1)}, u32[]{:S(2)}, u32[]{:S(2)}) collective-permute-start(bf16[512,256]{1,0:T(8,128)(2,1)} %refs_5_.7), channel_id=1, source_target_pairs={{0,2},{2,0},{4,6},{6,4},{8,10},{10,8},{12,14},{14,12},{16,18},{18,... | collective-permute-start | bytes 786440 | tf_op jit(solution)/shard_map/ppermute | solution.py:36
  2.3 0.9 %copy-start.4 = (bf16[512,128]{1,0:T(8,128)(2,1)S(1)}, bf16[512,128]{1,0:T(8,128)(2,1)}, u32[]{:S(2)}) copy-start(bf16[512,128]{1,0:T(8,128)(2,1)} %keys.1) | copy-start | bytes 393220
  3.2 0.9 %copy-start.5 = (bf16[512,128]{1,0:T(8,128)(2,1)S(1)}, bf16[512,128]{1,0:T(8,128)(2,1)}, u32[]{:S(2)}) copy-start(bf16[512,128]{1,0:T(8,128)(2,1)} %values.1) | copy-start | bytes 393220
  4.1 10.4 %copy-start.7 = (s32[512]{0:T(512)S(1)}, s32[512]{0:T(512)}, u32[]{:S(2)}) copy-start(s32[512]{0:T(512)} %param.9) | copy-start | bytes 6148
  4.4 10.1 %collective-permute-start.3 = (bf16[2,512,128]{2,1,0:T(8,128)(2,1)S(1)}, bf16[2,512,128]{2,1,0:T(8,128)(2,1)S(1)}, u32[]{:S(2)}, u32[]{:S(2)}) collective-permute-start(bf16[2,512,128]{2,1,0:T(8,128)(2,1)S(1)} %pack.1.refs_0_.refs_2_), channel_id=1, source_target_pairs={{0,4},{2,6},{4,8},{6,10},{8,12},{10,14},{12,0},{14,2},{16,20},{18,... | collective-permute-start | bytes 786440 | tf_op jit(solution)/shard_map/ppermute | solution.py:31
  5.8 8.8 %collective-permute-start.4 = (bf16[2,512,128]{2,1,0:T(8,128)(2,1)S(1)}, bf16[2,512,128]{2,1,0:T(8,128)(2,1)S(1)}, u32[]{:S(2)}, u32[]{:S(2)}) collective-permute-start(bf16[2,512,128]{2,1,0:T(8,128)(2,1)S(1)} %pack.1.refs_0_.refs_2_), channel_id=1, source_target_pairs={{0,8},{2,14},{4,12},{6,2},{8,0},{10,6},{12,4},{14,10},{16,24},{18,... | collective-permute-start | bytes 786440 | tf_op jit(solution)/shard_map/ppermute | solution.py:31
  7.1 3.1 %collective-permute-start.2 = (s32[1,512]{1,0:T(1,128)}, s32[1,512]{1,0:T(1,128)S(1)}, u32[]{:S(2)}, u32[]{:S(2)}) collective-permute-start(s32[1,512]{1,0:T(1,128)} %bitcast.4), channel_id=1, source_target_pairs={{0,2},{2,0},{4,6},{6,4},{8,10},{10,8},{12,14},{14,12},{16,18},{18,... | collective-permute-start | bytes 6152 | tf_op jit(solution)/shard_map/ppermute | solution.py:36
  10.2 9.9 %collective-permute-start.5 = (bf16[2,512,128]{2,1,0:T(8,128)(2,1)S(1)}, bf16[2,512,128]{2,1,0:T(8,128)(2,1)S(1)}, u32[]{:S(2)}, u32[]{:S(2)}) collective-permute-start(bf16[2,512,128]{2,1,0:T(8,128)(2,1)S(1)} %pack.1.refs_0_.refs_2_), channel_id=1, source_target_pairs={{0,12},{2,10},{4,0},{6,14},{8,4},{10,2},{12,8},{14,6},{16,28},{18,... | collective-permute-start | bytes 786440 | tf_op jit(solution)/shard_map/ppermute | solution.py:31
  10.8 1.0 %copy-start = (bf16[512,256]{1,0:T(8,128)(2,1)S(1)}, bf16[512,256]{1,0:T(8,128)(2,1)}, u32[]{:S(2)}) copy-start(bf16[512,256]{1,0:T(8,128)(2,1)} %refs_3_.9) | copy-start | bytes 786436
  11.7 0.9 %copy-start.2 = (bf16[512,256]{1,0:T(8,128)(2,1)S(1)}, bf16[512,256]{1,0:T(8,128)(2,1)}, u32[]{:S(2)}) copy-start(bf16[512,256]{1,0:T(8,128)(2,1)} %refs_5_.7) | copy-start | bytes 786436
  12.7 0.7 %copy-start.6 = (s32[512]{0:T(512)S(1)}, s32[512]{0:T(512)}, u32[]{:S(2)}) copy-start(s32[512]{0:T(512)} %param.9) | copy-start | bytes 6148
  20.1 1.9 %collective-permute-start.6 = (f32[12,512]{1,0:T(8,128)S(1)}, f32[12,512]{1,0:T(8,128)S(1)}, u32[]{:S(2)}, u32[]{:S(2)}) collective-permute-start(f32[12,512]{1,0:T(8,128)S(1)} %get-tuple-element.27.refs_0_), channel_id=1, source_target_pairs={{0,2},{2,0},{4,6},{6,4},{8,10},{10,8},{12,14},{14,12},{16,18},{18,... | collective-permute-start | bytes 73736 | tf_op jit(solution)/shard_map/ppermute | solution.py:36
  22.2 13.4 %collective-permute-start.8 = (bf16[2,512,128]{2,1,0:T(8,128)(2,1)S(1)}, bf16[2,512,128]{2,1,0:T(8,128)(2,1)S(1)}, u32[]{:S(2)}, u32[]{:S(2)}) collective-permute-start(bf16[2,512,128]{2,1,0:T(8,128)(2,1)S(1)} %get-tuple-element.41), channel_id=1, source_target_pairs={{0,8},{2,6},{4,12},{6,10},{8,0},{10,14},{12,4},{14,2},{16,24},{18,... | collective-permute-start | bytes 786440 | tf_op jit(solution)/shard_map/ppermute | solution.py:31
  23.2 17.8 %collective-permute-start.10 = (bf16[2,512,128]{2,1,0:T(8,128)(2,1)S(1)}, bf16[2,512,128]{2,1,0:T(8,128)(2,1)S(1)}, u32[]{:S(2)}, u32[]{:S(2)}) collective-permute-start(bf16[2,512,128]{2,1,0:T(8,128)(2,1)S(1)} %get-tuple-element.43), channel_id=1, source_target_pairs={{0,4},{2,10},{4,8},{6,14},{8,12},{10,2},{12,0},{14,6},{16,20},{18,... | collective-permute-start | bytes 786440 | tf_op jit(solution)/shard_map/ppermute | solution.py:31
  32.1 8.8 %collective-permute-start.9 = (bf16[2,512,128]{2,1,0:T(8,128)(2,1)S(1)}, bf16[2,512,128]{2,1,0:T(8,128)(2,1)S(1)}, u32[]{:S(2)}, u32[]{:S(2)}) collective-permute-start(bf16[2,512,128]{2,1,0:T(8,128)(2,1)S(1)} %get-tuple-element.42), channel_id=1, source_target_pairs={{0,12},{2,14},{4,0},{6,2},{8,4},{10,6},{12,8},{14,10},{16,28},{18,... | collective-permute-start | bytes 786440 | tf_op jit(solution)/shard_map/ppermute | solution.py:31
  33.9 10.2 %collective-permute-start.7 = (f32[256,512]{1,0:T(8,128)S(1)}, f32[256,512]{1,0:T(8,128)S(1)}, u32[]{:S(2)}, u32[]{:S(2)}) collective-permute-start(f32[256,512]{1,0:T(8,128)S(1)} %slice_bitcast_fusion), channel_id=1, source_target_pairs={{0,2},{2,0},{4,6},{6,4},{8,10},{10,8},{12,14},{14,12},{16,18},{18,... | collective-permute-start | bytes 1572872 | tf_op jit(solution)/shard_map/ppermute | solution.py:36
  41.0 9.9 %collective-permute-start.11 = (bf16[2,512,128]{2,1,0:T(8,128)(2,1)S(1)}, bf16[2,512,128]{2,1,0:T(8,128)(2,1)S(1)}, u32[]{:S(2)}, u32[]{:S(2)}) collective-permute-start(bf16[2,512,128]{2,1,0:T(8,128)(2,1)S(1)} %shard_map.79.mine), channel_id=1, source_target_pairs={{0,1},{1,0},{2,3},{3,2},{4,5},{5,4},{6,7},{7,6},{8,9},{9,8},{10,11... | collective-permute-start | bytes 786440 | tf_op jit(solution)/shard_map/ppermute | solution.py:40

commit v4 on v3

v4 whole, which is shorter than its diff:
```python
import functools
import math

import jax
import jax.numpy as jnp
from jax import lax
from jax.experimental import pallas as pl
from jax.experimental.pallas import tpu as pltpu
from jax.sharding import PartitionSpec as P

HDIM = 128
GROUP = 8
SCALE = 1.0 / math.sqrt(HDIM)
EXP_SCALE = SCALE * math.log2(math.e)
MASKED = -1e30
FLOOR = -1e29
KERNEL_VMEM = 16 * 2**20

NT = (((1,), (1,)), ((), ()))
NN = (((1,), (0,)), ((), ()))
TN = (((0,), (0,)), ((), ()))


def dot(a, b, dims):
    return lax.dot_general(a, b, dims, preferred_element_type=jnp.float32)


def chip_shift(array, even, odd):
    n = lax.axis_size("cp")
    pairs = [(i, i - i % GROUP + (i % GROUP + 2 * (odd if i % 2 else even)) % GROUP) for i in range(n)]
    return lax.ppermute(array, "cp", pairs)


def core_swap(array):
    n = lax.axis_size("cp")
    return lax.ppermute(array, "cp", [(i, i ^ 1) for i in range(n)])


def hd_swap(array):
    return lax.ppermute(array, "hd", [(0, 1), (1, 0)])


def masked_scores(k, q, starts, row_base, key_base, diagonal):
    s = dot(k, q, NT)
    key_pos = key_base + lax.broadcasted_iota(jnp.int32, s.shape, 0)
    allowed = key_pos >= starts
    if diagonal:
        row_pos = row_base + lax.broadcasted_iota(jnp.int32, s.shape, 1)
        allowed = allowed & (key_pos <= row_pos)
    return jnp.where(allowed, s, MASKED)


def slot_distance(slot, cp):
    return slot if slot < 2 else slot + lax.rem(cp, 2) * (5 - 2 * slot)


def stats_kernel(slot, pos_ref, *refs):
    if slot:
        stats_in, *refs = refs
    if slot > 1:
        refs = refs[2:]
    kv, q_own, q_sib, g_own, g_sib, st_own, st_sib, stats, *kept = refs
    cp = pos_ref[0]
    in_group = lax.rem(cp, GROUP)
    size = q_own.shape[0]
    if slot:
        stats[...] = stats_in[...]
    else:
        for at in range(0, 12, 3):
            stats[at : at + 1, :] = jnp.full((1, size), FLOOR)
            stats[at + 1 : at + 3, :] = jnp.zeros((2, size))
    chips = slot_distance(slot, cp)
    key_block = cp - 2 * chips
    for group, (q, g, st) in enumerate(((q_own, g_own, st_own), (q_sib, g_sib, st_sib))):
        row_block = cp if group == 0 else cp + 1 - 2 * lax.rem(cp, 2)

        def work(q=q, g=g, st=st, group=group, row_block=row_block):
            for head in range(2):
                cols = pl.ds(head * HDIM, HDIM)
                s = masked_scores(kv[0], q[:, cols], st[...], row_block * size, key_block * size, slot == 0 and group == 0)
                dp = dot(kv[1], g[:, cols], NT)
                if slot:
                    kept[0][chips - 1, 2 * group + head] = s
                    kept[1][chips - 1, 2 * group + head] = dp
                at = 3 * (2 * group + head)
                m = stats[at : at + 1, :]
                new = jnp.maximum(m, jnp.max(s, axis=0, keepdims=True))
                p = jnp.exp2((s - new) * EXP_SCALE)
                f = jnp.exp2((m - new) * EXP_SCALE)
                stats[at : at + 1, :] = new
                stats[at + 1 : at + 2, :] = stats[at + 1 : at + 2, :] * f + jnp.sum(p, axis=0, keepdims=True)
                stats[at + 2 : at + 3, :] = stats[at + 2 : at + 3, :] * f + jnp.sum(p * dp, axis=0, keepdims=True)

        if slot == 0 and group == 0:
            work()
        elif slot == 0:
            pl.when(lax.rem(cp, 2) == 0)(work)
        else:
            pl.when(in_group >= 2 * chips)(work)


def merged(stats, other, at, other_at):
    m, m2 = stats[at : at + 1, :], other[other_at : other_at + 1, :]
    top = jnp.maximum(m, m2)
    f, f2 = jnp.exp2((m - top) * EXP_SCALE), jnp.exp2((m2 - top) * EXP_SCALE)
    total = stats[at + 1 : at + 2, :] * f + other[other_at + 1 : other_at + 2, :] * f2
    weighted = stats[at + 2 : at + 3, :] * f + other[other_at + 2 : other_at + 3, :] * f2
    return top * EXP_SCALE + jnp.log2(total), weighted / total


def stage_distance(stage, cp):
    odd = lax.rem(cp, 2)
    return (2, 3 - 2 * odd, 1 + 2 * odd, 0)[stage]


def grads_kernel(stage, pos_ref, *refs):
    before, (even, odd, q_own, q_sib, g_own, g_sib, kept0, kept1, dq, dkv, *refs) = refs[:2], refs[2:]
    acc = refs[-1]
    if stage == 0:
        (stats, other), fin = before, refs[0]
        for s in range(4):
            log_sum, delta = merged(stats, other, 3 * s, 3 * (s ^ 2))
            fin[2 * s : 2 * s + 1, :] = log_sum
            fin[2 * s + 1 : 2 * s + 2, :] = delta
        dq[...] = jnp.zeros_like(dq)
    else:
        dq_in, fin = before
        dq[...] = dq_in[...]
    cp = pos_ref[0]
    in_group = lax.rem(cp, GROUP)
    size = q_own.shape[0]
    acc[...] = jnp.zeros_like(acc)
    chips = stage_distance(stage, cp)
    k = even[0] if stage == 3 else jnp.where(lax.rem(cp, 2) == 0, even[0], odd[0])
    k_t = k.T
    for group, (q, g) in enumerate(((q_own, g_own), (q_sib, g_sib))):
        row_block = cp if group == 0 else cp + 1 - 2 * lax.rem(cp, 2)

        def work(q=q, g=g, group=group, row_block=row_block):
            for head in range(2):
                cols = pl.ds(head * HDIM, HDIM)
                if stage < 3:
                    s = kept0[chips - 1, 2 * group + head]
                    dp = kept1[chips - 1, 2 * group + head]
                else:
                    starts = (kept0, kept1)[group][...]
                    s = masked_scores(k, q[:, cols], starts, row_block * size, cp * size, group == 0)
                    dp = dot(even[1], g[:, cols], NT)
                at = 2 * (2 * group + head)
                p = jnp.exp2(s * EXP_SCALE - fin[at : at + 1, :])
                ds = (p * (dp - fin[at + 1 : at + 2, :])).astype(jnp.bfloat16)
                acc[0] += dot(ds, q[:, cols], NN)
                acc[1] += dot(p.astype(jnp.bfloat16), g[:, cols], NN)
                dq[group, cols, :] += dot(k_t, ds, NN)

        if stage == 3 and group == 0:
            work()
        elif stage == 3:
            pl.when(lax.rem(cp, 2) == 0)(work)
        else:
            pl.when(in_group >= 2 * chips)(work)
    dkv[...] = acc[...].astype(dkv.dtype)


def query_kernel(mine, other, out, done):
    done[...] = jnp.zeros_like(done)
    out[...] = ((mine[0] + other[...]) * SCALE).T.astype(out.dtype)


def add_kernel(total, part, out):
    out[...] = (total[...] + part[...].astype(jnp.float32)).astype(out.dtype)


def last_kernel(mine, other, _, grad_keys, grad_values):
    total = mine[...].astype(jnp.float32) + other[...].astype(jnp.float32)
    grad_keys[...] = (total[0] * SCALE).astype(grad_keys.dtype)
    grad_values[...] = total[1].astype(grad_values.dtype)


VM = pl.BlockSpec(memory_space=pltpu.VMEM)
SM = pl.BlockSpec(memory_space=pltpu.SMEM)


BLOCK_COST = pl.CostEstimate(flops=10 * 512 * 512 * 128 // 10, bytes_accessed=2**10, transcendentals=0)
LONG_COST = pl.CostEstimate(flops=40 * 10 * 512 * 512 * 128, bytes_accessed=2**20, transcendentals=0)
NO_COST = pl.CostEstimate(flops=0, bytes_accessed=2**10, transcendentals=0)


def simple(kernel, out, *args, cost=NO_COST):
    return pl.pallas_call(
        kernel,
        out_shape=out,
        in_specs=[VM] * len(args),
        out_specs=jax.tree.map(lambda _: VM, out),
        compiler_params=pltpu.CompilerParams(vmem_limit_bytes=8 * 2**20),
        cost_estimate=cost,
    )(*args)


def call_stats(slot, cp, before, kv, rows):
    size = kv.shape[1]
    out = [jax.ShapeDtypeStruct((12, size), jnp.float32)]
    if slot:
        out += [jax.ShapeDtypeStruct((3, 4, size, size), jnp.float32)] * 2
    kept = len(before[1:])
    return pl.pallas_call(
        functools.partial(stats_kernel, slot),
        out_shape=out,
        in_specs=[SM] + [VM] * len(before[:1]) + [pl.BlockSpec(memory_space=pl.ANY)] * kept + [VM] * (1 + len(rows)),
        out_specs=[VM] * len(out),
        input_output_aliases={2: 1, 3: 2} if kept else {},
        compiler_params=pltpu.CompilerParams(vmem_limit_bytes=KERNEL_VMEM),
        cost_estimate=BLOCK_COST,
        name="stats",
    )(cp, *before, kv, *rows)


def call_grads(stage, cp, before, even, odd, rows, kept):
    size = even.shape[1]
    out = [
        jax.ShapeDtypeStruct((2, 2 * HDIM, size), jnp.float32),
        jax.ShapeDtypeStruct((2, size, HDIM), jnp.float32 if stage == 3 else jnp.bfloat16),
    ]
    if stage == 0:
        out.append(jax.ShapeDtypeStruct((8, size), jnp.float32))
    return pl.pallas_call(
        functools.partial(grads_kernel, stage),
        out_shape=out,
        in_specs=[SM] + [VM] * 10,
        out_specs=[VM] * len(out),
        scratch_shapes=[pltpu.VMEM((2, size, HDIM), jnp.float32)],
        compiler_params=pltpu.CompilerParams(vmem_limit_bytes=KERNEL_VMEM),
        cost_estimate=NO_COST if stage == 3 else BLOCK_COST,
        name="grads",
    )(cp, *before, even, odd, *rows[:4], *kept)


def body(query, keys, values, grad_out, doc_start):
    size = query.shape[0]
    position = lax.axis_index("cp").astype(jnp.int32)
    cp = position.reshape(1)
    kv = jnp.where(lax.broadcasted_iota(jnp.int32, (2, *keys.shape), 0) == 0, keys[None], values[None])
    slot1 = chip_shift(kv, 1, 1)
    slot2 = chip_shift(kv, 2, 3)
    slot3 = chip_shift(kv, 3, 2)
    starts = doc_start.reshape(1, size)
    rows = (query, core_swap(query), grad_out, core_swap(grad_out), starts, core_swap(starts))

    (stats,) = call_stats(0, cp, (), kv, rows)
    before = call_stats(1, cp, (stats,), slot1, rows)
    before = call_stats(2, cp, before, slot2, rows)
    stats, *kept = call_stats(3, cp, before, slot3, rows)

    dq, part, fin = call_grads(0, cp, (stats, core_swap(stats)), slot2, slot3, rows, kept)
    back_a = chip_shift(part, 2, 2)
    dq, part = call_grads(1, cp, (dq, fin), slot3, slot1, rows, kept)
    back_b = chip_shift(part, 1, 3)
    dq, part = call_grads(2, cp, (dq, fin), slot1, slot2, rows, kept)
    back_c = chip_shift(part, 3, 1)
    dq, own = call_grads(3, cp, (dq, fin), kv, kv, rows, rows[4:])

    dq_other = core_swap(dq[1])
    token = jax.ShapeDtypeStruct((8, HDIM), jnp.float32)
    grad_query, done = simple(query_kernel, [jax.ShapeDtypeStruct(query.shape, query.dtype), token], dq, dq_other)
    total = jax.ShapeDtypeStruct(own.shape, own.dtype)
    half = simple(add_kernel, total, own, back_a, cost=BLOCK_COST)
    half = simple(add_kernel, total, half, back_b, cost=LONG_COST)
    half = simple(add_kernel, jax.ShapeDtypeStruct(kv.shape, kv.dtype), half, back_c)
    other = hd_swap(half)
    near = jax.ShapeDtypeStruct(keys.shape, keys.dtype)
    grad_keys, grad_values = simple(last_kernel, [near] * 2, half, other, done)
    return grad_query, grad_keys, grad_values


def solution(mesh):
    in_specs = (P("cp", "hd"), P("cp", None), P("cp", None), P("cp", "hd"), P("cp"))
    out_specs = (P("cp", "hd"), P("cp", None), P("cp", None))
    return jax.shard_map(body, mesh=mesh, in_specs=in_specs, out_specs=out_specs, check_vma=False)
```

time: 51.9 us -> 49.1 us (0.946)
  the two profiles are of different devices: /device:TPU:1 before, /device:TPU:0 now
where the time goes in v4:
time: 49.1 us; the launch traced here: 48.2 us
  starting transfers between devices  19.2 us (39%)
  waiting for transfers between devices  14.3 us (29%)
  Pallas kernels  7.76 us (16%)
  local copies, waits for them, and re-layouts  5.2 us (11%)
  other arithmetic  1.06 us (2%)
  between operations  0.76 us (2%)
    ppermute x6, starting transfers between devices, chip_shift(): return lax.ppermute(array, 'cp', pairs)  15.1 us
    ppermute x6, waiting for transfers between devices, chip_shift(): return lax.ppermute(array, 'cp', pairs)  6.75 us
    unnamed x18, local copies, waits for them, and re-layouts  5.17 us
    ppermute x1, waiting for transfers between devices, hd_swap(): return lax.ppermute(array, 'hd', [(0, 1), (1, 0)])  4.99 us
    pallas_call x4, Pallas kernels, call_grads(): pl.pallas_call(functools.partial(grads_kernel, stage), out_shape=out, in_...  3.9 us
    ppermute x1, starting transfers between devices, hd_swap(): return lax.ppermute(array, 'hd', [(0, 1), (1, 0)])  3.35 us
    ppermute x5, waiting for transfers between devices, core_swap(): return lax.ppermute(array, 'cp', [(i, i ^ 1) for i in range(n)])  2.57 us
    pallas_call x4, Pallas kernels, call_stats(): pl.pallas_call(functools.partial(stats_kernel, slot), out_shape=out, in_s...  2.06 us
  transfers between devices with their start and end apart: 12, of which 6 were waited for; matrix products, arithmetic and copies ran while one was open for 2% of the time, Pallas kernels for 14%

profile of v4, /device:TPU:0, one launch (start us, length us, event | category | flops | bytes accessed | tf_op | source)
XLA Modules:
  0.0 48.2 jit_solution(4309228135231576813)
XLA Ops:
  0.6 0.1 collective-permute-start
  0.7 0.5 %collective-permute-start.1 = (bf16[512,256]{1,0:T(8,128)(2,1)}, bf16[512,256]{1,0:T(8,128)(2,1)S(1)}, u32[]{:S(2)}, u32[]{:S(2)}) collective-permute-start(bf16[512,256]{1,0:T(8,128)(2,1)} %refs_6_.11), channel_id=1, source_target_pairs={{0,2},{2,0},{4,6},{6,4},{8,10},{10,8},{12,14},{14,12},{16,18},{18,... | collective-permute-start | bytes 786440 | tf_op jit(solution)/shard_map/ppermute | solution.py:36
  1.2 1.1 %broadcast_select_fusion.refs_0_.refs_2_.refs_3_ = bf16[2,512,128]{2,1,0:T(8,128)(2,1)S(1)} fusion(pred[2]{0:T(512)(128)(4,1)S(1)} %iota_compare_fusion, bf16[512,128]{1,0:T(8,128)(2,1)} %param.7, bf16[512,128]{1,0:T(8,128)(2,1)} %param.6), kind=kLoop, calls=%fused_computation.1 | loop fusion | flops 131072 | bytes 524290 | tf_op jit(solution)/shard_map/jit(_where)/select_n | solution.py:242
  2.3 1.6 %collective-permute-start.3 = (bf16[2,512,128]{2,1,0:T(8,128)(2,1)S(1)}, bf16[2,512,128]{2,1,0:T(8,128)(2,1)S(1)}, u32[]{:S(2)}, u32[]{:S(2)}) collective-permute-start(bf16[2,512,128]{2,1,0:T(8,128)(2,1)S(1)} %broadcast_select_fusion.refs_0_.refs_2_.refs_3_), channel_id=1, source_target_pairs={{0,4},{2,6},{4,8},{6,10},{8,12},{10,14},{12,0},{14,2},{16,20},{18,... | collective-permute-start | bytes 786440 | tf_op jit(solution)/shard_map/ppermute | solution.py:31
  3.9 2.7 %collective-permute-start.4 = (bf16[2,512,128]{2,1,0:T(8,128)(2,1)S(1)}, bf16[2,512,128]{2,1,0:T(8,128)(2,1)S(1)}, u32[]{:S(2)}, u32[]{:S(2)}) collective-permute-start(bf16[2,512,128]{2,1,0:T(8,128)(2,1)S(1)} %broadcast_select_fusion.refs_0_.refs_2_.refs_3_), channel_id=1, source_target_pairs={{0,8},{2,14},{4,12},{6,2},{8,0},{10,6},{12,4},{14,10},{16,24},{18,... | collective-permute-start | bytes 786440 | tf_op jit(solution)/shard_map/ppermute | solution.py:31
  6.7 0.0 collective-permute-start.2
  6.7 1.4 %collective-permute-done.2.refs_6_.refs_7_.refs_9_ = s32[1,512]{1,0:T(1,128)S(1)} collective-permute-done((s32[1,512]{1,0:T(1,128)}, s32[1,512]{1,0:T(1,128)S(1)}, u32[]{:S(2)}, u32[]{:S(2)}) %collective-permute-start.2) | collective-permute-done | bytes 2080 | tf_op jit(solution)/shard_map/ppermute | solution.py:36
  8.0 1.4 %collective-permute-start.5 = (bf16[2,512,128]{2,1,0:T(8,128)(2,1)S(1)}, bf16[2,512,128]{2,1,0:T(8,128)(2,1)S(1)}, u32[]{:S(2)}, u32[]{:S(2)}) collective-permute-start(bf16[2,512,128]{2,1,0:T(8,128)(2,1)S(1)} %broadcast_select_fusion.refs_0_.refs_2_.refs_3_), channel_id=1, source_target_pairs={{0,12},{2,10},{4,0},{6,14},{8,4},{10,2},{12,8},{14,6},{16,28},{18,... | collective-permute-start | bytes 786440 | tf_op jit(solution)/shard_map/ppermute | solution.py:31
  9.5 0.0 collective-permute-done.refs_2_.refs_3_.refs_5_
  9.5 0.0 collective-permute-done.1.refs_4_.refs_5_.refs_7_
  9.5 0.0 copy-start
  9.5 0.9 %copy-done = bf16[512,256]{1,0:T(8,128)(2,1)S(1)} copy-done((bf16[512,256]{1,0:T(8,128)(2,1)S(1)}, bf16[512,256]{1,0:T(8,128)(2,1)}, u32[]{:S(2)}) %copy-start) | copy-done | bytes 262168
  10.4 0.0 copy-start.3
  10.4 0.9 %copy-done.3 = bf16[512,256]{1,0:T(8,128)(2,1)S(1)} copy-done((bf16[512,256]{1,0:T(8,128)(2,1)S(1)}, bf16[512,256]{1,0:T(8,128)(2,1)}, u32[]{:S(2)}) %copy-start.3) | copy-done | bytes 262168
  11.4 0.0 copy-start.6
  11.4 0.7 %copy-done.6 = s32[512]{0:T(512)S(1)} copy-done((s32[512]{0:T(512)S(1)}, s32[512]{0:T(512)}, u32[]{:S(2)}) %copy-start.6) | copy-done | bytes 2072
  12.1 2.0 %stats.4.refs_0_ = f32[12,512]{1,0:T(8,128)S(1)} custom-call(s32[1]{0:T(128)} %bitcast.pos_ref, bf16[2,512,128]{2,1,0:T(8,128)(2,1)S(1)} %broadcast_select_fusion.refs_0_.refs_2_.refs_3_, bf16[512,256]{1,0:T(8,128)(2,1)S(1)} %copy-done, bf16[512,256]{1,0:T(8,128)(2,1)S(1)} %collective-permute-done.refs_2_.refs_3_.refs_5_, bf16[512,256]{1,0:T(8,128)(2,1)S(1)} %copy-done.3, ...), custom_call_target="tpu_custom_call" | custom-call | flops 33554432 | bytes 1024 | tf_op jit(solution)/shard_map/stats/pallas_call | solution.py:206
  14.1 0.0 collective-permute-done.3.refs_1_.refs_3_.refs_2_
  14.1 0.0 copy-start.1
  14.1 0.9 %copy-done.1 = bf16[512,256]{1,0:T(8,128)(2,1)S(1)} copy-done((bf16[512,256]{1,0:T(8,128)(2,1)S(1)}, bf16[512,256]{1,0:T(8,128)(2,1)}, u32[]{:S(2)}) %copy-start.1) | copy-done | bytes 262168
  15.1 0.0 copy-start.4
  15.1 0.9 %copy-done.4 = bf16[512,256]{1,0:T(8,128)(2,1)S(1)} copy-done((bf16[512,256]{1,0:T(8,128)(2,1)S(1)}, bf16[512,256]{1,0:T(8,128)(2,1)}, u32[]{:S(2)}) %copy-start.4) | copy-done | bytes 262168
  16.0 0.0 copy-start.7
  16.0 0.7 %copy-done.7 = s32[512]{0:T(512)S(1)} copy-done((s32[512]{0:T(512)S(1)}, s32[512]{0:T(512)}, u32[]{:S(2)}) %copy-start.7) | copy-done | bytes 2072
  16.7 1.9 %collective-permute-done.4.refs_3_.refs_2_ = bf16[2,512,128]{2,1,0:T(8,128)(2,1)S(1)} collective-permute-done((bf16[2,512,128]{2,1,0:T(8,128)(2,1)S(1)}, bf16[2,512,128]{2,1,0:T(8,128)(2,1)S(1)}, u32[]{:S(2)}, u32[]{:S(2)}) %collective-permute-start.4) | collective-permute-done | bytes 262176 | tf_op jit(solution)/shard_map/ppermute | solution.py:31
  18.6 0.0 collective-permute-done.5.refs_3_.refs_2_
  18.6 0.1 collective-permute-start.6
  18.7 1.2 %collective-permute-done.6.refs_1_ = f32[12,512]{1,0:T(8,128)S(1)} collective-permute-done((f32[12,512]{1,0:T(8,128)S(1)}, f32[12,512]{1,0:T(8,128)S(1)}, u32[]{:S(2)}, u32[]{:S(2)}) %collective-permute-start.6) | collective-permute-done | bytes 24608 | tf_op jit(solution)/shard_map/ppermute | solution.py:36
  19.9 0.2 grads.4
  20.1 4.3 %collective-permute-start.8 = (bf16[2,512,128]{2,1,0:T(8,128)(2,1)S(1)}, bf16[2,512,128]{2,1,0:T(8,128)(2,1)S(1)}, u32[]{:S(2)}, u32[]{:S(2)}) collective-permute-start(bf16[2,512,128]{2,1,0:T(8,128)(2,1)S(1)} %get-tuple-element.41), channel_id=1, source_target_pairs={{0,8},{2,10},{4,12},{6,14},{8,0},{10,2},{12,4},{14,6},{16,24},{18,... | collective-permute-start | bytes 786440 | tf_op jit(solution)/shard_map/ppermute | solution.py:31
  24.3 0.3 grads.5
  24.7 2.0 %collective-permute-start.9 = (bf16[2,512,128]{2,1,0:T(8,128)(2,1)S(1)}, bf16[2,512,128]{2,1,0:T(8,128)(2,1)S(1)}, u32[]{:S(2)}, u32[]{:S(2)}) collective-permute-start(bf16[2,512,128]{2,1,0:T(8,128)(2,1)S(1)} %get-tuple-element.42), channel_id=1, source_target_pairs={{0,4},{2,14},{4,8},{6,2},{8,12},{10,6},{12,0},{14,10},{16,20},{18,... | collective-permute-start | bytes 786440 | tf_op jit(solution)/shard_map/ppermute | solution.py:31
  26.6 0.0 copy-start.2
  26.6 0.0 copy-start.5
  26.6 0.0 copy-start.8
  26.6 0.2 grads.6
  26.8 3.0 %collective-permute-start.10 = (bf16[2,512,128]{2,1,0:T(8,128)(2,1)S(1)}, bf16[2,512,128]{2,1,0:T(8,128)(2,1)S(1)}, u32[]{:S(2)}, u32[]{:S(2)}) collective-permute-start(bf16[2,512,128]{2,1,0:T(8,128)(2,1)S(1)} %get-tuple-element.43), channel_id=1, source_target_pairs={{0,12},{2,6},{4,0},{6,10},{8,4},{10,14},{12,8},{14,2},{16,28},{18,... | collective-permute-start | bytes 786440 | tf_op jit(solution)/shard_map/ppermute | solution.py:31
  29.8 0.0 copy-done.2
  29.8 0.0 copy-done.5
  29.8 0.0 copy-done.8
  29.8 3.2 %grads.7 = (f32[2,256,512]{2,1,0:T(8,128)S(1)}, f32[2,512,128]{2,1,0:T(8,128)S(1)}) custom-call(s32[1]{0:T(128)} %bitcast.pos_ref, f32[2,256,512]{2,1,0:T(8,128)S(1)} %get-tuple-element.37.refs_0_, f32[8,512]{1,0:T(8,128)S(1)} %get-tuple-element.35.refs_1_, bf16[2,512,128]{2,1,0:T(8,128)(2,1)S(1)} %broadcast_select_fusion.refs_0_.refs_2_.refs_3_, ...), custom_call_target="tpu_custom_call" | custom-call | bytes 1024 | tf_op jit(solution)/shard_map/grads/pallas_call | solution.py:226
  33.1 0.1 collective-permute-start.7
  33.2 0.0 collective-permute-done.8.part
  33.2 0.1 shard_map.77.total
  33.3 3.0 %collective-permute-done.9.part = bf16[2,512,128]{2,1,0:T(8,128)(2,1)S(1)} collective-permute-done((bf16[2,512,128]{2,1,0:T(8,128)(2,1)S(1)}, bf16[2,512,128]{2,1,0:T(8,128)(2,1)S(1)}, u32[]{:S(2)}, u32[]{:S(2)}) %collective-permute-start.9) | collective-permute-done | bytes 262176 | tf_op jit(solution)/shard_map/ppermute | solution.py:31
  36.3 1.9 %collective-permute-done.10.part = bf16[2,512,128]{2,1,0:T(8,128)(2,1)S(1)} collective-permute-done((bf16[2,512,128]{2,1,0:T(8,128)(2,1)S(1)}, bf16[2,512,128]{2,1,0:T(8,128)(2,1)S(1)}, u32[]{:S(2)}, u32[]{:S(2)}) %collective-permute-start.10) | collective-permute-done | bytes 262176 | tf_op jit(solution)/shard_map/ppermute | solution.py:31
  38.2 0.1 shard_map.79.mine
  38.3 3.3 %collective-permute-start.11 = (bf16[2,512,128]{2,1,0:T(8,128)(2,1)S(1)}, bf16[2,512,128]{2,1,0:T(8,128)(2,1)S(1)}, u32[]{:S(2)}, u32[]{:S(2)}) collective-permute-start(bf16[2,512,128]{2,1,0:T(8,128)(2,1)S(1)} %shard_map.79.mine), channel_id=1, source_target_pairs={{0,1},{1,0},{2,3},{3,2},{4,5},{5,4},{6,7},{7,6},{8,9},{9,8},{10,11... | collective-permute-start | bytes 786440 | tf_op jit(solution)/shard_map/ppermute | solution.py:40
  41.6 0.0 collective-permute-done.7.other
  41.6 0.9 %shard_map.76 = (bf16[512,256]{1,0:T(8,128)(2,1)}, f32[8,128]{1,0:T(8,128)S(1)}) custom-call(f32[2,256,512]{2,1,0:T(8,128)S(1)} %get-tuple-element.38.mine, f32[256,512]{1,0:T(8,128)S(1)} %collective-permute-done.7.other), custom_call_target="tpu_custom_call" | custom-call | bytes 1024 | tf_op jit(solution)/shard_map/pallas_call | solution.py:190
  42.5 5.0 %collective-permute-done.11.other = bf16[2,512,128]{2,1,0:T(8,128)(2,1)S(1)} collective-permute-done((bf16[2,512,128]{2,1,0:T(8,128)(2,1)S(1)}, bf16[2,512,128]{2,1,0:T(8,128)(2,1)S(1)}, u32[]{:S(2)}, u32[]{:S(2)}) %collective-permute-start.11) | collective-permute-done | bytes 262176 | tf_op jit(solution)/shard_map/ppermute | solution.py:40
  47.5 0.7 %shard_map.80 = (bf16[512,128]{1,0:T(8,128)(2,1)}, bf16[512,128]{1,0:T(8,128)(2,1)}) custom-call(bf16[2,512,128]{2,1,0:T(8,128)(2,1)S(1)} %shard_map.79.mine, bf16[2,512,128]{2,1,0:T(8,128)(2,1)S(1)} %collective-permute-done.11.other, f32[8,128]{1,0:T(8,128)S(1)} %get-tuple-element.44._), custom_call_target="tpu_custom_call" | custom-call | bytes 1024 | tf_op jit(solution)/shard_map/pallas_call | solution.py:190
  (6 shorter events, 0.1 us)
Async XLA Ops:
  0.6 8.8 %collective-permute-start = (bf16[512,256]{1,0:T(8,128)(2,1)}, bf16[512,256]{1,0:T(8,128)(2,1)S(1)}, u32[]{:S(2)}, u32[]{:S(2)}) collective-permute-start(bf16[512,256]{1,0:T(8,128)(2,1)} %refs_4_.13), channel_id=1, source_target_pairs={{0,2},{2,0},{4,6},{6,4},{8,10},{10,8},{12,14},{14,12},{16,18},{18,... | collective-permute-start | bytes 786440 | tf_op jit(solution)/shard_map/ppermute | solution.py:36
  0.7 8.7 %collective-permute-start.1 = (bf16[512,256]{1,0:T(8,128)(2,1)}, bf16[512,256]{1,0:T(8,128)(2,1)S(1)}, u32[]{:S(2)}, u32[]{:S(2)}) collective-permute-start(bf16[512,256]{1,0:T(8,128)(2,1)} %refs_6_.11), channel_id=1, source_target_pairs={{0,2},{2,0},{4,6},{6,4},{8,10},{10,8},{12,14},{14,12},{16,18},{18,... | collective-permute-start | bytes 786440 | tf_op jit(solution)/shard_map/ppermute | solution.py:36
  2.3 11.8 %collective-permute-start.3 = (bf16[2,512,128]{2,1,0:T(8,128)(2,1)S(1)}, bf16[2,512,128]{2,1,0:T(8,128)(2,1)S(1)}, u32[]{:S(2)}, u32[]{:S(2)}) collective-permute-start(bf16[2,512,128]{2,1,0:T(8,128)(2,1)S(1)} %broadcast_select_fusion.refs_0_.refs_2_.refs_3_), channel_id=1, source_target_pairs={{0,4},{2,6},{4,8},{6,10},{8,12},{10,14},{12,0},{14,2},{16,20},{18,... | collective-permute-start | bytes 786440 | tf_op jit(solution)/shard_map/ppermute | solution.py:31
  3.9 14.6 %collective-permute-start.4 = (bf16[2,512,128]{2,1,0:T(8,128)(2,1)S(1)}, bf16[2,512,128]{2,1,0:T(8,128)(2,1)S(1)}, u32[]{:S(2)}, u32[]{:S(2)}) collective-permute-start(bf16[2,512,128]{2,1,0:T(8,128)(2,1)S(1)} %broadcast_select_fusion.refs_0_.refs_2_.refs_3_), channel_id=1, source_target_pairs={{0,8},{2,14},{4,12},{6,2},{8,0},{10,6},{12,4},{14,10},{16,24},{18,... | collective-permute-start | bytes 786440 | tf_op jit(solution)/shard_map/ppermute | solution.py:31
  6.7 1.4 %collective-permute-start.2 = (s32[1,512]{1,0:T(1,128)}, s32[1,512]{1,0:T(1,128)S(1)}, u32[]{:S(2)}, u32[]{:S(2)}) collective-permute-start(s32[1,512]{1,0:T(1,128)} %bitcast.4), channel_id=1, source_target_pairs={{0,2},{2,0},{4,6},{6,4},{8,10},{10,8},{12,14},{14,12},{16,18},{18,... | collective-permute-start | bytes 6152 | tf_op jit(solution)/shard_map/ppermute | solution.py:36
  8.0 10.5 %collective-permute-start.5 = (bf16[2,512,128]{2,1,0:T(8,128)(2,1)S(1)}, bf16[2,512,128]{2,1,0:T(8,128)(2,1)S(1)}, u32[]{:S(2)}, u32[]{:S(2)}) collective-permute-start(bf16[2,512,128]{2,1,0:T(8,128)(2,1)S(1)} %broadcast_select_fusion.refs_0_.refs_2_.refs_3_), channel_id=1, source_target_pairs={{0,12},{2,10},{4,0},{6,14},{8,4},{10,2},{12,8},{14,6},{16,28},{18,... | collective-permute-start | bytes 786440 | tf_op jit(solution)/shard_map/ppermute | solution.py:31
  9.5 1.0 %copy-start = (bf16[512,256]{1,0:T(8,128)(2,1)S(1)}, bf16[512,256]{1,0:T(8,128)(2,1)}, u32[]{:S(2)}) copy-start(bf16[512,256]{1,0:T(8,128)(2,1)} %refs_4_.13) | copy-start | bytes 786436
  10.4 0.9 %copy-start.3 = (bf16[512,256]{1,0:T(8,128)(2,1)S(1)}, bf16[512,256]{1,0:T(8,128)(2,1)}, u32[]{:S(2)}) copy-start(bf16[512,256]{1,0:T(8,128)(2,1)} %refs_6_.11) | copy-start | bytes 786436
  11.4 0.7 %copy-start.6 = (s32[512]{0:T(512)S(1)}, s32[512]{0:T(512)}, u32[]{:S(2)}) copy-start(s32[512]{0:T(512)} %param.9) | copy-start | bytes 6148
  14.1 1.0 %copy-start.1 = (bf16[512,256]{1,0:T(8,128)(2,1)S(1)}, bf16[512,256]{1,0:T(8,128)(2,1)}, u32[]{:S(2)}) copy-start(bf16[512,256]{1,0:T(8,128)(2,1)} %refs_4_.13) | copy-start | bytes 786436
  15.1 0.9 %copy-start.4 = (bf16[512,256]{1,0:T(8,128)(2,1)S(1)}, bf16[512,256]{1,0:T(8,128)(2,1)}, u32[]{:S(2)}) copy-start(bf16[512,256]{1,0:T(8,128)(2,1)} %refs_6_.11) | copy-start | bytes 786436
  16.0 0.7 %copy-start.7 = (s32[512]{0:T(512)S(1)}, s32[512]{0:T(512)}, u32[]{:S(2)}) copy-start(s32[512]{0:T(512)} %param.9) | copy-start | bytes 6148
  18.6 1.3 %collective-permute-start.6 = (f32[12,512]{1,0:T(8,128)S(1)}, f32[12,512]{1,0:T(8,128)S(1)}, u32[]{:S(2)}, u32[]{:S(2)}) collective-permute-start(f32[12,512]{1,0:T(8,128)S(1)} %get-tuple-element.31.refs_0_), channel_id=1, source_target_pairs={{0,2},{2,0},{4,6},{6,4},{8,10},{10,8},{12,14},{14,12},{16,18},{18,... | collective-permute-start | bytes 73736 | tf_op jit(solution)/shard_map/ppermute | solution.py:36
  20.1 13.1 %collective-permute-start.8 = (bf16[2,512,128]{2,1,0:T(8,128)(2,1)S(1)}, bf16[2,512,128]{2,1,0:T(8,128)(2,1)S(1)}, u32[]{:S(2)}, u32[]{:S(2)}) collective-permute-start(bf16[2,512,128]{2,1,0:T(8,128)(2,1)S(1)} %get-tuple-element.41), channel_id=1, source_target_pairs={{0,8},{2,10},{4,12},{6,14},{8,0},{10,2},{12,4},{14,6},{16,24},{18,... | collective-permute-start | bytes 786440 | tf_op jit(solution)/shard_map/ppermute | solution.py:31
  24.7 11.6 %collective-permute-start.9 = (bf16[2,512,128]{2,1,0:T(8,128)(2,1)S(1)}, bf16[2,512,128]{2,1,0:T(8,128)(2,1)S(1)}, u32[]{:S(2)}, u32[]{:S(2)}) collective-permute-start(bf16[2,512,128]{2,1,0:T(8,128)(2,1)S(1)} %get-tuple-element.42), channel_id=1, source_target_pairs={{0,4},{2,14},{4,8},{6,2},{8,12},{10,6},{12,0},{14,10},{16,20},{18,... | collective-permute-start | bytes 786440 | tf_op jit(solution)/shard_map/ppermute | solution.py:31
  26.6 3.2 %copy-start.2 = (bf16[512,256]{1,0:T(8,128)(2,1)S(1)}, bf16[512,256]{1,0:T(8,128)(2,1)}, u32[]{:S(2)}) copy-start(bf16[512,256]{1,0:T(8,128)(2,1)} %refs_4_.13) | copy-start | bytes 786436
  26.6 3.2 %copy-start.5 = (bf16[512,256]{1,0:T(8,128)(2,1)S(1)}, bf16[512,256]{1,0:T(8,128)(2,1)}, u32[]{:S(2)}) copy-start(bf16[512,256]{1,0:T(8,128)(2,1)} %refs_6_.11) | copy-start | bytes 786436
  26.6 3.2 %copy-start.8 = (s32[512]{0:T(512)S(1)}, s32[512]{0:T(512)}, u32[]{:S(2)}) copy-start(s32[512]{0:T(512)} %param.9) | copy-start | bytes 6148
  26.8 11.4 %collective-permute-start.10 = (bf16[2,512,128]{2,1,0:T(8,128)(2,1)S(1)}, bf16[2,512,128]{2,1,0:T(8,128)(2,1)S(1)}, u32[]{:S(2)}, u32[]{:S(2)}) collective-permute-start(bf16[2,512,128]{2,1,0:T(8,128)(2,1)S(1)} %get-tuple-element.43), channel_id=1, source_target_pairs={{0,12},{2,6},{4,0},{6,10},{8,4},{10,14},{12,8},{14,2},{16,28},{18,... | collective-permute-start | bytes 786440 | tf_op jit(solution)/shard_map/ppermute | solution.py:31
  33.1 8.5 %collective-permute-start.7 = (f32[256,512]{1,0:T(8,128)S(1)}, f32[256,512]{1,0:T(8,128)S(1)}, u32[]{:S(2)}, u32[]{:S(2)}) collective-permute-start(f32[256,512]{1,0:T(8,128)S(1)} %slice_bitcast_fusion), channel_id=1, source_target_pairs={{0,2},{2,0},{4,6},{6,4},{8,10},{10,8},{12,14},{14,12},{16,18},{18,... | collective-permute-start | bytes 1572872 | tf_op jit(solution)/shard_map/ppermute | solution.py:36
  38.3 9.2 %collective-permute-start.11 = (bf16[2,512,128]{2,1,0:T(8,128)(2,1)S(1)}, bf16[2,512,128]{2,1,0:T(8,128)(2,1)S(1)}, u32[]{:S(2)}, u32[]{:S(2)}) collective-permute-start(bf16[2,512,128]{2,1,0:T(8,128)(2,1)S(1)} %shard_map.79.mine), channel_id=1, source_target_pairs={{0,1},{1,0},{2,3},{3,2},{4,5},{5,4},{6,7},{7,6},{8,9},{9,8},{10,11... | collective-permute-start | bytes 786440 | tf_op jit(solution)/shard_map/ppermute | solution.py:40

commit v5 on v4

--- a/solution.py
+++ b/solution.py
@@ -28,6 +28,12 @@
 def chip_shift(array, even, odd):
     n = lax.axis_size("cp")
     pairs = [(i, i - i % GROUP + (i % GROUP + 2 * (odd if i % 2 else even)) % GROUP) for i in range(n)]
+    return lax.ppermute(array, "cp", pairs)
+
+
+def chip_permute(array, even, odd):
+    n = lax.axis_size("cp")
+    pairs = [(i, i - i % GROUP + 2 * (odd if i % 2 else even)[i % GROUP // 2] + i % 2) for i in range(n)]
     return lax.ppermute(array, "cp", pairs)
 
 
@@ -55,14 +61,22 @@
 
 
 def stats_kernel(slot, pos_ref, *refs):
-    if slot:
+    if slot == 0:
+        kv, q_own, g_own, st_own, stats, *copies = refs
+        for src, dst in zip((q_own, g_own, st_own), copies):
+            dst[...] = src[...]
+        rows = ((q_own, g_own, st_own),)
+    else:
         stats_in, *refs = refs
-    if slot > 1:
-        refs = refs[2:]
-    kv, q_own, q_sib, g_own, g_sib, st_own, st_sib, stats, *kept = refs
+        if slot == 1:
+            own, *refs = refs
+        else:
+            refs = refs[2:]
+        kv, q_own, q_sib, g_own, g_sib, st_own, st_sib, stats, *kept = refs
+        rows = ((q_own, g_own, st_own), (q_sib, g_sib, st_sib))
     cp = pos_ref[0]
     in_group = lax.rem(cp, GROUP)
-    size = q_own.shape[0]
+    size = kv.shape[1]
     if slot:
         stats[...] = stats_in[...]
     else:
@@ -70,33 +84,37 @@
             stats[at : at + 1, :] = jnp.full((1, size), FLOOR)
             stats[at + 1 : at + 3, :] = jnp.zeros((2, size))
     chips = slot_distance(slot, cp)
-    key_block = cp - 2 * chips
-    for group, (q, g, st) in enumerate(((q_own, g_own, st_own), (q_sib, g_sib, st_sib))):
-        row_block = cp if group == 0 else cp + 1 - 2 * lax.rem(cp, 2)
-
-        def work(q=q, g=g, st=st, group=group, row_block=row_block):
-            for head in range(2):
-                cols = pl.ds(head * HDIM, HDIM)
-                s = masked_scores(kv[0], q[:, cols], st[...], row_block * size, key_block * size, slot == 0 and group == 0)
-                dp = dot(kv[1], g[:, cols], NT)
-                if slot:
-                    kept[0][chips - 1, 2 * group + head] = s
-                    kept[1][chips - 1, 2 * group + head] = dp
-                at = 3 * (2 * group + head)
-                m = stats[at : at + 1, :]
-                new = jnp.maximum(m, jnp.max(s, axis=0, keepdims=True))
-                p = jnp.exp2((s - new) * EXP_SCALE)
-                f = jnp.exp2((m - new) * EXP_SCALE)
-                stats[at : at + 1, :] = new
-                stats[at + 1 : at + 2, :] = stats[at + 1 : at + 2, :] * f + jnp.sum(p, axis=0, keepdims=True)
-                stats[at + 2 : at + 3, :] = stats[at + 2 : at + 3, :] * f + jnp.sum(p * dp, axis=0, keepdims=True)
-
-        if slot == 0 and group == 0:
-            work()
-        elif slot == 0:
-            pl.when(lax.rem(cp, 2) == 0)(work)
-        else:
-            pl.when(in_group >= 2 * chips)(work)
+
+    def work(kv, group, chips, keep):
+        q, g, st = rows[group]
+        key_base = (cp - 2 * chips) * size
+        row_base = (cp if group == 0 else cp + 1 - 2 * lax.rem(cp, 2)) * size
+        for head in range(2):
+            cols = pl.ds(head * HDIM, HDIM)
+            s = masked_scores(kv[0], q[:, cols], st[...], row_base, key_base, slot == 0)
+            dp = dot(kv[1], g[:, cols], NT)
+            if keep:
+                kept[0][chips - 1, 2 * group + head] = s
+                kept[1][chips - 1, 2 * group + head] = dp
+            at = 3 * (2 * group + head)
+            m = stats[at : at + 1, :]
+            new = jnp.maximum(m, jnp.max(s, axis=0, keepdims=True))
+            p = jnp.exp2((s - new) * EXP_SCALE)
+            f = jnp.exp2((m - new) * EXP_SCALE)
+            stats[at : at + 1, :] = new
+            stats[at + 1 : at + 2, :] = stats[at + 1 : at + 2, :] * f + jnp.sum(p, axis=0, keepdims=True)
+            stats[at + 2 : at + 3, :] = stats[at + 2 : at + 3, :] * f + jnp.sum(p * dp, axis=0, keepdims=True)
+
+    if slot == 0:
+        work(kv, 0, 0, False)
+    if slot == 1:
+        pl.when(lax.rem(cp, 2) == 0)(lambda: work(own, 1, 0, False))
+    if slot:
+
+        @pl.when(in_group >= 2 * chips)
+        def _():
+            work(kv, 0, chips, True)
+            work(kv, 1, chips, True)
 
 
 def merged(stats, other, at, other_at):
@@ -202,15 +220,19 @@
     out = [jax.ShapeDtypeStruct((12, size), jnp.float32)]
     if slot:
         out += [jax.ShapeDtypeStruct((3, 4, size, size), jnp.float32)] * 2
-    kept = len(before[1:])
+    else:
+        out += [jax.ShapeDtypeStruct(a.shape, a.dtype) for a in rows]
+    in_specs = [SM] + [VM] * (len(before) + 1 + len(rows))
+    if slot > 1:
+        in_specs[2:4] = [pl.BlockSpec(memory_space=pl.ANY)] * 2
     return pl.pallas_call(
         functools.partial(stats_kernel, slot),
         out_shape=out,
-        in_specs=[SM] + [VM] * len(before[:1]) + [pl.BlockSpec(memory_space=pl.ANY)] * kept + [VM] * (1 + len(rows)),
+        in_specs=in_specs,
         out_specs=[VM] * len(out),
-        input_output_aliases={2: 1, 3: 2} if kept else {},
+        input_output_aliases={2: 1, 3: 2} if slot > 1 else {},
         compiler_params=pltpu.CompilerParams(vmem_limit_bytes=KERNEL_VMEM),
-        cost_estimate=BLOCK_COST,
+        cost_estimate=NO_COST,
         name="stats",
     )(cp, *before, kv, *rows)
 
@@ -244,15 +266,18 @@
     slot2 = chip_shift(kv, 2, 3)
     slot3 = chip_shift(kv, 3, 2)
     starts = doc_start.reshape(1, size)
-    rows = (query, core_swap(query), grad_out, core_swap(grad_out), starts, core_swap(starts))
-
-    (stats,) = call_stats(0, cp, (), kv, rows)
-    before = call_stats(1, cp, (stats,), slot1, rows)
+    kv, near_query, near_grad = lax.optimization_barrier((kv, query, grad_out))
+    far_query, near_starts = lax.optimization_barrier((core_swap(near_query), starts))
+    far_grad, far_starts = core_swap(near_grad), core_swap(near_starts)
+
+    stats, *own_rows = call_stats(0, cp, (), kv, (query, grad_out, starts))
+    rows = (own_rows[0], far_query, own_rows[1], far_grad, own_rows[2], far_starts)
+    before = call_stats(1, cp, (stats, kv), slot1, rows)
     before = call_stats(2, cp, before, slot2, rows)
     stats, *kept = call_stats(3, cp, before, slot3, rows)
 
     dq, part, fin = call_grads(0, cp, (stats, core_swap(stats)), slot2, slot3, rows, kept)
-    back_a = chip_shift(part, 2, 2)
+    back_a = chip_permute(part, (3, 2, 0, 1), (3, 2, 0, 1))
     dq, part = call_grads(1, cp, (dq, fin), slot3, slot1, rows, kept)
     back_b = chip_shift(part, 1, 3)
     dq, part = call_grads(2, cp, (dq, fin), slot1, slot2, rows, kept)

time: 49.1 us -> 48 us (0.978)
  the two profiles are of different devices: /device:TPU:0 before, /device:TPU:14 now
where the time goes in v5:
time: 48 us; the launch traced here: 47.7 us
  Pallas kernels  17.8 us (37%)
  waiting for transfers between devices  17.2 us (36%)
  starting transfers between devices  8.26 us (17%)
  local copies, waits for them, and re-layouts  2.61 us (5%)
  other arithmetic  1.07 us (2%)
  between operations  0.79 us (2%)
    ppermute x5, waiting for transfers between devices, chip_shift(): return lax.ppermute(array, 'cp', pairs)  8.95 us
    pallas_call x4, Pallas kernels, call_grads(): pl.pallas_call(functools.partial(grads_kernel, stage), out_shape=out, in_...  8.7 us
    pallas_call x4, Pallas kernels, call_stats(): pl.pallas_call(functools.partial(stats_kernel, slot), out_shape=out, in_s...  7.35 us
    ppermute x1, waiting for transfers between devices, hd_swap(): return lax.ppermute(array, 'hd', [(0, 1), (1, 0)])  5.96 us
    ppermute x5, starting transfers between devices, chip_shift(): return lax.ppermute(array, 'cp', pairs)  5.06 us
    unnamed x6, local copies, waits for them, and re-layouts  2.58 us
    ppermute x1, starting transfers between devices, hd_swap(): return lax.ppermute(array, 'hd', [(0, 1), (1, 0)])  2.37 us
    pallas_call x5, Pallas kernels, simple(): pl.pallas_call(kernel, out_shape=out, in_specs=[VM] * len(args), out_spec...  1.77 us
  transfers between devices with their start and end apart: 12, of which 7 were waited for; matrix products, arithmetic and copies ran while one was open for 0% of the time, Pallas kernels for 28%

profile of v5, /device:TPU:14, one launch (start us, length us, event | category | flops | bytes accessed | tf_op | source)
XLA Modules:
  0.0 47.7 jit_solution(13386672971898032610)
XLA Ops:
  0.6 1.1 %broadcast_select_fusion.refs_0_.refs_1_.refs_2_.refs_3_ = bf16[2,512,128]{2,1,0:T(8,128)(2,1)S(1)} fusion(pred[2]{0:T(512)(128)(4,1)S(1)} %iota_compare_fusion, bf16[512,128]{1,0:T(8,128)(2,1)} %param.7, bf16[512,128]{1,0:T(8,128)(2,1)} %param.6), kind=kLoop, calls=%fused_computation.1 | loop fusion | flops 131072 | bytes 524290 | tf_op jit(solution)/shard_map/jit(_where)/select_n | solution.py:264
  1.7 0.1 collective-permute-start.1
  1.8 0.5 %collective-permute-start.2 = (bf16[512,256]{1,0:T(8,128)(2,1)}, bf16[512,256]{1,0:T(8,128)(2,1)S(1)}, u32[]{:S(2)}, u32[]{:S(2)}) collective-permute-start(bf16[512,256]{1,0:T(8,128)(2,1)} %refs_2_.1), channel_id=1, source_target_pairs={{0,2},{2,0},{4,6},{6,4},{8,10},{10,8},{12,14},{14,12},{16,18},{18,... | collective-permute-start | bytes 786440 | tf_op jit(solution)/shard_map/ppermute | solution.py:42
  2.3 0.5 %collective-permute-start = (bf16[2,512,128]{2,1,0:T(8,128)(2,1)S(1)}, bf16[2,512,128]{2,1,0:T(8,128)(2,1)S(1)}, u32[]{:S(2)}, u32[]{:S(2)}) collective-permute-start(bf16[2,512,128]{2,1,0:T(8,128)(2,1)S(1)} %broadcast_select_fusion.refs_0_.refs_1_.refs_2_.refs_3_), channel_id=1, source_target_pairs={{0,4},{2,6},{4,8},{6,10},{8,12},{10,14},{12,0},{14,2},{16,20},{18,... | collective-permute-start | bytes 786440 | tf_op jit(solution)/shard_map/ppermute | solution.py:31
  2.8 2.4 %collective-permute-start.4 = (bf16[2,512,128]{2,1,0:T(8,128)(2,1)S(1)}, bf16[2,512,128]{2,1,0:T(8,128)(2,1)S(1)}, u32[]{:S(2)}, u32[]{:S(2)}) collective-permute-start(bf16[2,512,128]{2,1,0:T(8,128)(2,1)S(1)} %broadcast_select_fusion.refs_0_.refs_1_.refs_2_.refs_3_), channel_id=1, source_target_pairs={{0,8},{2,14},{4,12},{6,2},{8,0},{10,6},{12,4},{14,10},{16,24},{18,... | collective-permute-start | bytes 786440 | tf_op jit(solution)/shard_map/ppermute | solution.py:31
  5.2 0.0 collective-permute-start.5
  5.2 0.0 collective-permute-done.1.refs_4_.refs_5_
  5.2 0.0 collective-permute-start.3
  5.2 0.0 copy-start
  5.2 0.9 %copy-done = bf16[512,256]{1,0:T(8,128)(2,1)S(1)} copy-done((bf16[512,256]{1,0:T(8,128)(2,1)S(1)}, bf16[512,256]{1,0:T(8,128)(2,1)}, u32[]{:S(2)}) %copy-start) | copy-done | bytes 262168
  6.2 0.0 copy-start.1
  6.2 0.9 %copy-done.1 = bf16[512,256]{1,0:T(8,128)(2,1)S(1)} copy-done((bf16[512,256]{1,0:T(8,128)(2,1)S(1)}, bf16[512,256]{1,0:T(8,128)(2,1)}, u32[]{:S(2)}) %copy-start.1) | copy-done | bytes 262168
  7.1 0.0 copy-start.2
  7.1 0.7 %copy-done.2 = s32[512]{0:T(512)S(1)} copy-done((s32[512]{0:T(512)S(1)}, s32[512]{0:T(512)}, u32[]{:S(2)}) %copy-start.2) | copy-done | bytes 2072
  7.8 1.2 %stats.4 = (f32[12,512]{1,0:T(8,128)S(1)}, bf16[512,256]{1,0:T(8,128)(2,1)S(1)}, bf16[512,256]{1,0:T(8,128)(2,1)S(1)}, s32[1,512]{1,0:T(1,128)S(1)}) custom-call(s32[1]{0:T(128)} %bitcast.pos_ref, bf16[2,512,128]{2,1,0:T(8,128)(2,1)S(1)} %broadcast_select_fusion.refs_0_.refs_1_.refs_2_.refs_3_, bf16[512,256]{1,0:T(8,128)(2,1)S(1)} %copy-done, ...), custom_call_target="tpu_custom_call" | custom-call | bytes 1024 | tf_op jit(solution)/shard_map/stats/pallas_call | solution.py:228
  9.0 0.0 collective-permute-done.2.refs_6_.refs_7_
  9.0 2.5 %collective-permute-done.refs_2_.refs_3_ = bf16[2,512,128]{2,1,0:T(8,128)(2,1)S(1)} collective-permute-done((bf16[2,512,128]{2,1,0:T(8,128)(2,1)S(1)}, bf16[2,512,128]{2,1,0:T(8,128)(2,1)S(1)}, u32[]{:S(2)}, u32[]{:S(2)}) %collective-permute-start) | collective-permute-done | bytes 262176 | tf_op jit(solution)/shard_map/ppermute | solution.py:31
  11.5 0.0 collective-permute-done.3.refs_8_.refs_9_
  11.5 2.7 %stats.5 = (f32[12,512]{1,0:T(8,128)S(1)}, f32[3,4,512,512]{3,2,1,0:T(8,128)S(1)}, f32[3,4,512,512]{3,2,1,0:T(8,128)S(1)}) custom-call(s32[1]{0:T(128)} %bitcast.pos_ref, f32[12,512]{1,0:T(8,128)S(1)} %get-tuple-element.35.refs_0_, bf16[2,512,128]{2,1,0:T(8,128)(2,1)S(1)} %broadcast_select_fusion.refs_0_.refs_1_.refs_2_.refs_3_, ...), custom_call_target="tpu_custom_call" | custom-call | bytes 1024 | tf_op jit(solution)/shard_map/stats/pallas_call | solution.py:228
  14.1 0.0 collective-permute-done.4.refs_3_.refs_2_
  14.1 1.8 %stats.6 = (f32[12,512]{1,0:T(8,128)S(1)}, f32[3,4,512,512]{3,2,1,0:T(8,128)S(1)}, f32[3,4,512,512]{3,2,1,0:T(8,128)S(1)}) custom-call(s32[1]{0:T(128)} %bitcast.pos_ref, f32[12,512]{1,0:T(8,128)S(1)} %get-tuple-element.43.refs_0_, f32[3,4,512,512]{3,2,1,0:T(8,128)S(1)} %get-tuple-element.44.refs_1_, ...), custom_call_target="tpu_custom_call", output_to_operand_aliasing={{1}: (2, {}), {2}: (3, {})} | custom-call | bytes 1024 | tf_op jit(solution)/shard_map/stats/pallas_call | solution.py:228
  15.9 1.7 %collective-permute-done.5.refs_3_.refs_2_ = bf16[2,512,128]{2,1,0:T(8,128)(2,1)S(1)} collective-permute-done((bf16[2,512,128]{2,1,0:T(8,128)(2,1)S(1)}, bf16[2,512,128]{2,1,0:T(8,128)(2,1)S(1)}, u32[]{:S(2)}, u32[]{:S(2)}) %collective-permute-start.5) | collective-permute-done | bytes 262176 | tf_op jit(solution)/shard_map/ppermute | solution.py:31
  17.6 1.8 %stats.7 = (f32[12,512]{1,0:T(8,128)S(1)}, f32[3,4,512,512]{3,2,1,0:T(8,128)S(1)}, f32[3,4,512,512]{3,2,1,0:T(8,128)S(1)}) custom-call(s32[1]{0:T(128)} %bitcast.pos_ref, f32[12,512]{1,0:T(8,128)S(1)} %get-tuple-element.46.refs_0_, f32[3,4,512,512]{3,2,1,0:T(8,128)S(1)} %get-tuple-element.47.refs_1_, ...), custom_call_target="tpu_custom_call", output_to_operand_aliasing={{1}: (2, {}), {2}: (3, {})} | custom-call | bytes 1024 | tf_op jit(solution)/shard_map/stats/pallas_call | solution.py:228
  19.4 0.1 collective-permute-start.6
  19.5 1.2 %collective-permute-done.6.refs_1_ = f32[12,512]{1,0:T(8,128)S(1)} collective-permute-done((f32[12,512]{1,0:T(8,128)S(1)}, f32[12,512]{1,0:T(8,128)S(1)}, u32[]{:S(2)}, u32[]{:S(2)}) %collective-permute-start.6) | collective-permute-done | bytes 24608 | tf_op jit(solution)/shard_map/ppermute | solution.py:42
  20.7 1.8 %grads.4 = (f32[2,256,512]{2,1,0:T(8,128)S(1)}, bf16[2,512,128]{2,1,0:T(8,128)(2,1)S(1)}, f32[8,512]{1,0:T(8,128)S(1)}) custom-call(s32[1]{0:T(128)} %bitcast.pos_ref, f32[12,512]{1,0:T(8,128)S(1)} %get-tuple-element.49.refs_0_, f32[12,512]{1,0:T(8,128)S(1)} %collective-permute-done.6.refs_1_, ...), custom_call_target="tpu_custom_call" | custom-call | flops 33554432 | bytes 1024 | tf_op jit(solution)/shard_map/grads/pallas_call | solution.py:248
  22.4 0.1 collective-permute-start.8
  22.5 1.9 %grads.5 = (f32[2,256,512]{2,1,0:T(8,128)S(1)}, bf16[2,512,128]{2,1,0:T(8,128)(2,1)S(1)}) custom-call(s32[1]{0:T(128)} %bitcast.pos_ref, f32[2,256,512]{2,1,0:T(8,128)S(1)} %get-tuple-element.52.refs_0_, f32[8,512]{1,0:T(8,128)S(1)} %get-tuple-element.53.refs_1_, bf16[2,512,128]{2,1,0:T(8,128)(2,1)S(1)} %collective-permute-done.5.refs_3_.refs_2_, ...), custom_call_target="tpu_custom_call" | custom-call | flops 33554432 | bytes 1024 | tf_op jit(solution)/shard_map/grads/pallas_call | solution.py:248
  24.5 1.7 %collective-permute-start.9 = (bf16[2,512,128]{2,1,0:T(8,128)(2,1)S(1)}, bf16[2,512,128]{2,1,0:T(8,128)(2,1)S(1)}, u32[]{:S(2)}, u32[]{:S(2)}) collective-permute-start(bf16[2,512,128]{2,1,0:T(8,128)(2,1)S(1)} %get-tuple-element.60), channel_id=1, source_target_pairs={{0,4},{2,14},{4,8},{6,2},{8,12},{10,6},{12,0},{14,10},{16,20},{18,... | collective-permute-start | bytes 786440 | tf_op jit(solution)/shard_map/ppermute | solution.py:31
  26.2 1.8 %grads.6 = (f32[2,256,512]{2,1,0:T(8,128)S(1)}, bf16[2,512,128]{2,1,0:T(8,128)(2,1)S(1)}) custom-call(s32[1]{0:T(128)} %bitcast.pos_ref, f32[2,256,512]{2,1,0:T(8,128)S(1)} %get-tuple-element.54.refs_0_, f32[8,512]{1,0:T(8,128)S(1)} %get-tuple-element.53.refs_1_, bf16[2,512,128]{2,1,0:T(8,128)(2,1)S(1)} %collective-permute-done.refs_2_.refs_3_, ...), custom_call_target="tpu_custom_call" | custom-call | flops 33554432 | bytes 1024 | tf_op jit(solution)/shard_map/grads/pallas_call | solution.py:248
  27.9 0.5 collective-permute-start.10
  28.4 3.2 %grads.7 = (f32[2,256,512]{2,1,0:T(8,128)S(1)}, f32[2,512,128]{2,1,0:T(8,128)S(1)}) custom-call(s32[1]{0:T(128)} %bitcast.pos_ref, f32[2,256,512]{2,1,0:T(8,128)S(1)} %get-tuple-element.55.refs_0_, f32[8,512]{1,0:T(8,128)S(1)} %get-tuple-element.53.refs_1_, bf16[2,512,128]{2,1,0:T(8,128)(2,1)S(1)} %broadcast_select_fusion.refs_0_.refs_1_.refs_2_.refs_3_, ...), custom_call_target="tpu_custom_call" | custom-call | bytes 1024 | tf_op jit(solution)/shard_map/grads/pallas_call | solution.py:248
  31.7 0.1 collective-permute-start.7
  31.8 1.1 %collective-permute-done.8.part = bf16[2,512,128]{2,1,0:T(8,128)(2,1)S(1)} collective-permute-done((bf16[2,512,128]{2,1,0:T(8,128)(2,1)S(1)}, bf16[2,512,128]{2,1,0:T(8,128)(2,1)S(1)}, u32[]{:S(2)}, u32[]{:S(2)}) %collective-permute-start.8) | collective-permute-done | bytes 262176 | tf_op jit(solution)/shard_map/ppermute | solution.py:37
  32.9 0.6 %collective-permute-done.9.part = bf16[2,512,128]{2,1,0:T(8,128)(2,1)S(1)} collective-permute-done((bf16[2,512,128]{2,1,0:T(8,128)(2,1)S(1)}, bf16[2,512,128]{2,1,0:T(8,128)(2,1)S(1)}, u32[]{:S(2)}, u32[]{:S(2)}) %collective-permute-start.9) | collective-permute-done | bytes 262176 | tf_op jit(solution)/shard_map/ppermute | solution.py:31
  33.6 4.1 %collective-permute-done.10.part = bf16[2,512,128]{2,1,0:T(8,128)(2,1)S(1)} collective-permute-done((bf16[2,512,128]{2,1,0:T(8,128)(2,1)S(1)}, bf16[2,512,128]{2,1,0:T(8,128)(2,1)S(1)}, u32[]{:S(2)}, u32[]{:S(2)}) %collective-permute-start.10) | collective-permute-done | bytes 262176 | tf_op jit(solution)/shard_map/ppermute | solution.py:31
  37.7 0.1 shard_map.79.mine
  37.8 2.4 %collective-permute-start.11 = (bf16[2,512,128]{2,1,0:T(8,128)(2,1)S(1)}, bf16[2,512,128]{2,1,0:T(8,128)(2,1)S(1)}, u32[]{:S(2)}, u32[]{:S(2)}) collective-permute-start(bf16[2,512,128]{2,1,0:T(8,128)(2,1)S(1)} %shard_map.79.mine), channel_id=1, source_target_pairs={{0,1},{1,0},{2,3},{3,2},{4,5},{5,4},{6,7},{7,6},{8,9},{9,8},{10,11... | collective-permute-start | bytes 786440 | tf_op jit(solution)/shard_map/ppermute | solution.py:46
  40.2 0.0 collective-permute-done.7.other
  40.2 0.9 %shard_map.76 = (bf16[512,256]{1,0:T(8,128)(2,1)}, f32[8,128]{1,0:T(8,128)S(1)}) custom-call(f32[2,256,512]{2,1,0:T(8,128)S(1)} %get-tuple-element.56.mine, f32[256,512]{1,0:T(8,128)S(1)} %collective-permute-done.7.other), custom_call_target="tpu_custom_call" | custom-call | bytes 1024 | tf_op jit(solution)/shard_map/pallas_call | solution.py:208
  41.0 6.0 %collective-permute-done.11.other = bf16[2,512,128]{2,1,0:T(8,128)(2,1)S(1)} collective-permute-done((bf16[2,512,128]{2,1,0:T(8,128)(2,1)S(1)}, bf16[2,512,128]{2,1,0:T(8,128)(2,1)S(1)}, u32[]{:S(2)}, u32[]{:S(2)}) %collective-permute-start.11) | collective-permute-done | bytes 262176 | tf_op jit(solution)/shard_map/ppermute | solution.py:46
  47.0 0.7 %shard_map.80 = (bf16[512,128]{1,0:T(8,128)(2,1)}, bf16[512,128]{1,0:T(8,128)(2,1)}) custom-call(bf16[2,512,128]{2,1,0:T(8,128)(2,1)S(1)} %shard_map.79.mine, bf16[2,512,128]{2,1,0:T(8,128)(2,1)S(1)} %collective-permute-done.11.other, f32[8,128]{1,0:T(8,128)S(1)} %get-tuple-element.62._), custom_call_target="tpu_custom_call" | custom-call | bytes 1024 | tf_op jit(solution)/shard_map/pallas_call | solution.py:208
  (4 shorter events, 0.1 us)
Async XLA Ops:
  1.7 3.5 %collective-permute-start.1 = (bf16[512,256]{1,0:T(8,128)(2,1)}, bf16[512,256]{1,0:T(8,128)(2,1)S(1)}, u32[]{:S(2)}, u32[]{:S(2)}) collective-permute-start(bf16[512,256]{1,0:T(8,128)(2,1)} %refs_1_.1), channel_id=1, source_target_pairs={{0,2},{2,0},{4,6},{6,4},{8,10},{10,8},{12,14},{14,12},{16,18},{18,... | collective-permute-start | bytes 786440 | tf_op jit(solution)/shard_map/ppermute | solution.py:42
  1.8 7.2 %collective-permute-start.2 = (bf16[512,256]{1,0:T(8,128)(2,1)}, bf16[512,256]{1,0:T(8,128)(2,1)S(1)}, u32[]{:S(2)}, u32[]{:S(2)}) collective-permute-start(bf16[512,256]{1,0:T(8,128)(2,1)} %refs_2_.1), channel_id=1, source_target_pairs={{0,2},{2,0},{4,6},{6,4},{8,10},{10,8},{12,14},{14,12},{16,18},{18,... | collective-permute-start | bytes 786440 | tf_op jit(solution)/shard_map/ppermute | solution.py:42
  2.3 9.2 %collective-permute-start = (bf16[2,512,128]{2,1,0:T(8,128)(2,1)S(1)}, bf16[2,512,128]{2,1,0:T(8,128)(2,1)S(1)}, u32[]{:S(2)}, u32[]{:S(2)}) collective-permute-start(bf16[2,512,128]{2,1,0:T(8,128)(2,1)S(1)} %broadcast_select_fusion.refs_0_.refs_1_.refs_2_.refs_3_), channel_id=1, source_target_pairs={{0,4},{2,6},{4,8},{6,10},{8,12},{10,14},{12,0},{14,2},{16,20},{18,... | collective-permute-start | bytes 786440 | tf_op jit(solution)/shard_map/ppermute | solution.py:31
  2.8 11.4 %collective-permute-start.4 = (bf16[2,512,128]{2,1,0:T(8,128)(2,1)S(1)}, bf16[2,512,128]{2,1,0:T(8,128)(2,1)S(1)}, u32[]{:S(2)}, u32[]{:S(2)}) collective-permute-start(bf16[2,512,128]{2,1,0:T(8,128)(2,1)S(1)} %broadcast_select_fusion.refs_0_.refs_1_.refs_2_.refs_3_), channel_id=1, source_target_pairs={{0,8},{2,14},{4,12},{6,2},{8,0},{10,6},{12,4},{14,10},{16,24},{18,... | collective-permute-start | bytes 786440 | tf_op jit(solution)/shard_map/ppermute | solution.py:31
  5.2 12.4 %collective-permute-start.5 = (bf16[2,512,128]{2,1,0:T(8,128)(2,1)S(1)}, bf16[2,512,128]{2,1,0:T(8,128)(2,1)S(1)}, u32[]{:S(2)}, u32[]{:S(2)}) collective-permute-start(bf16[2,512,128]{2,1,0:T(8,128)(2,1)S(1)} %broadcast_select_fusion.refs_0_.refs_1_.refs_2_.refs_3_), channel_id=1, source_target_pairs={{0,12},{2,10},{4,0},{6,14},{8,4},{10,2},{12,8},{14,6},{16,28},{18,... | collective-permute-start | bytes 786440 | tf_op jit(solution)/shard_map/ppermute | solution.py:31
  5.2 6.3 %collective-permute-start.3 = (s32[1,512]{1,0:T(1,128)}, s32[1,512]{1,0:T(1,128)S(1)}, u32[]{:S(2)}, u32[]{:S(2)}) collective-permute-start(s32[1,512]{1,0:T(1,128)} %bitcast.4), channel_id=1, source_target_pairs={{0,2},{2,0},{4,6},{6,4},{8,10},{10,8},{12,14},{14,12},{16,18},{18,... | collective-permute-start | bytes 6152 | tf_op jit(solution)/shard_map/ppermute | solution.py:42
  5.2 1.0 %copy-start = (bf16[512,256]{1,0:T(8,128)(2,1)S(1)}, bf16[512,256]{1,0:T(8,128)(2,1)}, u32[]{:S(2)}) copy-start(bf16[512,256]{1,0:T(8,128)(2,1)} %refs_1_.1) | copy-start | bytes 786436
  6.2 0.9 %copy-start.1 = (bf16[512,256]{1,0:T(8,128)(2,1)S(1)}, bf16[512,256]{1,0:T(8,128)(2,1)}, u32[]{:S(2)}) copy-start(bf16[512,256]{1,0:T(8,128)(2,1)} %refs_2_.1) | copy-start | bytes 786436
  7.1 0.7 %copy-start.2 = (s32[512]{0:T(512)S(1)}, s32[512]{0:T(512)}, u32[]{:S(2)}) copy-start(s32[512]{0:T(512)} %param.9) | copy-start | bytes 6148
  19.4 1.3 %collective-permute-start.6 = (f32[12,512]{1,0:T(8,128)S(1)}, f32[12,512]{1,0:T(8,128)S(1)}, u32[]{:S(2)}, u32[]{:S(2)}) collective-permute-start(f32[12,512]{1,0:T(8,128)S(1)} %get-tuple-element.49.refs_0_), channel_id=1, source_target_pairs={{0,2},{2,0},{4,6},{6,4},{8,10},{10,8},{12,14},{14,12},{16,18},{18,... | collective-permute-start | bytes 73736 | tf_op jit(solution)/shard_map/ppermute | solution.py:42
  22.4 10.4 %collective-permute-start.8 = (bf16[2,512,128]{2,1,0:T(8,128)(2,1)S(1)}, bf16[2,512,128]{2,1,0:T(8,128)(2,1)S(1)}, u32[]{:S(2)}, u32[]{:S(2)}) collective-permute-start(bf16[2,512,128]{2,1,0:T(8,128)(2,1)S(1)} %get-tuple-element.59), channel_id=1, source_target_pairs={{0,12},{2,14},{4,8},{6,10},{8,0},{10,2},{12,4},{14,6},{16,28},{18,... | collective-permute-start | bytes 786440 | tf_op jit(solution)/shard_map/ppermute | solution.py:37
  24.5 9.1 %collective-permute-start.9 = (bf16[2,512,128]{2,1,0:T(8,128)(2,1)S(1)}, bf16[2,512,128]{2,1,0:T(8,128)(2,1)S(1)}, u32[]{:S(2)}, u32[]{:S(2)}) collective-permute-start(bf16[2,512,128]{2,1,0:T(8,128)(2,1)S(1)} %get-tuple-element.60), channel_id=1, source_target_pairs={{0,4},{2,14},{4,8},{6,2},{8,12},{10,6},{12,0},{14,10},{16,20},{18,... | collective-permute-start | bytes 786440 | tf_op jit(solution)/shard_map/ppermute | solution.py:31
  27.9 9.8 %collective-permute-start.10 = (bf16[2,512,128]{2,1,0:T(8,128)(2,1)S(1)}, bf16[2,512,128]{2,1,0:T(8,128)(2,1)S(1)}, u32[]{:S(2)}, u32[]{:S(2)}) collective-permute-start(bf16[2,512,128]{2,1,0:T(8,128)(2,1)S(1)} %get-tuple-element.61), channel_id=1, source_target_pairs={{0,12},{2,6},{4,0},{6,10},{8,4},{10,14},{12,8},{14,2},{16,28},{18,... | collective-permute-start | bytes 786440 | tf_op jit(solution)/shard_map/ppermute | solution.py:31
  31.7 8.5 %collective-permute-start.7 = (f32[256,512]{1,0:T(8,128)S(1)}, f32[256,512]{1,0:T(8,128)S(1)}, u32[]{:S(2)}, u32[]{:S(2)}) collective-permute-start(f32[256,512]{1,0:T(8,128)S(1)} %slice_bitcast_fusion), channel_id=1, source_target_pairs={{0,2},{2,0},{4,6},{6,4},{8,10},{10,8},{12,14},{14,12},{16,18},{18,... | collective-permute-start | bytes 1572872 | tf_op jit(solution)/shard_map/ppermute | solution.py:42
  37.8 9.2 %collective-permute-start.11 = (bf16[2,512,128]{2,1,0:T(8,128)(2,1)S(1)}, bf16[2,512,128]{2,1,0:T(8,128)(2,1)S(1)}, u32[]{:S(2)}, u32[]{:S(2)}) collective-permute-start(bf16[2,512,128]{2,1,0:T(8,128)(2,1)S(1)} %shard_map.79.mine), channel_id=1, source_target_pairs={{0,1},{1,0},{2,3},{3,2},{4,5},{5,4},{6,7},{7,6},{8,9},{9,8},{10,11... | collective-permute-start | bytes 786440 | tf_op jit(solution)/shard_map/ppermute | solution.py:46

commit v6 on v5

v6 whole, which is shorter than its diff:
```python
import functools
import math

import jax
import jax.numpy as jnp
from jax import lax
from jax.experimental import pallas as pl
from jax.experimental.pallas import tpu as pltpu
from jax.sharding import PartitionSpec as P

HDIM = 128
GROUP = 8
SCALE = 1.0 / math.sqrt(HDIM)
EXP_SCALE = SCALE * math.log2(math.e)
MASKED = -1e30
FLOOR = -1e29
KERNEL_VMEM = 16 * 2**20
KEYS = 512

NT = (((1,), (1,)), ((), ()))
NN = (((1,), (0,)), ((), ()))
TN = (((0,), (0,)), ((), ()))


def dot(a, b, dims):
    return lax.dot_general(a, b, dims, preferred_element_type=jnp.float32)


def chip_shift(array, even, odd):
    n = lax.axis_size("cp")
    pairs = [(i, i - i % GROUP + (i % GROUP + 2 * (odd if i % 2 else even)) % GROUP) for i in range(n)]
    return lax.ppermute(array, "cp", pairs)


def chip_permute(array, even, odd):
    n = lax.axis_size("cp")
    to = [(odd if i % 2 else even)[i % GROUP // 2] for i in range(n)]
    pairs = [(i, i - i % GROUP + 2 * to[i] + i % 2) for i in range(n) if to[i] is not None]
    return lax.ppermute(array, "cp", pairs)


def core_swap(array):
    n = lax.axis_size("cp")
    return lax.ppermute(array, "cp", [(i, i ^ 1) for i in range(n)])


def hd_swap(array):
    return lax.ppermute(array, "hd", [(0, 1), (1, 0)])


def masked_scores(k, q, starts, row_base, key_base, diagonal):
    s = dot(k, q, NT)
    key_pos = key_base + lax.broadcasted_iota(jnp.int32, s.shape, 0)
    allowed = key_pos >= starts
    if diagonal:
        row_pos = row_base + lax.broadcasted_iota(jnp.int32, s.shape, 1)
        allowed = allowed & (key_pos <= row_pos)
    return jnp.where(allowed, s, MASKED)


def slot_distance(slot, cp):
    return slot if slot < 2 else slot + lax.rem(cp, 2) * (5 - 2 * slot)


def stats_kernel(step, slot, groups, pos_ref, *refs):
    if step == 0:
        kv, q_own, g_own, st_own, stats, *copies = refs
        for src, dst in zip((q_own, g_own, st_own), copies):
            dst[...] = src[...]
        rows = ((q_own, g_own, st_own),)
    else:
        stats_in, *refs = refs
        if step == 1:
            own, *refs = refs
        else:
            refs = refs[2:]
        kv, q_own, q_sib, g_own, g_sib, st_own, st_sib, stats, *kept = refs
        rows = ((q_own, g_own, st_own), (q_sib, g_sib, st_sib))
    cp = pos_ref[0]
    in_group = lax.rem(cp, GROUP)
    size = kv.shape[1]
    base = 6 * groups[0]
    if step:
        stats[...] = stats_in[base : base + stats.shape[0], :]
    else:
        for at in range(0, 12, 3):
            stats[at : at + 1, :] = jnp.full((1, size), FLOOR)
            stats[at + 1 : at + 3, :] = jnp.zeros((2, size))
    chips = slot_distance(slot, cp)

    def work(kv, group, chips, keep):
        q, g, st = rows[group]
        key_base = (cp - 2 * chips) * size
        row_base = (cp if group == 0 else cp + 1 - 2 * lax.rem(cp, 2)) * size
        for head in range(2):
            cols = pl.ds(head * HDIM, HDIM)
            at = 3 * (2 * group + head) - base
            for first in range(0, size, KEYS):
                keys = pl.ds(first, KEYS)
                s = masked_scores(kv[0, keys], q[:, cols], st[...], row_base, key_base + first, step == 0)
                dp = dot(kv[1, keys], g[:, cols], NT)
                if keep:
                    kept[0][chips - 1, 2 * group + head, keys] = s
                    kept[1][chips - 1, 2 * group + head, keys] = dp
                m = stats[at : at + 1, :]
                new = jnp.maximum(m, jnp.max(s, axis=0, keepdims=True))
                p = jnp.exp2((s - new) * EXP_SCALE)
                f = jnp.exp2((m - new) * EXP_SCALE)
                stats[at : at + 1, :] = new
                stats[at + 1 : at + 2, :] = stats[at + 1 : at + 2, :] * f + jnp.sum(p, axis=0, keepdims=True)
                stats[at + 2 : at + 3, :] = stats[at + 2 : at + 3, :] * f + jnp.sum(p * dp, axis=0, keepdims=True)

    if step == 0:
        work(kv, 0, 0, False)
    if step == 1:
        pl.when(lax.rem(cp, 2) == 0)(lambda: work(own, 1, 0, False))
    if step:

        @pl.when(in_group >= 2 * chips)
        def _():
            for group in groups:
                work(kv, group, chips, True)


def merged(stats, other, at):
    m, m2 = stats[at : at + 1, :], other[at : at + 1, :]
    top = jnp.maximum(m, m2)
    f, f2 = jnp.exp2((m - top) * EXP_SCALE), jnp.exp2((m2 - top) * EXP_SCALE)
    total = stats[at + 1 : at + 2, :] * f + other[at + 1 : at + 2, :] * f2
    weighted = stats[at + 2 : at + 3, :] * f + other[at + 2 : at + 3, :] * f2
    return top * EXP_SCALE + jnp.log2(total), weighted / total


def stage_distance(stage, cp):
    odd = lax.rem(cp, 2)
    return (2, 1 + 2 * odd, 3 - 2 * odd, 0)[stage]


def add_grads(q, g, s, dp, fin, at, acc, cols):
    p = jnp.exp2(s * EXP_SCALE - fin[at : at + 1, :])
    ds = (p * (dp - fin[at + 1 : at + 2, :])).astype(jnp.bfloat16)
    acc[0] += dot(ds, q[:, cols], NN)
    acc[1] += dot(p.astype(jnp.bfloat16), g[:, cols], NN)
    return ds


def first_kernel(group, pos_ref, *refs):
    if group == 0:
        acc_in, *refs = refs
    stats, other, q, g, kept0, kept1, kept, fin, *refs = refs
    acc = refs[-1]
    for head in range(2):
        log_sum, delta = merged(stats, other, 3 * head)
        fin[2 * head : 2 * head + 1, :] = log_sum
        fin[2 * head + 1 : 2 * head + 2, :] = delta
    acc[...] = acc_in[...] if group == 0 else jnp.zeros_like(acc)
    cp = pos_ref[0]
    chips = stage_distance(0, cp)

    @pl.when(lax.rem(cp, GROUP) >= 2 * chips)
    def _():
        for head in range(2):
            at = 2 * group + head
            cols = pl.ds(head * HDIM, HDIM)
            kept[head] = add_grads(q, g, kept0[chips - 1, at], kept1[chips - 1, at], fin, 2 * head, acc, cols)

    if group == 0:
        refs[0][...] = acc[...].astype(jnp.bfloat16)


def grads_kernel(stage, pos_ref, *refs):
    if stage > 1:
        dq_in, refs = refs[:2], refs[2:]
    (fin_own, fin_sib), refs = refs[:2], refs[2:]
    even, odd, q_own, q_sib, g_own, g_sib, kept0, kept1, *refs = refs
    if stage == 3:
        first_even, first_odd, *first, dq_own, dq_sib, dkv, acc = refs
    else:
        dq_own, dq_sib, dkv, acc = refs
    cp = pos_ref[0]
    in_group = lax.rem(cp, GROUP)
    even_core = lax.rem(cp, 2) == 0
    size = q_own.shape[0]
    acc[...] = jnp.zeros_like(acc)
    for i, dq in enumerate((dq_own, dq_sib)):
        dq[...] = dq_in[i][...] if stage > 1 else jnp.zeros_like(dq)
    chips = stage_distance(stage, cp)
    k = even[0] if stage == 3 else jnp.where(even_core, even[0], odd[0])
    k_t = k.T
    groups = ((q_own, g_own, fin_own, dq_own), (q_sib, g_sib, fin_sib, dq_sib))
    for group, (q, g, fin, dq) in enumerate(groups):

        def work(group=group, q=q, g=g, fin=fin, dq=dq):
            for head in range(2):
                cols = pl.ds(head * HDIM, HDIM)
                if stage < 3:
                    s = kept0[chips - 1, 2 * group + head]
                    dp = kept1[chips - 1, 2 * group + head]
                else:
                    starts = (kept0, kept1)[group][...]
                    s = masked_scores(k, q[:, cols], starts, (cp + group) * size, cp * size, group == 0)
                    dp = dot(even[1], g[:, cols], NT)
                ds = add_grads(q, g, s, dp, fin, 2 * head, acc, cols)
                dq[cols, :] += dot(k_t, ds, NN)

        if stage == 3 and group == 0:
            work()
        elif stage == 3:
            pl.when(even_core)(work)
        else:
            pl.when(in_group >= 2 * chips)(work)
    dkv[...] = acc[...].astype(dkv.dtype)
    if stage == 3:

        @pl.when(in_group >= 2 * stage_distance(0, cp))
        def _():
            first_t = jnp.where(even_core, first_even[0], first_odd[0]).T
            for ds, dq in zip(first, (dq_own, dq_sib)):
                for head in range(2):
                    dq[pl.ds(head * HDIM, HDIM), :] += dot(first_t, ds[head], NN)


def query_kernel(mine, other, out, done):
    done[...] = jnp.zeros_like(done)
    out[...] = ((mine[...] + other[...]) * SCALE).T.astype(out.dtype)


def add_kernel(total, part, out):
    out[...] = (total[...] + part[...].astype(jnp.float32)).astype(out.dtype)


def last_kernel(mine, other, _, grad_keys, grad_values):
    total = mine[...].astype(jnp.float32) + other[...].astype(jnp.float32)
    grad_keys[...] = (total[0] * SCALE).astype(grad_keys.dtype)
    grad_values[...] = total[1].astype(grad_values.dtype)


VM = pl.BlockSpec(memory_space=pltpu.VMEM)
SM = pl.BlockSpec(memory_space=pltpu.SMEM)


BLOCK_COST = pl.CostEstimate(flops=10 * 512 * 512 * 128 // 10, bytes_accessed=2**10, transcendentals=0)
LONG_COST = pl.CostEstimate(flops=40 * 10 * 512 * 512 * 128, bytes_accessed=2**20, transcendentals=0)
NO_COST = pl.CostEstimate(flops=0, bytes_accessed=2**10, transcendentals=0)


def simple(kernel, out, *args, cost=NO_COST):
    return pl.pallas_call(
        kernel,
        out_shape=out,
        in_specs=[VM] * len(args),
        out_specs=jax.tree.map(lambda _: VM, out),
        compiler_params=pltpu.CompilerParams(vmem_limit_bytes=8 * 2**20),
        cost_estimate=cost,
    )(*args)


def call_stats(step, slot, cp, before, kv, rows, groups=(0, 1)):
    size = kv.shape[1]
    out = [jax.ShapeDtypeStruct((6 * len(groups), size), jnp.float32)]
    if step:
        out += [jax.ShapeDtypeStruct((3, 4, size, size), jnp.float32)] * 2
    else:
        out += [jax.ShapeDtypeStruct(a.shape, a.dtype) for a in rows]
    in_specs = [SM] + [VM] * (len(before) + 1 + len(rows))
    if step > 1:
        in_specs[2:4] = [pl.BlockSpec(memory_space=pl.ANY)] * 2
    return pl.pallas_call(
        functools.partial(stats_kernel, step, slot, groups),
        out_shape=out,
        in_specs=in_specs,
        out_specs=[VM] * len(out),
        input_output_aliases={2: 1, 3: 2} if step > 1 else {},
        compiler_params=pltpu.CompilerParams(vmem_limit_bytes=KERNEL_VMEM),
        cost_estimate=NO_COST,
        name="stats",
    )(cp, *before, kv, *rows)


def call_grads(kernel, cp, out, args, cost, scratch=()):
    return pl.pallas_call(
        kernel,
        out_shape=out,
        in_specs=[SM] + [VM] * len(args),
        out_specs=[VM] * len(out),
        scratch_shapes=scratch,
        compiler_params=pltpu.CompilerParams(vmem_limit_bytes=KERNEL_VMEM),
        cost_estimate=cost,
        name="grads",
    )(cp, *args)


def call_first(group, cp, before, rows, kept):
    size = rows[0].shape[0]
    total = (2, size, HDIM)
    out = [jax.ShapeDtypeStruct((2, size, size), jnp.bfloat16), jax.ShapeDtypeStruct((4, size), jnp.float32)]
    out.append(jax.ShapeDtypeStruct(total, jnp.float32 if group else jnp.bfloat16))
    scratch = [] if group else [pltpu.VMEM(total, jnp.float32)]
    args = (*before, rows[group], rows[2 + group], *kept)
    return call_grads(functools.partial(first_kernel, group), cp, out, args, NO_COST if group else BLOCK_COST, scratch)


def call_stage(stage, cp, dq, fin, blocks, rows, kept):
    size = rows[0].shape[0]
    total = (2, size, HDIM)
    out = [jax.ShapeDtypeStruct((2 * HDIM, size), jnp.float32)] * 2
    out.append(jax.ShapeDtypeStruct(total, jnp.float32 if stage == 3 else jnp.bfloat16))
    args = (*dq, *fin, *blocks, *rows[:4], *kept)
    cost = NO_COST if stage == 3 else BLOCK_COST
    *dq, part = call_grads(functools.partial(grads_kernel, stage), cp, out, args, cost, [pltpu.VMEM(total, jnp.float32)])
    return dq, part


def body(query, keys, values, grad_out, doc_start):
    size = query.shape[0]
    position = lax.axis_index("cp").astype(jnp.int32)
    cp = position.reshape(1)
    kv = jnp.where(lax.broadcasted_iota(jnp.int32, (2, *keys.shape), 0) == 0, keys[None], values[None])
    slot1 = chip_shift(kv, 1, 1)
    slot2 = chip_permute(kv, (2, 3, 0, 1), (3, 0, 1, 2))
    slot3 = chip_permute(kv, (3, 0, 1, 2), (2, 3, 0, 1))
    starts = doc_start.reshape(1, size)
    kv, near_query, near_grad = lax.optimization_barrier((kv, query, grad_out))
    far_query, near_starts = lax.optimization_barrier((core_swap(near_query), starts))
    far_grad, far_starts = core_swap(near_grad), core_swap(near_starts)

    stats, *own_rows = call_stats(0, 0, cp, (), kv, (query, grad_out, starts))
    rows = (own_rows[0], far_query, own_rows[1], far_grad, own_rows[2], far_starts)
    before = call_stats(1, 1, cp, (stats, kv), slot1, rows)
    before = call_stats(2, 2, cp, before, slot2, rows)
    stats = before[0]
    near, *kept = call_stats(3, 3, cp, before, slot3, rows, (0,))
    far_other = core_swap(near)
    far, *kept = call_stats(3, 3, cp, (stats, *kept), slot3, rows, (1,))
    near_other = core_swap(far)

    ds_far, fin_far, part = call_first(1, cp, (far, far_other), rows, kept)
    ds_near, fin_near, part = call_first(0, cp, (part, near, near_other), rows, kept)
    back_a = chip_permute(part, (3, 2, 0, 1), (3, 2, 0, 1))
    fin = (fin_near, fin_far)
    dq, part = call_stage(1, cp, (), fin, (slot1, slot2), rows, kept)
    back_b = chip_permute(part, (None, 0, 1, 2), (1, 2, 3, 0))
    dq, part = call_stage(2, cp, dq, fin, (slot3, slot1), rows, kept)
    back_c = chip_permute(part, (1, 2, 3, 0), (None, 0, 1, 2))
    dq, own = call_stage(3, cp, dq, fin, (kv, kv), rows, (*rows[4:], slot2, slot3, ds_near, ds_far))

    dq_other = core_swap(dq[1])
    token = jax.ShapeDtypeStruct((8, HDIM), jnp.float32)
    grad_query, done = simple(query_kernel, [jax.ShapeDtypeStruct(query.shape, query.dtype), token], dq[0], dq_other)
    total = jax.ShapeDtypeStruct(own.shape, own.dtype)
    half = simple(add_kernel, total, own, back_a, cost=BLOCK_COST)
    half = simple(add_kernel, total, half, back_b, cost=LONG_COST)
    half = simple(add_kernel, jax.ShapeDtypeStruct(kv.shape, kv.dtype), half, back_c)
    other = hd_swap(half)
    near = jax.ShapeDtypeStruct(keys.shape, keys.dtype)
    grad_keys, grad_values = simple(last_kernel, [near] * 2, half, other, done)
    return grad_query, grad_keys, grad_values


def solution(mesh):
    in_specs = (P("cp", "hd"), P("cp", None), P("cp", None), P("cp", "hd"), P("cp"))
    out_specs = (P("cp", "hd"), P("cp", None), P("cp", None))
    return jax.shard_map(body, mesh=mesh, in_specs=in_specs, out_specs=out_specs, check_vma=False)
```

time: 48 us -> 47.2 us (0.983)
  the two profiles are of different devices: /device:TPU:14 before, /device:TPU:0 now
where the time goes in v6:
time: 47.2 us; the launch traced here: 47 us
  starting transfers between devices  20.9 us (44%)
  waiting for transfers between devices  13.9 us (29%)
  Pallas kernels  7.74 us (16%)
  local copies, waits for them, and re-layouts  2.58 us (5%)
  other arithmetic  1.07 us (2%)
  between operations  0.79 us (2%)
    ppermute x5, starting transfers between devices, chip_permute(): return lax.ppermute(array, 'cp', pairs)  14.8 us
    ppermute x5, waiting for transfers between devices, chip_permute(): return lax.ppermute(array, 'cp', pairs)  8.17 us
    ppermute x1, waiting for transfers between devices, hd_swap(): return lax.ppermute(array, 'hd', [(0, 1), (1, 0)])  4.94 us
    pallas_call x5, Pallas kernels, call_grads(): pl.pallas_call(kernel, out_shape=out, in_specs=[SM] + [VM] * len(args), o...  3.89 us
    ppermute x1, starting transfers between devices, hd_swap(): return lax.ppermute(array, 'hd', [(0, 1), (1, 0)])  3.28 us
    unnamed x6, local copies, waits for them, and re-layouts  2.58 us
    pallas_call x5, Pallas kernels, call_stats(): pl.pallas_call(functools.partial(stats_kernel, step, slot, groups), out_s...  2.11 us
    pallas_call x5, Pallas kernels, simple(): pl.pallas_call(kernel, out_shape=out, in_specs=[VM] * len(args), out_spec...  1.74 us
  transfers between devices with their start and end apart: 13, of which 6 were waited for; matrix products, arithmetic and copies ran while one was open for 0% of the time, Pallas kernels for 15%

profile of v6, /device:TPU:0, one launch (start us, length us, event | category | flops | bytes accessed | tf_op | source)
XLA Modules:
  0.0 47.0 jit_solution(2932905415335397387)
XLA Ops:
  0.6 1.1 %broadcast_select_fusion.refs_0_.refs_1_.refs_4_.refs_5_ = bf16[2,512,128]{2,1,0:T(8,128)(2,1)S(1)} fusion(pred[2]{0:T(512)(128)(4,1)S(1)} %iota_compare_fusion, bf16[512,128]{1,0:T(8,128)(2,1)} %param.7, bf16[512,128]{1,0:T(8,128)(2,1)} %param.6), kind=kLoop, calls=%fused_computation | loop fusion | flops 131072 | bytes 524290 | tf_op jit(solution)/shard_map/jit(_where)/select_n | solution.py:318
  1.7 0.1 collective-permute-start.1
  1.8 0.5 %collective-permute-start.2 = (bf16[512,256]{1,0:T(8,128)(2,1)}, bf16[512,256]{1,0:T(8,128)(2,1)S(1)}, u32[]{:S(2)}, u32[]{:S(2)}) collective-permute-start(bf16[512,256]{1,0:T(8,128)(2,1)} %refs_2_.1), channel_id=1, source_target_pairs={{0,2},{2,0},{4,6},{6,4},{8,10},{10,8},{12,14},{14,12},{16,18},{18,... | collective-permute-start | bytes 786440 | tf_op jit(solution)/shard_map/ppermute | solution.py:44
  2.3 1.6 %collective-permute-start = (bf16[2,512,128]{2,1,0:T(8,128)(2,1)S(1)}, bf16[2,512,128]{2,1,0:T(8,128)(2,1)S(1)}, u32[]{:S(2)}, u32[]{:S(2)}) collective-permute-start(bf16[2,512,128]{2,1,0:T(8,128)(2,1)S(1)} %broadcast_select_fusion.refs_0_.refs_1_.refs_4_.refs_5_), channel_id=1, source_target_pairs={{0,4},{2,6},{4,8},{6,10},{8,12},{10,14},{12,0},{14,2},{16,20},{18,... | collective-permute-start | bytes 786440 | tf_op jit(solution)/shard_map/ppermute | solution.py:32
  3.9 2.7 %collective-permute-start.4 = (bf16[2,512,128]{2,1,0:T(8,128)(2,1)S(1)}, bf16[2,512,128]{2,1,0:T(8,128)(2,1)S(1)}, u32[]{:S(2)}, u32[]{:S(2)}) collective-permute-start(bf16[2,512,128]{2,1,0:T(8,128)(2,1)S(1)} %broadcast_select_fusion.refs_0_.refs_1_.refs_4_.refs_5_), channel_id=1, source_target_pairs={{0,8},{2,14},{4,12},{6,2},{8,0},{10,6},{12,4},{14,10},{16,24},{18,... | collective-permute-start | bytes 786440 | tf_op jit(solution)/shard_map/ppermute | solution.py:39
  6.6 1.4 %collective-permute-start.5 = (bf16[2,512,128]{2,1,0:T(8,128)(2,1)S(1)}, bf16[2,512,128]{2,1,0:T(8,128)(2,1)S(1)}, u32[]{:S(2)}, u32[]{:S(2)}) collective-permute-start(bf16[2,512,128]{2,1,0:T(8,128)(2,1)S(1)} %broadcast_select_fusion.refs_0_.refs_1_.refs_4_.refs_5_), channel_id=1, source_target_pairs={{0,12},{2,10},{4,0},{6,14},{8,4},{10,2},{12,8},{14,6},{16,28},{18,... | collective-permute-start | bytes 786440 | tf_op jit(solution)/shard_map/ppermute | solution.py:39
  8.0 0.0 collective-permute-done.1.refs_4_.refs_5_.refs_2_.refs_7_
  8.0 0.0 collective-permute-start.3
  8.0 0.0 copy-start
  8.0 0.9 %copy-done = bf16[512,256]{1,0:T(8,128)(2,1)S(1)} copy-done((bf16[512,256]{1,0:T(8,128)(2,1)S(1)}, bf16[512,256]{1,0:T(8,128)(2,1)}, u32[]{:S(2)}) %copy-start) | copy-done | bytes 262168
  9.0 0.0 copy-start.1
  9.0 0.9 %copy-done.1 = bf16[512,256]{1,0:T(8,128)(2,1)S(1)} copy-done((bf16[512,256]{1,0:T(8,128)(2,1)S(1)}, bf16[512,256]{1,0:T(8,128)(2,1)}, u32[]{:S(2)}) %copy-start.1) | copy-done | bytes 262168
  9.9 0.0 copy-start.2
  9.9 0.7 %copy-done.2 = s32[512]{0:T(512)S(1)} copy-done((s32[512]{0:T(512)S(1)}, s32[512]{0:T(512)}, u32[]{:S(2)}) %copy-start.2) | copy-done | bytes 2072
  10.6 1.2 %stats.5 = (f32[12,512]{1,0:T(8,128)S(1)}, bf16[512,256]{1,0:T(8,128)(2,1)S(1)}, bf16[512,256]{1,0:T(8,128)(2,1)S(1)}, s32[1,512]{1,0:T(1,128)S(1)}) custom-call(s32[1]{0:T(128)} %bitcast.pos_ref, bf16[2,512,128]{2,1,0:T(8,128)(2,1)S(1)} %broadcast_select_fusion.refs_0_.refs_1_.refs_4_.refs_5_, bf16[512,256]{1,0:T(8,128)(2,1)S(1)} %copy-done, ...), custom_call_target="tpu_custom_call" | custom-call | bytes 1024 | tf_op jit(solution)/shard_map/stats/pallas_call | solution.py:268
  11.8 0.0 collective-permute-done.2.refs_6_.refs_7_.refs_3_.refs_9_
  11.8 0.0 collective-permute-done.refs_2_.refs_5_
  11.8 0.0 collective-permute-done.3.refs_8_.refs_9_.refs_11_
  11.8 0.9 %stats.6 = (f32[12,512]{1,0:T(8,128)S(1)}, f32[3,4,512,512]{3,2,1,0:T(8,128)S(1)}, f32[3,4,512,512]{3,2,1,0:T(8,128)S(1)}) custom-call(s32[1]{0:T(128)} %bitcast.pos_ref, f32[12,512]{1,0:T(8,128)S(1)} %get-tuple-element.44.refs_0_, bf16[2,512,128]{2,1,0:T(8,128)(2,1)S(1)} %broadcast_select_fusion.refs_0_.refs_1_.refs_4_.refs_5_, ...), custom_call_target="tpu_custom_call" | custom-call | bytes 1024 | tf_op jit(solution)/shard_map/stats/pallas_call | solution.py:268
  12.8 5.7 %collective-permute-done.4.refs_3_.refs_12_ = bf16[2,512,128]{2,1,0:T(8,128)(2,1)S(1)} collective-permute-done((bf16[2,512,128]{2,1,0:T(8,128)(2,1)S(1)}, bf16[2,512,128]{2,1,0:T(8,128)(2,1)S(1)}, u32[]{:S(2)}, u32[]{:S(2)}) %collective-permute-start.4) | collective-permute-done | bytes 262176 | tf_op jit(solution)/shard_map/ppermute | solution.py:39
  18.5 0.0 collective-permute-done.5.refs_3_.refs_4_.refs_13_
  18.5 0.1 collective-permute-start.6
  18.6 0.5 %collective-permute-start.7 = (f32[6,512]{1,0:T(8,128)S(1)}, f32[6,512]{1,0:T(8,128)S(1)}, u32[]{:S(2)}, u32[]{:S(2)}) collective-permute-start(f32[6,512]{1,0:T(8,128)S(1)} %get-tuple-element.60.refs_0_), channel_id=1, source_target_pairs={{0,2},{2,0},{4,6},{6,4},{8,10},{10,8},{12,14},{14,12},{16,18},{18,... | collective-permute-start | bytes 36872 | tf_op jit(solution)/shard_map/ppermute | solution.py:44
  19.1 0.7 %collective-permute-done.6.refs_1_ = f32[6,512]{1,0:T(8,128)S(1)} collective-permute-done((f32[6,512]{1,0:T(8,128)S(1)}, f32[6,512]{1,0:T(8,128)S(1)}, u32[]{:S(2)}, u32[]{:S(2)}) %collective-permute-start.6) | collective-permute-done | bytes 12320 | tf_op jit(solution)/shard_map/ppermute | solution.py:44
  19.8 0.1 collective-permute-done.7.refs_2_
  20.0 0.1 grads.6
  20.0 4.8 %collective-permute-start.9 = (bf16[2,512,128]{2,1,0:T(8,128)(2,1)S(1)}, bf16[2,512,128]{2,1,0:T(8,128)(2,1)S(1)}, u32[]{:S(2)}, u32[]{:S(2)}) collective-permute-start(bf16[2,512,128]{2,1,0:T(8,128)(2,1)S(1)} %get-tuple-element.77), channel_id=1, source_target_pairs={{0,12},{2,14},{4,8},{6,10},{8,0},{10,2},{12,4},{14,6},{16,28},{18,... | collective-permute-start | bytes 786440 | tf_op jit(solution)/shard_map/ppermute | solution.py:39
  24.8 0.3 grads.7
  25.1 1.3 %collective-permute-start.10 = (bf16[2,512,128]{2,1,0:T(8,128)(2,1)S(1)}, bf16[2,512,128]{2,1,0:T(8,128)(2,1)S(1)}, u32[]{:S(2)}, u32[]{:S(2)}) collective-permute-start(bf16[2,512,128]{2,1,0:T(8,128)(2,1)S(1)} %get-tuple-element.78), channel_id=1, source_target_pairs={{2,6},{4,0},{6,10},{8,4},{10,14},{12,8},{14,2},{18,22},{20,16},{22... | collective-permute-start | bytes 786440 | tf_op jit(solution)/shard_map/ppermute | solution.py:39
  26.4 0.2 grads.8
  26.6 4.6 %collective-permute-start.11 = (bf16[2,512,128]{2,1,0:T(8,128)(2,1)S(1)}, bf16[2,512,128]{2,1,0:T(8,128)(2,1)S(1)}, u32[]{:S(2)}, u32[]{:S(2)}) collective-permute-start(bf16[2,512,128]{2,1,0:T(8,128)(2,1)S(1)} %get-tuple-element.79), channel_id=1, source_target_pairs={{0,4},{4,8},{6,2},{8,12},{10,6},{12,0},{14,10},{16,20},{20,24},{22... | collective-permute-start | bytes 786440 | tf_op jit(solution)/shard_map/ppermute | solution.py:39
  31.2 3.3 %grads.9 = (f32[256,512]{1,0:T(8,128)S(1)}, f32[256,512]{1,0:T(8,128)S(1)}, f32[2,512,128]{2,1,0:T(8,128)S(1)}) custom-call(s32[1]{0:T(128)} %bitcast.pos_ref, f32[256,512]{1,0:T(8,128)S(1)} %get-tuple-element.69.refs_0_, f32[256,512]{1,0:T(8,128)S(1)} %get-tuple-element.70.refs_1_, f32[4,512]{1,0:T(4,128)S(1)} %get-tuple-element.65.refs_0_.refs_2_, ...), custom_call_target="tpu_custom_call" | custom-call | bytes 1024 | tf_op jit(solution)/shard_map/grads/pallas_call | solution.py:281
  34.5 0.1 collective-permute-start.8
  34.6 0.0 collective-permute-done.9.part
  34.6 0.4 collective-permute-done.10.part
  35.1 2.0 %collective-permute-done.11.part = bf16[2,512,128]{2,1,0:T(8,128)(2,1)S(1)} collective-permute-done((bf16[2,512,128]{2,1,0:T(8,128)(2,1)S(1)}, bf16[2,512,128]{2,1,0:T(8,128)(2,1)S(1)}, u32[]{:S(2)}, u32[]{:S(2)}) %collective-permute-start.11) | collective-permute-done | bytes 262176 | tf_op jit(solution)/shard_map/ppermute | solution.py:39
  37.1 0.1 shard_map.79.mine
  37.2 3.3 %collective-permute-start.12 = (bf16[2,512,128]{2,1,0:T(8,128)(2,1)S(1)}, bf16[2,512,128]{2,1,0:T(8,128)(2,1)S(1)}, u32[]{:S(2)}, u32[]{:S(2)}) collective-permute-start(bf16[2,512,128]{2,1,0:T(8,128)(2,1)S(1)} %shard_map.79.mine), channel_id=1, source_target_pairs={{0,1},{1,0},{2,3},{3,2},{4,5},{5,4},{6,7},{7,6},{8,9},{9,8},{10,11... | collective-permute-start | bytes 786440 | tf_op jit(solution)/shard_map/ppermute | solution.py:48
  40.4 0.0 collective-permute-done.8.other
  40.4 0.8 %shard_map.76 = (bf16[512,256]{1,0:T(8,128)(2,1)}, f32[8,128]{1,0:T(8,128)S(1)}) custom-call(f32[256,512]{1,0:T(8,128)S(1)} %get-tuple-element.73.mine, f32[256,512]{1,0:T(8,128)S(1)} %collective-permute-done.8.other), custom_call_target="tpu_custom_call" | custom-call | bytes 1024 | tf_op jit(solution)/shard_map/pallas_call | solution.py:248
  41.3 4.9 %collective-permute-done.12.other = bf16[2,512,128]{2,1,0:T(8,128)(2,1)S(1)} collective-permute-done((bf16[2,512,128]{2,1,0:T(8,128)(2,1)S(1)}, bf16[2,512,128]{2,1,0:T(8,128)(2,1)S(1)}, u32[]{:S(2)}, u32[]{:S(2)}) %collective-permute-start.12) | collective-permute-done | bytes 262176 | tf_op jit(solution)/shard_map/ppermute | solution.py:48
  46.2 0.7 %shard_map.80 = (bf16[512,128]{1,0:T(8,128)(2,1)}, bf16[512,128]{1,0:T(8,128)(2,1)}) custom-call(bf16[2,512,128]{2,1,0:T(8,128)(2,1)S(1)} %shard_map.79.mine, bf16[2,512,128]{2,1,0:T(8,128)(2,1)S(1)} %collective-permute-done.12.other, f32[8,128]{1,0:T(8,128)S(1)} %get-tuple-element.80._), custom_call_target="tpu_custom_call" | custom-call | bytes 1024 | tf_op jit(solution)/shard_map/pallas_call | solution.py:248
  (7 shorter events, 0.2 us)
Async XLA Ops:
  1.7 6.3 %collective-permute-start.1 = (bf16[512,256]{1,0:T(8,128)(2,1)}, bf16[512,256]{1,0:T(8,128)(2,1)S(1)}, u32[]{:S(2)}, u32[]{:S(2)}) collective-permute-start(bf16[512,256]{1,0:T(8,128)(2,1)} %refs_1_.1), channel_id=1, source_target_pairs={{0,2},{2,0},{4,6},{6,4},{8,10},{10,8},{12,14},{14,12},{16,18},{18,... | collective-permute-start | bytes 786440 | tf_op jit(solution)/shard_map/ppermute | solution.py:44
  1.8 10.0 %collective-permute-start.2 = (bf16[512,256]{1,0:T(8,128)(2,1)}, bf16[512,256]{1,0:T(8,128)(2,1)S(1)}, u32[]{:S(2)}, u32[]{:S(2)}) collective-permute-start(bf16[512,256]{1,0:T(8,128)(2,1)} %refs_2_.1), channel_id=1, source_target_pairs={{0,2},{2,0},{4,6},{6,4},{8,10},{10,8},{12,14},{14,12},{16,18},{18,... | collective-permute-start | bytes 786440 | tf_op jit(solution)/shard_map/ppermute | solution.py:44
  2.3 9.5 %collective-permute-start = (bf16[2,512,128]{2,1,0:T(8,128)(2,1)S(1)}, bf16[2,512,128]{2,1,0:T(8,128)(2,1)S(1)}, u32[]{:S(2)}, u32[]{:S(2)}) collective-permute-start(bf16[2,512,128]{2,1,0:T(8,128)(2,1)S(1)} %broadcast_select_fusion.refs_0_.refs_1_.refs_4_.refs_5_), channel_id=1, source_target_pairs={{0,4},{2,6},{4,8},{6,10},{8,12},{10,14},{12,0},{14,2},{16,20},{18,... | collective-permute-start | bytes 786440 | tf_op jit(solution)/shard_map/ppermute | solution.py:32
  3.9 14.6 %collective-permute-start.4 = (bf16[2,512,128]{2,1,0:T(8,128)(2,1)S(1)}, bf16[2,512,128]{2,1,0:T(8,128)(2,1)S(1)}, u32[]{:S(2)}, u32[]{:S(2)}) collective-permute-start(bf16[2,512,128]{2,1,0:T(8,128)(2,1)S(1)} %broadcast_select_fusion.refs_0_.refs_1_.refs_4_.refs_5_), channel_id=1, source_target_pairs={{0,8},{2,14},{4,12},{6,2},{8,0},{10,6},{12,4},{14,10},{16,24},{18,... | collective-permute-start | bytes 786440 | tf_op jit(solution)/shard_map/ppermute | solution.py:39
  6.6 11.9 %collective-permute-start.5 = (bf16[2,512,128]{2,1,0:T(8,128)(2,1)S(1)}, bf16[2,512,128]{2,1,0:T(8,128)(2,1)S(1)}, u32[]{:S(2)}, u32[]{:S(2)}) collective-permute-start(bf16[2,512,128]{2,1,0:T(8,128)(2,1)S(1)} %broadcast_select_fusion.refs_0_.refs_1_.refs_4_.refs_5_), channel_id=1, source_target_pairs={{0,12},{2,10},{4,0},{6,14},{8,4},{10,2},{12,8},{14,6},{16,28},{18,... | collective-permute-start | bytes 786440 | tf_op jit(solution)/shard_map/ppermute | solution.py:39
  8.0 3.8 %collective-permute-start.3 = (s32[1,512]{1,0:T(1,128)}, s32[1,512]{1,0:T(1,128)S(1)}, u32[]{:S(2)}, u32[]{:S(2)}) collective-permute-start(s32[1,512]{1,0:T(1,128)} %bitcast.2), channel_id=1, source_target_pairs={{0,2},{2,0},{4,6},{6,4},{8,10},{10,8},{12,14},{14,12},{16,18},{18,... | collective-permute-start | bytes 6152 | tf_op jit(solution)/shard_map/ppermute | solution.py:44
  8.0 1.0 %copy-start = (bf16[512,256]{1,0:T(8,128)(2,1)S(1)}, bf16[512,256]{1,0:T(8,128)(2,1)}, u32[]{:S(2)}) copy-start(bf16[512,256]{1,0:T(8,128)(2,1)} %refs_1_.1) | copy-start | bytes 786436
  9.0 0.9 %copy-start.1 = (bf16[512,256]{1,0:T(8,128)(2,1)S(1)}, bf16[512,256]{1,0:T(8,128)(2,1)}, u32[]{:S(2)}) copy-start(bf16[512,256]{1,0:T(8,128)(2,1)} %refs_2_.1) | copy-start | bytes 786436
  9.9 0.7 %copy-start.2 = (s32[512]{0:T(512)S(1)}, s32[512]{0:T(512)}, u32[]{:S(2)}) copy-start(s32[512]{0:T(512)} %param.9) | copy-start | bytes 6148
  18.5 1.3 %collective-permute-start.6 = (f32[6,512]{1,0:T(8,128)S(1)}, f32[6,512]{1,0:T(8,128)S(1)}, u32[]{:S(2)}, u32[]{:S(2)}) collective-permute-start(f32[6,512]{1,0:T(8,128)S(1)} %get-tuple-element.61.refs_1_), channel_id=1, source_target_pairs={{0,2},{2,0},{4,6},{6,4},{8,10},{10,8},{12,14},{14,12},{16,18},{18,... | collective-permute-start | bytes 36872 | tf_op jit(solution)/shard_map/ppermute | solution.py:44
  18.6 1.3 %collective-permute-start.7 = (f32[6,512]{1,0:T(8,128)S(1)}, f32[6,512]{1,0:T(8,128)S(1)}, u32[]{:S(2)}, u32[]{:S(2)}) collective-permute-start(f32[6,512]{1,0:T(8,128)S(1)} %get-tuple-element.60.refs_0_), channel_id=1, source_target_pairs={{0,2},{2,0},{4,6},{6,4},{8,10},{10,8},{12,14},{14,12},{16,18},{18,... | collective-permute-start | bytes 36872 | tf_op jit(solution)/shard_map/ppermute | solution.py:44
  20.0 14.5 %collective-permute-start.9 = (bf16[2,512,128]{2,1,0:T(8,128)(2,1)S(1)}, bf16[2,512,128]{2,1,0:T(8,128)(2,1)S(1)}, u32[]{:S(2)}, u32[]{:S(2)}) collective-permute-start(bf16[2,512,128]{2,1,0:T(8,128)(2,1)S(1)} %get-tuple-element.77), channel_id=1, source_target_pairs={{0,12},{2,14},{4,8},{6,10},{8,0},{10,2},{12,4},{14,6},{16,28},{18,... | collective-permute-start | bytes 786440 | tf_op jit(solution)/shard_map/ppermute | solution.py:39
  25.1 9.9 %collective-permute-start.10 = (bf16[2,512,128]{2,1,0:T(8,128)(2,1)S(1)}, bf16[2,512,128]{2,1,0:T(8,128)(2,1)S(1)}, u32[]{:S(2)}, u32[]{:S(2)}) collective-permute-start(bf16[2,512,128]{2,1,0:T(8,128)(2,1)S(1)} %get-tuple-element.78), channel_id=1, source_target_pairs={{2,6},{4,0},{6,10},{8,4},{10,14},{12,8},{14,2},{18,22},{20,16},{22... | collective-permute-start | bytes 786440 | tf_op jit(solution)/shard_map/ppermute | solution.py:39
  26.6 10.5 %collective-permute-start.11 = (bf16[2,512,128]{2,1,0:T(8,128)(2,1)S(1)}, bf16[2,512,128]{2,1,0:T(8,128)(2,1)S(1)}, u32[]{:S(2)}, u32[]{:S(2)}) collective-permute-start(bf16[2,512,128]{2,1,0:T(8,128)(2,1)S(1)} %get-tuple-element.79), channel_id=1, source_target_pairs={{0,4},{4,8},{6,2},{8,12},{10,6},{12,0},{14,10},{16,20},{20,24},{22... | collective-permute-start | bytes 786440 | tf_op jit(solution)/shard_map/ppermute | solution.py:39
  34.5 6.0 %collective-permute-start.8 = (f32[256,512]{1,0:T(8,128)S(1)}, f32[256,512]{1,0:T(8,128)S(1)}, u32[]{:S(2)}, u32[]{:S(2)}) collective-permute-start(f32[256,512]{1,0:T(8,128)S(1)} %get-tuple-element.74), channel_id=1, source_target_pairs={{0,2},{2,0},{4,6},{6,4},{8,10},{10,8},{12,14},{14,12},{16,18},{18,... | collective-permute-start | bytes 1572872 | tf_op jit(solution)/shard_map/ppermute | solution.py:44
  37.2 9.1 %collective-permute-start.12 = (bf16[2,512,128]{2,1,0:T(8,128)(2,1)S(1)}, bf16[2,512,128]{2,1,0:T(8,128)(2,1)S(1)}, u32[]{:S(2)}, u32[]{:S(2)}) collective-permute-start(bf16[2,512,128]{2,1,0:T(8,128)(2,1)S(1)} %shard_map.79.mine), channel_id=1, source_target_pairs={{0,1},{1,0},{2,3},{3,2},{4,5},{5,4},{6,7},{7,6},{8,9},{9,8},{10,11... | collective-permute-start | bytes 786440 | tf_op jit(solution)/shard_map/ppermute | solution.py:48

commit v7 on v6

--- a/solution.py
+++ b/solution.py
@@ -317,8 +317,8 @@
     cp = position.reshape(1)
     kv = jnp.where(lax.broadcasted_iota(jnp.int32, (2, *keys.shape), 0) == 0, keys[None], values[None])
     slot1 = chip_shift(kv, 1, 1)
-    slot2 = chip_permute(kv, (2, 3, 0, 1), (3, 0, 1, 2))
-    slot3 = chip_permute(kv, (3, 0, 1, 2), (2, 3, 0, 1))
+    slot2 = chip_permute(kv, (2, 3, 1, 0), (3, 0, 1, 2))
+    slot3 = chip_permute(kv, (3, 0, 1, 2), (2, 3, 1, 0))
     starts = doc_start.reshape(1, size)
     kv, near_query, near_grad = lax.optimization_barrier((kv, query, grad_out))
     far_query, near_starts = lax.optimization_barrier((core_swap(near_query), starts))

time: 47.2 us -> 47.2 us (level)
    ppermute x5, waiting for transfers between devices: 8.17 us -> 6.39 us  [chip_permute(): return lax.ppermute(array, 'cp', pairs)]
    ppermute x1, waiting for transfers between devices: 0.01 us -> 1.79 us  [chip_shift(): return lax.ppermute(array, 'cp', pairs)]
  transfers between devices with their start and end apart: 13 -> 13, of which waited for: 6 -> 8; matrix products, arithmetic and copies ran while one was open for 0% -> 0% of each run, Pallas kernels for 15% -> 15%
where the time goes in v7:
time: 47.2 us; the launch traced here: 47 us
  starting transfers between devices  20.9 us (44%)
  waiting for transfers between devices  13.9 us (29%)
  Pallas kernels  7.72 us (16%)
  local copies, waits for them, and re-layouts  2.58 us (5%)
  other arithmetic  1.07 us (2%)
  between operations  0.77 us (2%)
    ppermute x5, starting transfers between devices, chip_permute(): return lax.ppermute(array, 'cp', pairs)  14.9 us
    ppermute x5, waiting for transfers between devices, chip_permute(): return lax.ppermute(array, 'cp', pairs)  6.39 us
    ppermute x1, waiting for transfers between devices, hd_swap(): return lax.ppermute(array, 'hd', [(0, 1), (1, 0)])  4.94 us
    pallas_call x5, Pallas kernels, call_grads(): pl.pallas_call(kernel, out_shape=out, in_specs=[SM] + [VM] * len(args), o...  3.89 us
    ppermute x1, starting transfers between devices, hd_swap(): return lax.ppermute(array, 'hd', [(0, 1), (1, 0)])  3.28 us
    unnamed x6, local copies, waits for them, and re-layouts  2.58 us
    pallas_call x5, Pallas kernels, call_stats(): pl.pallas_call(functools.partial(stats_kernel, step, slot, groups), out_s...  2.09 us
    ppermute x1, waiting for transfers between devices, chip_shift(): return lax.ppermute(array, 'cp', pairs)  1.79 us
  transfers between devices with their start and end apart: 13, of which 8 were waited for; matrix products, arithmetic and copies ran while one was open for 0% of the time, Pallas kernels for 15%

profile of v7, /device:TPU:0, one launch (start us, length us, event | category | flops | bytes accessed | tf_op | source)
XLA Modules:
  0.0 47.0 jit_solution(4735285093229590875)
XLA Ops:
  0.6 1.1 %broadcast_select_fusion.refs_0_.refs_1_.refs_4_.refs_5_ = bf16[2,512,128]{2,1,0:T(8,128)(2,1)S(1)} fusion(pred[2]{0:T(512)(128)(4,1)S(1)} %iota_compare_fusion, bf16[512,128]{1,0:T(8,128)(2,1)} %param.7, bf16[512,128]{1,0:T(8,128)(2,1)} %param.6), kind=kLoop, calls=%fused_computation | loop fusion | flops 131072 | bytes 524290 | tf_op jit(solution)/shard_map/jit(_where)/select_n | solution.py:318
  1.7 0.1 collective-permute-start.1
  1.8 0.5 %collective-permute-start.2 = (bf16[512,256]{1,0:T(8,128)(2,1)}, bf16[512,256]{1,0:T(8,128)(2,1)S(1)}, u32[]{:S(2)}, u32[]{:S(2)}) collective-permute-start(bf16[512,256]{1,0:T(8,128)(2,1)} %refs_2_.1), channel_id=1, source_target_pairs={{0,2},{2,0},{4,6},{6,4},{8,10},{10,8},{12,14},{14,12},{16,18},{18,... | collective-permute-start | bytes 786440 | tf_op jit(solution)/shard_map/ppermute | solution.py:44
  2.3 1.6 %collective-permute-start = (bf16[2,512,128]{2,1,0:T(8,128)(2,1)S(1)}, bf16[2,512,128]{2,1,0:T(8,128)(2,1)S(1)}, u32[]{:S(2)}, u32[]{:S(2)}) collective-permute-start(bf16[2,512,128]{2,1,0:T(8,128)(2,1)S(1)} %broadcast_select_fusion.refs_0_.refs_1_.refs_4_.refs_5_), channel_id=1, source_target_pairs={{0,4},{2,6},{4,8},{6,10},{8,12},{10,14},{12,0},{14,2},{16,20},{18,... | collective-permute-start | bytes 786440 | tf_op jit(solution)/shard_map/ppermute | solution.py:32
  3.9 2.7 %collective-permute-start.4 = (bf16[2,512,128]{2,1,0:T(8,128)(2,1)S(1)}, bf16[2,512,128]{2,1,0:T(8,128)(2,1)S(1)}, u32[]{:S(2)}, u32[]{:S(2)}) collective-permute-start(bf16[2,512,128]{2,1,0:T(8,128)(2,1)S(1)} %broadcast_select_fusion.refs_0_.refs_1_.refs_4_.refs_5_), channel_id=1, source_target_pairs={{0,8},{2,14},{4,12},{6,2},{8,4},{10,6},{12,0},{14,10},{16,24},{18,... | collective-permute-start | bytes 786440 | tf_op jit(solution)/shard_map/ppermute | solution.py:39
  6.6 0.5 %collective-permute-start.5 = (bf16[2,512,128]{2,1,0:T(8,128)(2,1)S(1)}, bf16[2,512,128]{2,1,0:T(8,128)(2,1)S(1)}, u32[]{:S(2)}, u32[]{:S(2)}) collective-permute-start(bf16[2,512,128]{2,1,0:T(8,128)(2,1)S(1)} %broadcast_select_fusion.refs_0_.refs_1_.refs_4_.refs_5_), channel_id=1, source_target_pairs={{0,12},{2,10},{4,0},{6,14},{8,4},{10,6},{12,8},{14,2},{16,28},{18,... | collective-permute-start | bytes 786440 | tf_op jit(solution)/shard_map/ppermute | solution.py:39
  7.1 0.0 collective-permute-done.1.refs_4_.refs_5_.refs_2_.refs_7_
  7.1 0.0 collective-permute-start.3
  7.1 0.0 copy-start
  7.1 0.9 %copy-done = bf16[512,256]{1,0:T(8,128)(2,1)S(1)} copy-done((bf16[512,256]{1,0:T(8,128)(2,1)S(1)}, bf16[512,256]{1,0:T(8,128)(2,1)}, u32[]{:S(2)}) %copy-start) | copy-done | bytes 262168
  8.1 0.0 copy-start.1
  8.1 0.9 %copy-done.1 = bf16[512,256]{1,0:T(8,128)(2,1)S(1)} copy-done((bf16[512,256]{1,0:T(8,128)(2,1)S(1)}, bf16[512,256]{1,0:T(8,128)(2,1)}, u32[]{:S(2)}) %copy-start.1) | copy-done | bytes 262168
  9.0 0.0 copy-start.2
  9.0 0.7 %copy-done.2 = s32[512]{0:T(512)S(1)} copy-done((s32[512]{0:T(512)S(1)}, s32[512]{0:T(512)}, u32[]{:S(2)}) %copy-start.2) | copy-done | bytes 2072
  9.7 1.2 %stats.5 = (f32[12,512]{1,0:T(8,128)S(1)}, bf16[512,256]{1,0:T(8,128)(2,1)S(1)}, bf16[512,256]{1,0:T(8,128)(2,1)S(1)}, s32[1,512]{1,0:T(1,128)S(1)}) custom-call(s32[1]{0:T(128)} %bitcast.pos_ref, bf16[2,512,128]{2,1,0:T(8,128)(2,1)S(1)} %broadcast_select_fusion.refs_0_.refs_1_.refs_4_.refs_5_, bf16[512,256]{1,0:T(8,128)(2,1)S(1)} %copy-done, ...), custom_call_target="tpu_custom_call" | custom-call | bytes 1024 | tf_op jit(solution)/shard_map/stats/pallas_call | solution.py:268
  10.9 0.0 collective-permute-done.2.refs_6_.refs_7_.refs_3_.refs_9_
  10.9 1.8 %collective-permute-done.refs_2_.refs_5_ = bf16[2,512,128]{2,1,0:T(8,128)(2,1)S(1)} collective-permute-done((bf16[2,512,128]{2,1,0:T(8,128)(2,1)S(1)}, bf16[2,512,128]{2,1,0:T(8,128)(2,1)S(1)}, u32[]{:S(2)}, u32[]{:S(2)}) %collective-permute-start) | collective-permute-done | bytes 262176 | tf_op jit(solution)/shard_map/ppermute | solution.py:32
  12.7 0.0 collective-permute-done.3.refs_8_.refs_9_.refs_11_
  12.7 0.9 %stats.6 = (f32[12,512]{1,0:T(8,128)S(1)}, f32[3,4,512,512]{3,2,1,0:T(8,128)S(1)}, f32[3,4,512,512]{3,2,1,0:T(8,128)S(1)}) custom-call(s32[1]{0:T(128)} %bitcast.pos_ref, f32[12,512]{1,0:T(8,128)S(1)} %get-tuple-element.44.refs_0_, bf16[2,512,128]{2,1,0:T(8,128)(2,1)S(1)} %broadcast_select_fusion.refs_0_.refs_1_.refs_4_.refs_5_, ...), custom_call_target="tpu_custom_call" | custom-call | bytes 1024 | tf_op jit(solution)/shard_map/stats/pallas_call | solution.py:268
  13.6 3.8 %collective-permute-done.4.refs_3_.refs_12_ = bf16[2,512,128]{2,1,0:T(8,128)(2,1)S(1)} collective-permute-done((bf16[2,512,128]{2,1,0:T(8,128)(2,1)S(1)}, bf16[2,512,128]{2,1,0:T(8,128)(2,1)S(1)}, u32[]{:S(2)}, u32[]{:S(2)}) %collective-permute-start.4) | collective-permute-done | bytes 262176 | tf_op jit(solution)/shard_map/ppermute | solution.py:39
  17.4 0.1 collective-permute-done.5.refs_3_.refs_4_.refs_13_
  17.6 0.0 collective-permute-start.6
  17.6 0.5 %collective-permute-start.7 = (f32[6,512]{1,0:T(8,128)S(1)}, f32[6,512]{1,0:T(8,128)S(1)}, u32[]{:S(2)}, u32[]{:S(2)}) collective-permute-start(f32[6,512]{1,0:T(8,128)S(1)} %get-tuple-element.60.refs_0_), channel_id=1, source_target_pairs={{0,2},{2,0},{4,6},{6,4},{8,10},{10,8},{12,14},{14,12},{16,18},{18,... | collective-permute-start | bytes 36872 | tf_op jit(solution)/shard_map/ppermute | solution.py:44
  18.1 0.7 %collective-permute-done.6.refs_1_ = f32[6,512]{1,0:T(8,128)S(1)} collective-permute-done((f32[6,512]{1,0:T(8,128)S(1)}, f32[6,512]{1,0:T(8,128)S(1)}, u32[]{:S(2)}, u32[]{:S(2)}) %collective-permute-start.6) | collective-permute-done | bytes 12320 | tf_op jit(solution)/shard_map/ppermute | solution.py:44
  18.8 0.1 collective-permute-done.7.refs_2_
  18.9 0.1 grads.6
  19.0 5.8 %collective-permute-start.9 = (bf16[2,512,128]{2,1,0:T(8,128)(2,1)S(1)}, bf16[2,512,128]{2,1,0:T(8,128)(2,1)S(1)}, u32[]{:S(2)}, u32[]{:S(2)}) collective-permute-start(bf16[2,512,128]{2,1,0:T(8,128)(2,1)S(1)} %get-tuple-element.77), channel_id=1, source_target_pairs={{0,12},{2,14},{4,8},{6,10},{8,0},{10,2},{12,4},{14,6},{16,28},{18,... | collective-permute-start | bytes 786440 | tf_op jit(solution)/shard_map/ppermute | solution.py:39
  24.8 0.3 grads.7
  25.1 1.3 %collective-permute-start.10 = (bf16[2,512,128]{2,1,0:T(8,128)(2,1)S(1)}, bf16[2,512,128]{2,1,0:T(8,128)(2,1)S(1)}, u32[]{:S(2)}, u32[]{:S(2)}) collective-permute-start(bf16[2,512,128]{2,1,0:T(8,128)(2,1)S(1)} %get-tuple-element.78), channel_id=1, source_target_pairs={{2,6},{4,0},{6,10},{8,4},{10,14},{12,8},{14,2},{18,22},{20,16},{22... | collective-permute-start | bytes 786440 | tf_op jit(solution)/shard_map/ppermute | solution.py:39
  26.4 0.2 grads.8
  26.6 4.6 %collective-permute-start.11 = (bf16[2,512,128]{2,1,0:T(8,128)(2,1)S(1)}, bf16[2,512,128]{2,1,0:T(8,128)(2,1)S(1)}, u32[]{:S(2)}, u32[]{:S(2)}) collective-permute-start(bf16[2,512,128]{2,1,0:T(8,128)(2,1)S(1)} %get-tuple-element.79), channel_id=1, source_target_pairs={{0,4},{4,8},{6,2},{8,12},{10,6},{12,0},{14,10},{16,20},{20,24},{22... | collective-permute-start | bytes 786440 | tf_op jit(solution)/shard_map/ppermute | solution.py:39
  31.2 3.3 %grads.9 = (f32[256,512]{1,0:T(8,128)S(1)}, f32[256,512]{1,0:T(8,128)S(1)}, f32[2,512,128]{2,1,0:T(8,128)S(1)}) custom-call(s32[1]{0:T(128)} %bitcast.pos_ref, f32[256,512]{1,0:T(8,128)S(1)} %get-tuple-element.69.refs_0_, f32[256,512]{1,0:T(8,128)S(1)} %get-tuple-element.70.refs_1_, f32[4,512]{1,0:T(4,128)S(1)} %get-tuple-element.65.refs_0_.refs_2_, ...), custom_call_target="tpu_custom_call" | custom-call | bytes 1024 | tf_op jit(solution)/shard_map/grads/pallas_call | solution.py:281
  34.5 0.1 collective-permute-start.8
  34.6 0.0 collective-permute-done.9.part
  34.6 0.4 collective-permute-done.10.part
  35.1 2.0 %collective-permute-done.11.part = bf16[2,512,128]{2,1,0:T(8,128)(2,1)S(1)} collective-permute-done((bf16[2,512,128]{2,1,0:T(8,128)(2,1)S(1)}, bf16[2,512,128]{2,1,0:T(8,128)(2,1)S(1)}, u32[]{:S(2)}, u32[]{:S(2)}) %collective-permute-start.11) | collective-permute-done | bytes 262176 | tf_op jit(solution)/shard_map/ppermute | solution.py:39
  37.1 0.1 shard_map.79.mine
  37.2 3.3 %collective-permute-start.12 = (bf16[2,512,128]{2,1,0:T(8,128)(2,1)S(1)}, bf16[2,512,128]{2,1,0:T(8,128)(2,1)S(1)}, u32[]{:S(2)}, u32[]{:S(2)}) collective-permute-start(bf16[2,512,128]{2,1,0:T(8,128)(2,1)S(1)} %shard_map.79.mine), channel_id=1, source_target_pairs={{0,1},{1,0},{2,3},{3,2},{4,5},{5,4},{6,7},{7,6},{8,9},{9,8},{10,11... | collective-permute-start | bytes 786440 | tf_op jit(solution)/shard_map/ppermute | solution.py:48
  40.4 0.0 collective-permute-done.8.other
  40.4 0.8 %shard_map.76 = (bf16[512,256]{1,0:T(8,128)(2,1)}, f32[8,128]{1,0:T(8,128)S(1)}) custom-call(f32[256,512]{1,0:T(8,128)S(1)} %get-tuple-element.73.mine, f32[256,512]{1,0:T(8,128)S(1)} %collective-permute-done.8.other), custom_call_target="tpu_custom_call" | custom-call | bytes 1024 | tf_op jit(solution)/shard_map/pallas_call | solution.py:248
  41.3 4.9 %collective-permute-done.12.other = bf16[2,512,128]{2,1,0:T(8,128)(2,1)S(1)} collective-permute-done((bf16[2,512,128]{2,1,0:T(8,128)(2,1)S(1)}, bf16[2,512,128]{2,1,0:T(8,128)(2,1)S(1)}, u32[]{:S(2)}, u32[]{:S(2)}) %collective-permute-start.12) | collective-permute-done | bytes 262176 | tf_op jit(solution)/shard_map/ppermute | solution.py:48
  46.2 0.7 %shard_map.80 = (bf16[512,128]{1,0:T(8,128)(2,1)}, bf16[512,128]{1,0:T(8,128)(2,1)}) custom-call(bf16[2,512,128]{2,1,0:T(8,128)(2,1)S(1)} %shard_map.79.mine, bf16[2,512,128]{2,1,0:T(8,128)(2,1)S(1)} %collective-permute-done.12.other, f32[8,128]{1,0:T(8,128)S(1)} %get-tuple-element.80._), custom_call_target="tpu_custom_call" | custom-call | bytes 1024 | tf_op jit(solution)/shard_map/pallas_call | solution.py:248
  (7 shorter events, 0.1 us)
Async XLA Ops:
  1.7 5.4 %collective-permute-start.1 = (bf16[512,256]{1,0:T(8,128)(2,1)}, bf16[512,256]{1,0:T(8,128)(2,1)S(1)}, u32[]{:S(2)}, u32[]{:S(2)}) collective-permute-start(bf16[512,256]{1,0:T(8,128)(2,1)} %refs_1_.1), channel_id=1, source_target_pairs={{0,2},{2,0},{4,6},{6,4},{8,10},{10,8},{12,14},{14,12},{16,18},{18,... | collective-permute-start | bytes 786440 | tf_op jit(solution)/shard_map/ppermute | solution.py:44
  1.8 9.1 %collective-permute-start.2 = (bf16[512,256]{1,0:T(8,128)(2,1)}, bf16[512,256]{1,0:T(8,128)(2,1)S(1)}, u32[]{:S(2)}, u32[]{:S(2)}) collective-permute-start(bf16[512,256]{1,0:T(8,128)(2,1)} %refs_2_.1), channel_id=1, source_target_pairs={{0,2},{2,0},{4,6},{6,4},{8,10},{10,8},{12,14},{14,12},{16,18},{18,... | collective-permute-start | bytes 786440 | tf_op jit(solution)/shard_map/ppermute | solution.py:44
  2.3 10.4 %collective-permute-start = (bf16[2,512,128]{2,1,0:T(8,128)(2,1)S(1)}, bf16[2,512,128]{2,1,0:T(8,128)(2,1)S(1)}, u32[]{:S(2)}, u32[]{:S(2)}) collective-permute-start(bf16[2,512,128]{2,1,0:T(8,128)(2,1)S(1)} %broadcast_select_fusion.refs_0_.refs_1_.refs_4_.refs_5_), channel_id=1, source_target_pairs={{0,4},{2,6},{4,8},{6,10},{8,12},{10,14},{12,0},{14,2},{16,20},{18,... | collective-permute-start | bytes 786440 | tf_op jit(solution)/shard_map/ppermute | solution.py:32
  3.9 13.6 %collective-permute-start.4 = (bf16[2,512,128]{2,1,0:T(8,128)(2,1)S(1)}, bf16[2,512,128]{2,1,0:T(8,128)(2,1)S(1)}, u32[]{:S(2)}, u32[]{:S(2)}) collective-permute-start(bf16[2,512,128]{2,1,0:T(8,128)(2,1)S(1)} %broadcast_select_fusion.refs_0_.refs_1_.refs_4_.refs_5_), channel_id=1, source_target_pairs={{0,8},{2,14},{4,12},{6,2},{8,4},{10,6},{12,0},{14,10},{16,24},{18,... | collective-permute-start | bytes 786440 | tf_op jit(solution)/shard_map/ppermute | solution.py:39
  6.6 10.9 %collective-permute-start.5 = (bf16[2,512,128]{2,1,0:T(8,128)(2,1)S(1)}, bf16[2,512,128]{2,1,0:T(8,128)(2,1)S(1)}, u32[]{:S(2)}, u32[]{:S(2)}) collective-permute-start(bf16[2,512,128]{2,1,0:T(8,128)(2,1)S(1)} %broadcast_select_fusion.refs_0_.refs_1_.refs_4_.refs_5_), channel_id=1, source_target_pairs={{0,12},{2,10},{4,0},{6,14},{8,4},{10,6},{12,8},{14,2},{16,28},{18,... | collective-permute-start | bytes 786440 | tf_op jit(solution)/shard_map/ppermute | solution.py:39
  7.1 5.6 %collective-permute-start.3 = (s32[1,512]{1,0:T(1,128)}, s32[1,512]{1,0:T(1,128)S(1)}, u32[]{:S(2)}, u32[]{:S(2)}) collective-permute-start(s32[1,512]{1,0:T(1,128)} %bitcast.2), channel_id=1, source_target_pairs={{0,2},{2,0},{4,6},{6,4},{8,10},{10,8},{12,14},{14,12},{16,18},{18,... | collective-permute-start | bytes 6152 | tf_op jit(solution)/shard_map/ppermute | solution.py:44
  7.1 1.0 %copy-start = (bf16[512,256]{1,0:T(8,128)(2,1)S(1)}, bf16[512,256]{1,0:T(8,128)(2,1)}, u32[]{:S(2)}) copy-start(bf16[512,256]{1,0:T(8,128)(2,1)} %refs_1_.1) | copy-start | bytes 786436
  8.1 0.9 %copy-start.1 = (bf16[512,256]{1,0:T(8,128)(2,1)S(1)}, bf16[512,256]{1,0:T(8,128)(2,1)}, u32[]{:S(2)}) copy-start(bf16[512,256]{1,0:T(8,128)(2,1)} %refs_2_.1) | copy-start | bytes 786436
  9.0 0.7 %copy-start.2 = (s32[512]{0:T(512)S(1)}, s32[512]{0:T(512)}, u32[]{:S(2)}) copy-start(s32[512]{0:T(512)} %param.9) | copy-start | bytes 6148
  17.6 1.2 %collective-permute-start.6 = (f32[6,512]{1,0:T(8,128)S(1)}, f32[6,512]{1,0:T(8,128)S(1)}, u32[]{:S(2)}, u32[]{:S(2)}) collective-permute-start(f32[6,512]{1,0:T(8,128)S(1)} %get-tuple-element.61.refs_1_), channel_id=1, source_target_pairs={{0,2},{2,0},{4,6},{6,4},{8,10},{10,8},{12,14},{14,12},{16,18},{18,... | collective-permute-start | bytes 36872 | tf_op jit(solution)/shard_map/ppermute | solution.py:44
  17.6 1.3 %collective-permute-start.7 = (f32[6,512]{1,0:T(8,128)S(1)}, f32[6,512]{1,0:T(8,128)S(1)}, u32[]{:S(2)}, u32[]{:S(2)}) collective-permute-start(f32[6,512]{1,0:T(8,128)S(1)} %get-tuple-element.60.refs_0_), channel_id=1, source_target_pairs={{0,2},{2,0},{4,6},{6,4},{8,10},{10,8},{12,14},{14,12},{16,18},{18,... | collective-permute-start | bytes 36872 | tf_op jit(solution)/shard_map/ppermute | solution.py:44
  19.0 15.6 %collective-permute-start.9 = (bf16[2,512,128]{2,1,0:T(8,128)(2,1)S(1)}, bf16[2,512,128]{2,1,0:T(8,128)(2,1)S(1)}, u32[]{:S(2)}, u32[]{:S(2)}) collective-permute-start(bf16[2,512,128]{2,1,0:T(8,128)(2,1)S(1)} %get-tuple-element.77), channel_id=1, source_target_pairs={{0,12},{2,14},{4,8},{6,10},{8,0},{10,2},{12,4},{14,6},{16,28},{18,... | collective-permute-start | bytes 786440 | tf_op jit(solution)/shard_map/ppermute | solution.py:39
  25.1 9.9 %collective-permute-start.10 = (bf16[2,512,128]{2,1,0:T(8,128)(2,1)S(1)}, bf16[2,512,128]{2,1,0:T(8,128)(2,1)S(1)}, u32[]{:S(2)}, u32[]{:S(2)}) collective-permute-start(bf16[2,512,128]{2,1,0:T(8,128)(2,1)S(1)} %get-tuple-element.78), channel_id=1, source_target_pairs={{2,6},{4,0},{6,10},{8,4},{10,14},{12,8},{14,2},{18,22},{20,16},{22... | collective-permute-start | bytes 786440 | tf_op jit(solution)/shard_map/ppermute | solution.py:39
  26.6 10.5 %collective-permute-start.11 = (bf16[2,512,128]{2,1,0:T(8,128)(2,1)S(1)}, bf16[2,512,128]{2,1,0:T(8,128)(2,1)S(1)}, u32[]{:S(2)}, u32[]{:S(2)}) collective-permute-start(bf16[2,512,128]{2,1,0:T(8,128)(2,1)S(1)} %get-tuple-element.79), channel_id=1, source_target_pairs={{0,4},{4,8},{6,2},{8,12},{10,6},{12,0},{14,10},{16,20},{20,24},{22... | collective-permute-start | bytes 786440 | tf_op jit(solution)/shard_map/ppermute | solution.py:39
  34.5 6.0 %collective-permute-start.8 = (f32[256,512]{1,0:T(8,128)S(1)}, f32[256,512]{1,0:T(8,128)S(1)}, u32[]{:S(2)}, u32[]{:S(2)}) collective-permute-start(f32[256,512]{1,0:T(8,128)S(1)} %get-tuple-element.74), channel_id=1, source_target_pairs={{0,2},{2,0},{4,6},{6,4},{8,10},{10,8},{12,14},{14,12},{16,18},{18,... | collective-permute-start | bytes 1572872 | tf_op jit(solution)/shard_map/ppermute | solution.py:44
  37.2 9.1 %collective-permute-start.12 = (bf16[2,512,128]{2,1,0:T(8,128)(2,1)S(1)}, bf16[2,512,128]{2,1,0:T(8,128)(2,1)S(1)}, u32[]{:S(2)}, u32[]{:S(2)}) collective-permute-start(bf16[2,512,128]{2,1,0:T(8,128)(2,1)S(1)} %shard_map.79.mine), channel_id=1, source_target_pairs={{0,1},{1,0},{2,3},{3,2},{4,5},{5,4},{6,7},{7,6},{8,9},{9,8},{10,11... | collective-permute-start | bytes 786440 | tf_op jit(solution)/shard_map/ppermute | solution.py:48

commit v8 on v6

--- a/solution.py
+++ b/solution.py
@@ -339,9 +339,9 @@
     back_a = chip_permute(part, (3, 2, 0, 1), (3, 2, 0, 1))
     fin = (fin_near, fin_far)
     dq, part = call_stage(1, cp, (), fin, (slot1, slot2), rows, kept)
-    back_b = chip_permute(part, (None, 0, 1, 2), (1, 2, 3, 0))
+    back_b = chip_permute(part, (None, 0, 1, 2), (None, 2, 3, 0))
     dq, part = call_stage(2, cp, dq, fin, (slot3, slot1), rows, kept)
-    back_c = chip_permute(part, (1, 2, 3, 0), (None, 0, 1, 2))
+    back_c = chip_permute(part, (None, 2, 3, 0), (None, 0, 1, 2))
     dq, own = call_stage(3, cp, dq, fin, (kv, kv), rows, (*rows[4:], slot2, slot3, ds_near, ds_far))
 
     dq_other = core_swap(dq[1])

time: 47.2 us -> 47.2 us (level)
  waiting for transfers between devices: 13.9 us -> 17.2 us
  starting transfers between devices: 20.9 us -> 17.6 us
    ppermute x5, waiting for transfers between devices: 8.17 us -> 11.4 us  [chip_permute(): return lax.ppermute(array, 'cp', pairs)]
    ppermute x5, starting transfers between devices: 14.8 us -> 11.5 us  [chip_permute(): return lax.ppermute(array, 'cp', pairs)]
  transfers between devices with their start and end apart: 13 -> 13, of which waited for: 6 -> 7; matrix products, arithmetic and copies ran while one was open for 0% -> 0% of each run, Pallas kernels for 15% -> 15%
where the time goes in v8:
time: 47.2 us; the launch traced here: 47 us
  starting transfers between devices  17.6 us (37%)
  waiting for transfers between devices  17.2 us (36%)
  Pallas kernels  7.74 us (16%)
  local copies, waits for them, and re-layouts  2.58 us (5%)
  other arithmetic  1.07 us (2%)
  between operations  0.78 us (2%)
    ppermute x5, starting transfers between devices, chip_permute(): return lax.ppermute(array, 'cp', pairs)  11.5 us
    ppermute x5, waiting for transfers between devices, chip_permute(): return lax.ppermute(array, 'cp', pairs)  11.4 us
    ppermute x1, waiting for transfers between devices, hd_swap(): return lax.ppermute(array, 'hd', [(0, 1), (1, 0)])  4.94 us
    pallas_call x5, Pallas kernels, call_grads(): pl.pallas_call(kernel, out_shape=out, in_specs=[SM] + [VM] * len(args), o...  3.89 us
    ppermute x1, starting transfers between devices, hd_swap(): return lax.ppermute(array, 'hd', [(0, 1), (1, 0)])  3.28 us
    unnamed x6, local copies, waits for them, and re-layouts  2.58 us
    pallas_call x5, Pallas kernels, call_stats(): pl.pallas_call(functools.partial(stats_kernel, step, slot, groups), out_s...  2.11 us
    pallas_call x5, Pallas kernels, simple(): pl.pallas_call(kernel, out_shape=out, in_specs=[VM] * len(args), out_spec...  1.74 us
  transfers between devices with their start and end apart: 13, of which 7 were waited for; matrix products, arithmetic and copies ran while one was open for 0% of the time, Pallas kernels for 15%

profile of v8, /device:TPU:0, one launch (start us, length us, event | category | flops | bytes accessed | tf_op | source)
XLA Modules:
  0.0 47.0 jit_solution(6740587808232456478)
XLA Ops:
  0.6 1.1 %broadcast_select_fusion.refs_0_.refs_1_.refs_4_.refs_5_ = bf16[2,512,128]{2,1,0:T(8,128)(2,1)S(1)} fusion(pred[2]{0:T(512)(128)(4,1)S(1)} %iota_compare_fusion, bf16[512,128]{1,0:T(8,128)(2,1)} %param.7, bf16[512,128]{1,0:T(8,128)(2,1)} %param.6), kind=kLoop, calls=%fused_computation | loop fusion | flops 131072 | bytes 524290 | tf_op jit(solution)/shard_map/jit(_where)/select_n | solution.py:318
  1.7 0.1 collective-permute-start.1
  1.8 0.5 %collective-permute-start.2 = (bf16[512,256]{1,0:T(8,128)(2,1)}, bf16[512,256]{1,0:T(8,128)(2,1)S(1)}, u32[]{:S(2)}, u32[]{:S(2)}) collective-permute-start(bf16[512,256]{1,0:T(8,128)(2,1)} %refs_2_.1), channel_id=1, source_target_pairs={{0,2},{2,0},{4,6},{6,4},{8,10},{10,8},{12,14},{14,12},{16,18},{18,... | collective-permute-start | bytes 786440 | tf_op jit(solution)/shard_map/ppermute | solution.py:44
  2.3 1.6 %collective-permute-start = (bf16[2,512,128]{2,1,0:T(8,128)(2,1)S(1)}, bf16[2,512,128]{2,1,0:T(8,128)(2,1)S(1)}, u32[]{:S(2)}, u32[]{:S(2)}) collective-permute-start(bf16[2,512,128]{2,1,0:T(8,128)(2,1)S(1)} %broadcast_select_fusion.refs_0_.refs_1_.refs_4_.refs_5_), channel_id=1, source_target_pairs={{0,4},{2,6},{4,8},{6,10},{8,12},{10,14},{12,0},{14,2},{16,20},{18,... | collective-permute-start | bytes 786440 | tf_op jit(solution)/shard_map/ppermute | solution.py:32
  3.9 2.7 %collective-permute-start.4 = (bf16[2,512,128]{2,1,0:T(8,128)(2,1)S(1)}, bf16[2,512,128]{2,1,0:T(8,128)(2,1)S(1)}, u32[]{:S(2)}, u32[]{:S(2)}) collective-permute-start(bf16[2,512,128]{2,1,0:T(8,128)(2,1)S(1)} %broadcast_select_fusion.refs_0_.refs_1_.refs_4_.refs_5_), channel_id=1, source_target_pairs={{0,8},{2,14},{4,12},{6,2},{8,0},{10,6},{12,4},{14,10},{16,24},{18,... | collective-permute-start | bytes 786440 | tf_op jit(solution)/shard_map/ppermute | solution.py:39
  6.6 1.4 %collective-permute-start.5 = (bf16[2,512,128]{2,1,0:T(8,128)(2,1)S(1)}, bf16[2,512,128]{2,1,0:T(8,128)(2,1)S(1)}, u32[]{:S(2)}, u32[]{:S(2)}) collective-permute-start(bf16[2,512,128]{2,1,0:T(8,128)(2,1)S(1)} %broadcast_select_fusion.refs_0_.refs_1_.refs_4_.refs_5_), channel_id=1, source_target_pairs={{0,12},{2,10},{4,0},{6,14},{8,4},{10,2},{12,8},{14,6},{16,28},{18,... | collective-permute-start | bytes 786440 | tf_op jit(solution)/shard_map/ppermute | solution.py:39
  8.0 0.0 collective-permute-done.1.refs_4_.refs_5_.refs_2_.refs_7_
  8.0 0.0 collective-permute-start.3
  8.0 0.0 copy-start
  8.0 0.9 %copy-done = bf16[512,256]{1,0:T(8,128)(2,1)S(1)} copy-done((bf16[512,256]{1,0:T(8,128)(2,1)S(1)}, bf16[512,256]{1,0:T(8,128)(2,1)}, u32[]{:S(2)}) %copy-start) | copy-done | bytes 262168
  9.0 0.0 copy-start.1
  9.0 0.9 %copy-done.1 = bf16[512,256]{1,0:T(8,128)(2,1)S(1)} copy-done((bf16[512,256]{1,0:T(8,128)(2,1)S(1)}, bf16[512,256]{1,0:T(8,128)(2,1)}, u32[]{:S(2)}) %copy-start.1) | copy-done | bytes 262168
  9.9 0.0 copy-start.2
  9.9 0.7 %copy-done.2 = s32[512]{0:T(512)S(1)} copy-done((s32[512]{0:T(512)S(1)}, s32[512]{0:T(512)}, u32[]{:S(2)}) %copy-start.2) | copy-done | bytes 2072
  10.6 1.2 %stats.5 = (f32[12,512]{1,0:T(8,128)S(1)}, bf16[512,256]{1,0:T(8,128)(2,1)S(1)}, bf16[512,256]{1,0:T(8,128)(2,1)S(1)}, s32[1,512]{1,0:T(1,128)S(1)}) custom-call(s32[1]{0:T(128)} %bitcast.pos_ref, bf16[2,512,128]{2,1,0:T(8,128)(2,1)S(1)} %broadcast_select_fusion.refs_0_.refs_1_.refs_4_.refs_5_, bf16[512,256]{1,0:T(8,128)(2,1)S(1)} %copy-done, ...), custom_call_target="tpu_custom_call" | custom-call | bytes 1024 | tf_op jit(solution)/shard_map/stats/pallas_call | solution.py:268
  11.8 0.0 collective-permute-done.2.refs_6_.refs_7_.refs_3_.refs_9_
  11.8 0.0 collective-permute-done.refs_2_.refs_5_
  11.8 0.0 collective-permute-done.3.refs_8_.refs_9_.refs_11_
  11.8 0.9 %stats.6 = (f32[12,512]{1,0:T(8,128)S(1)}, f32[3,4,512,512]{3,2,1,0:T(8,128)S(1)}, f32[3,4,512,512]{3,2,1,0:T(8,128)S(1)}) custom-call(s32[1]{0:T(128)} %bitcast.pos_ref, f32[12,512]{1,0:T(8,128)S(1)} %get-tuple-element.44.refs_0_, bf16[2,512,128]{2,1,0:T(8,128)(2,1)S(1)} %broadcast_select_fusion.refs_0_.refs_1_.refs_4_.refs_5_, ...), custom_call_target="tpu_custom_call" | custom-call | bytes 1024 | tf_op jit(solution)/shard_map/stats/pallas_call | solution.py:268
  12.8 5.7 %collective-permute-done.4.refs_3_.refs_12_ = bf16[2,512,128]{2,1,0:T(8,128)(2,1)S(1)} collective-permute-done((bf16[2,512,128]{2,1,0:T(8,128)(2,1)S(1)}, bf16[2,512,128]{2,1,0:T(8,128)(2,1)S(1)}, u32[]{:S(2)}, u32[]{:S(2)}) %collective-permute-start.4) | collective-permute-done | bytes 262176 | tf_op jit(solution)/shard_map/ppermute | solution.py:39
  18.5 0.0 collective-permute-done.5.refs_3_.refs_4_.refs_13_
  18.5 0.1 collective-permute-start.6
  18.6 0.5 %collective-permute-start.7 = (f32[6,512]{1,0:T(8,128)S(1)}, f32[6,512]{1,0:T(8,128)S(1)}, u32[]{:S(2)}, u32[]{:S(2)}) collective-permute-start(f32[6,512]{1,0:T(8,128)S(1)} %get-tuple-element.60.refs_0_), channel_id=1, source_target_pairs={{0,2},{2,0},{4,6},{6,4},{8,10},{10,8},{12,14},{14,12},{16,18},{18,... | collective-permute-start | bytes 36872 | tf_op jit(solution)/shard_map/ppermute | solution.py:44
  19.1 0.7 %collective-permute-done.6.refs_1_ = f32[6,512]{1,0:T(8,128)S(1)} collective-permute-done((f32[6,512]{1,0:T(8,128)S(1)}, f32[6,512]{1,0:T(8,128)S(1)}, u32[]{:S(2)}, u32[]{:S(2)}) %collective-permute-start.6) | collective-permute-done | bytes 12320 | tf_op jit(solution)/shard_map/ppermute | solution.py:44
  19.8 0.1 collective-permute-done.7.refs_2_
  20.0 0.1 grads.6
  20.0 4.8 %collective-permute-start.9 = (bf16[2,512,128]{2,1,0:T(8,128)(2,1)S(1)}, bf16[2,512,128]{2,1,0:T(8,128)(2,1)S(1)}, u32[]{:S(2)}, u32[]{:S(2)}) collective-permute-start(bf16[2,512,128]{2,1,0:T(8,128)(2,1)S(1)} %get-tuple-element.77), channel_id=1, source_target_pairs={{0,12},{2,14},{4,8},{6,10},{8,0},{10,2},{12,4},{14,6},{16,28},{18,... | collective-permute-start | bytes 786440 | tf_op jit(solution)/shard_map/ppermute | solution.py:39
  24.8 0.3 grads.7
  25.1 1.3 %collective-permute-start.10 = (bf16[2,512,128]{2,1,0:T(8,128)(2,1)S(1)}, bf16[2,512,128]{2,1,0:T(8,128)(2,1)S(1)}, u32[]{:S(2)}, u32[]{:S(2)}) collective-permute-start(bf16[2,512,128]{2,1,0:T(8,128)(2,1)S(1)} %get-tuple-element.78), channel_id=1, source_target_pairs={{4,0},{6,10},{8,4},{10,14},{12,8},{14,2},{20,16},{22,26},{24,20},{... | collective-permute-start | bytes 786440 | tf_op jit(solution)/shard_map/ppermute | solution.py:39
  26.4 0.2 grads.8
  26.6 1.3 %collective-permute-start.11 = (bf16[2,512,128]{2,1,0:T(8,128)(2,1)S(1)}, bf16[2,512,128]{2,1,0:T(8,128)(2,1)S(1)}, u32[]{:S(2)}, u32[]{:S(2)}) collective-permute-start(bf16[2,512,128]{2,1,0:T(8,128)(2,1)S(1)} %get-tuple-element.79), channel_id=1, source_target_pairs={{4,8},{6,2},{8,12},{10,6},{12,0},{14,10},{20,24},{22,18},{24,28},{... | collective-permute-start | bytes 786440 | tf_op jit(solution)/shard_map/ppermute | solution.py:39
  27.9 3.3 %grads.9 = (f32[256,512]{1,0:T(8,128)S(1)}, f32[256,512]{1,0:T(8,128)S(1)}, f32[2,512,128]{2,1,0:T(8,128)S(1)}) custom-call(s32[1]{0:T(128)} %bitcast.pos_ref, f32[256,512]{1,0:T(8,128)S(1)} %get-tuple-element.69.refs_0_, f32[256,512]{1,0:T(8,128)S(1)} %get-tuple-element.70.refs_1_, f32[4,512]{1,0:T(4,128)S(1)} %get-tuple-element.65.refs_0_.refs_2_, ...), custom_call_target="tpu_custom_call" | custom-call | bytes 1024 | tf_op jit(solution)/shard_map/grads/pallas_call | solution.py:281
  31.2 0.1 collective-permute-start.8
  31.3 0.4 collective-permute-done.9.part
  31.7 3.7 %collective-permute-done.10.part = bf16[2,512,128]{2,1,0:T(8,128)(2,1)S(1)} collective-permute-done((bf16[2,512,128]{2,1,0:T(8,128)(2,1)S(1)}, bf16[2,512,128]{2,1,0:T(8,128)(2,1)S(1)}, u32[]{:S(2)}, u32[]{:S(2)}) %collective-permute-start.10) | collective-permute-done | bytes 262176 | tf_op jit(solution)/shard_map/ppermute | solution.py:39
  35.5 1.6 %collective-permute-done.11.part = bf16[2,512,128]{2,1,0:T(8,128)(2,1)S(1)} collective-permute-done((bf16[2,512,128]{2,1,0:T(8,128)(2,1)S(1)}, bf16[2,512,128]{2,1,0:T(8,128)(2,1)S(1)}, u32[]{:S(2)}, u32[]{:S(2)}) %collective-permute-start.11) | collective-permute-done | bytes 262176 | tf_op jit(solution)/shard_map/ppermute | solution.py:39
  37.1 0.1 shard_map.79.mine
  37.2 3.3 %collective-permute-start.12 = (bf16[2,512,128]{2,1,0:T(8,128)(2,1)S(1)}, bf16[2,512,128]{2,1,0:T(8,128)(2,1)S(1)}, u32[]{:S(2)}, u32[]{:S(2)}) collective-permute-start(bf16[2,512,128]{2,1,0:T(8,128)(2,1)S(1)} %shard_map.79.mine), channel_id=1, source_target_pairs={{0,1},{1,0},{2,3},{3,2},{4,5},{5,4},{6,7},{7,6},{8,9},{9,8},{10,11... | collective-permute-start | bytes 786440 | tf_op jit(solution)/shard_map/ppermute | solution.py:48
  40.4 0.0 collective-permute-done.8.other
  40.4 0.8 %shard_map.76 = (bf16[512,256]{1,0:T(8,128)(2,1)}, f32[8,128]{1,0:T(8,128)S(1)}) custom-call(f32[256,512]{1,0:T(8,128)S(1)} %get-tuple-element.73.mine, f32[256,512]{1,0:T(8,128)S(1)} %collective-permute-done.8.other), custom_call_target="tpu_custom_call" | custom-call | bytes 1024 | tf_op jit(solution)/shard_map/pallas_call | solution.py:248
  41.3 4.9 %collective-permute-done.12.other = bf16[2,512,128]{2,1,0:T(8,128)(2,1)S(1)} collective-permute-done((bf16[2,512,128]{2,1,0:T(8,128)(2,1)S(1)}, bf16[2,512,128]{2,1,0:T(8,128)(2,1)S(1)}, u32[]{:S(2)}, u32[]{:S(2)}) %collective-permute-start.12) | collective-permute-done | bytes 262176 | tf_op jit(solution)/shard_map/ppermute | solution.py:48
  46.2 0.7 %shard_map.80 = (bf16[512,128]{1,0:T(8,128)(2,1)}, bf16[512,128]{1,0:T(8,128)(2,1)}) custom-call(bf16[2,512,128]{2,1,0:T(8,128)(2,1)S(1)} %shard_map.79.mine, bf16[2,512,128]{2,1,0:T(8,128)(2,1)S(1)} %collective-permute-done.12.other, f32[8,128]{1,0:T(8,128)S(1)} %get-tuple-element.80._), custom_call_target="tpu_custom_call" | custom-call | bytes 1024 | tf_op jit(solution)/shard_map/pallas_call | solution.py:248
  (7 shorter events, 0.2 us)
Async XLA Ops:
  1.7 6.3 %collective-permute-start.1 = (bf16[512,256]{1,0:T(8,128)(2,1)}, bf16[512,256]{1,0:T(8,128)(2,1)S(1)}, u32[]{:S(2)}, u32[]{:S(2)}) collective-permute-start(bf16[512,256]{1,0:T(8,128)(2,1)} %refs_1_.1), channel_id=1, source_target_pairs={{0,2},{2,0},{4,6},{6,4},{8,10},{10,8},{12,14},{14,12},{16,18},{18,... | collective-permute-start | bytes 786440 | tf_op jit(solution)/shard_map/ppermute | solution.py:44
  1.8 10.0 %collective-permute-start.2 = (bf16[512,256]{1,0:T(8,128)(2,1)}, bf16[512,256]{1,0:T(8,128)(2,1)S(1)}, u32[]{:S(2)}, u32[]{:S(2)}) collective-permute-start(bf16[512,256]{1,0:T(8,128)(2,1)} %refs_2_.1), channel_id=1, source_target_pairs={{0,2},{2,0},{4,6},{6,4},{8,10},{10,8},{12,14},{14,12},{16,18},{18,... | collective-permute-start | bytes 786440 | tf_op jit(solution)/shard_map/ppermute | solution.py:44
  2.3 9.5 %collective-permute-start = (bf16[2,512,128]{2,1,0:T(8,128)(2,1)S(1)}, bf16[2,512,128]{2,1,0:T(8,128)(2,1)S(1)}, u32[]{:S(2)}, u32[]{:S(2)}) collective-permute-start(bf16[2,512,128]{2,1,0:T(8,128)(2,1)S(1)} %broadcast_select_fusion.refs_0_.refs_1_.refs_4_.refs_5_), channel_id=1, source_target_pairs={{0,4},{2,6},{4,8},{6,10},{8,12},{10,14},{12,0},{14,2},{16,20},{18,... | collective-permute-start | bytes 786440 | tf_op jit(solution)/shard_map/ppermute | solution.py:32
  3.9 14.6 %collective-permute-start.4 = (bf16[2,512,128]{2,1,0:T(8,128)(2,1)S(1)}, bf16[2,512,128]{2,1,0:T(8,128)(2,1)S(1)}, u32[]{:S(2)}, u32[]{:S(2)}) collective-permute-start(bf16[2,512,128]{2,1,0:T(8,128)(2,1)S(1)} %broadcast_select_fusion.refs_0_.refs_1_.refs_4_.refs_5_), channel_id=1, source_target_pairs={{0,8},{2,14},{4,12},{6,2},{8,0},{10,6},{12,4},{14,10},{16,24},{18,... | collective-permute-start | bytes 786440 | tf_op jit(solution)/shard_map/ppermute | solution.py:39
  6.6 11.9 %collective-permute-start.5 = (bf16[2,512,128]{2,1,0:T(8,128)(2,1)S(1)}, bf16[2,512,128]{2,1,0:T(8,128)(2,1)S(1)}, u32[]{:S(2)}, u32[]{:S(2)}) collective-permute-start(bf16[2,512,128]{2,1,0:T(8,128)(2,1)S(1)} %broadcast_select_fusion.refs_0_.refs_1_.refs_4_.refs_5_), channel_id=1, source_target_pairs={{0,12},{2,10},{4,0},{6,14},{8,4},{10,2},{12,8},{14,6},{16,28},{18,... | collective-permute-start | bytes 786440 | tf_op jit(solution)/shard_map/ppermute | solution.py:39
  8.0 3.8 %collective-permute-start.3 = (s32[1,512]{1,0:T(1,128)}, s32[1,512]{1,0:T(1,128)S(1)}, u32[]{:S(2)}, u32[]{:S(2)}) collective-permute-start(s32[1,512]{1,0:T(1,128)} %bitcast.2), channel_id=1, source_target_pairs={{0,2},{2,0},{4,6},{6,4},{8,10},{10,8},{12,14},{14,12},{16,18},{18,... | collective-permute-start | bytes 6152 | tf_op jit(solution)/shard_map/ppermute | solution.py:44
  8.0 1.0 %copy-start = (bf16[512,256]{1,0:T(8,128)(2,1)S(1)}, bf16[512,256]{1,0:T(8,128)(2,1)}, u32[]{:S(2)}) copy-start(bf16[512,256]{1,0:T(8,128)(2,1)} %refs_1_.1) | copy-start | bytes 786436
  9.0 0.9 %copy-start.1 = (bf16[512,256]{1,0:T(8,128)(2,1)S(1)}, bf16[512,256]{1,0:T(8,128)(2,1)}, u32[]{:S(2)}) copy-start(bf16[512,256]{1,0:T(8,128)(2,1)} %refs_2_.1) | copy-start | bytes 786436
  9.9 0.7 %copy-start.2 = (s32[512]{0:T(512)S(1)}, s32[512]{0:T(512)}, u32[]{:S(2)}) copy-start(s32[512]{0:T(512)} %param.9) | copy-start | bytes 6148
  18.5 1.3 %collective-permute-start.6 = (f32[6,512]{1,0:T(8,128)S(1)}, f32[6,512]{1,0:T(8,128)S(1)}, u32[]{:S(2)}, u32[]{:S(2)}) collective-permute-start(f32[6,512]{1,0:T(8,128)S(1)} %get-tuple-element.61.refs_1_), channel_id=1, source_target_pairs={{0,2},{2,0},{4,6},{6,4},{8,10},{10,8},{12,14},{14,12},{16,18},{18,... | collective-permute-start | bytes 36872 | tf_op jit(solution)/shard_map/ppermute | solution.py:44
  18.6 1.3 %collective-permute-start.7 = (f32[6,512]{1,0:T(8,128)S(1)}, f32[6,512]{1,0:T(8,128)S(1)}, u32[]{:S(2)}, u32[]{:S(2)}) collective-permute-start(f32[6,512]{1,0:T(8,128)S(1)} %get-tuple-element.60.refs_0_), channel_id=1, source_target_pairs={{0,2},{2,0},{4,6},{6,4},{8,10},{10,8},{12,14},{14,12},{16,18},{18,... | collective-permute-start | bytes 36872 | tf_op jit(solution)/shard_map/ppermute | solution.py:44
  20.0 11.6 %collective-permute-start.9 = (bf16[2,512,128]{2,1,0:T(8,128)(2,1)S(1)}, bf16[2,512,128]{2,1,0:T(8,128)(2,1)S(1)}, u32[]{:S(2)}, u32[]{:S(2)}) collective-permute-start(bf16[2,512,128]{2,1,0:T(8,128)(2,1)S(1)} %get-tuple-element.77), channel_id=1, source_target_pairs={{0,12},{2,14},{4,8},{6,10},{8,0},{10,2},{12,4},{14,6},{16,28},{18,... | collective-permute-start | bytes 786440 | tf_op jit(solution)/shard_map/ppermute | solution.py:39
  25.1 10.3 %collective-permute-start.10 = (bf16[2,512,128]{2,1,0:T(8,128)(2,1)S(1)}, bf16[2,512,128]{2,1,0:T(8,128)(2,1)S(1)}, u32[]{:S(2)}, u32[]{:S(2)}) collective-permute-start(bf16[2,512,128]{2,1,0:T(8,128)(2,1)S(1)} %get-tuple-element.78), channel_id=1, source_target_pairs={{4,0},{6,10},{8,4},{10,14},{12,8},{14,2},{20,16},{22,26},{24,20},{... | collective-permute-start | bytes 786440 | tf_op jit(solution)/shard_map/ppermute | solution.py:39
  26.6 10.5 %collective-permute-start.11 = (bf16[2,512,128]{2,1,0:T(8,128)(2,1)S(1)}, bf16[2,512,128]{2,1,0:T(8,128)(2,1)S(1)}, u32[]{:S(2)}, u32[]{:S(2)}) collective-permute-start(bf16[2,512,128]{2,1,0:T(8,128)(2,1)S(1)} %get-tuple-element.79), channel_id=1, source_target_pairs={{4,8},{6,2},{8,12},{10,6},{12,0},{14,10},{20,24},{22,18},{24,28},{... | collective-permute-start | bytes 786440 | tf_op jit(solution)/shard_map/ppermute | solution.py:39
  31.2 9.2 %collective-permute-start.8 = (f32[256,512]{1,0:T(8,128)S(1)}, f32[256,512]{1,0:T(8,128)S(1)}, u32[]{:S(2)}, u32[]{:S(2)}) collective-permute-start(f32[256,512]{1,0:T(8,128)S(1)} %get-tuple-element.74), channel_id=1, source_target_pairs={{0,2},{2,0},{4,6},{6,4},{8,10},{10,8},{12,14},{14,12},{16,18},{18,... | collective-permute-start | bytes 1572872 | tf_op jit(solution)/shard_map/ppermute | solution.py:44
  37.2 9.1 %collective-permute-start.12 = (bf16[2,512,128]{2,1,0:T(8,128)(2,1)S(1)}, bf16[2,512,128]{2,1,0:T(8,128)(2,1)S(1)}, u32[]{:S(2)}, u32[]{:S(2)}) collective-permute-start(bf16[2,512,128]{2,1,0:T(8,128)(2,1)S(1)} %shard_map.79.mine), channel_id=1, source_target_pairs={{0,1},{1,0},{2,3},{3,2},{4,5},{5,4},{6,7},{7,6},{8,9},{9,8},{10,11... | collective-permute-start | bytes 786440 | tf_op jit(solution)/shard_map/ppermute | solution.py:48

commit v9 on v8

--- a/solution.py
+++ b/solution.py
@@ -339,9 +339,9 @@
     back_a = chip_permute(part, (3, 2, 0, 1), (3, 2, 0, 1))
     fin = (fin_near, fin_far)
     dq, part = call_stage(1, cp, (), fin, (slot1, slot2), rows, kept)
-    back_b = chip_permute(part, (None, 0, 1, 2), (None, 2, 3, 0))
+    back_b = chip_permute(part, (None, 0, 1, 2), (1, 2, None, 0))
     dq, part = call_stage(2, cp, dq, fin, (slot3, slot1), rows, kept)
-    back_c = chip_permute(part, (None, 2, 3, 0), (None, 0, 1, 2))
+    back_c = chip_permute(part, (1, 2, None, 0), (None, 0, 1, 2))
     dq, own = call_stage(3, cp, dq, fin, (kv, kv), rows, (*rows[4:], slot2, slot3, ds_near, ds_far))
 
     dq_other = core_swap(dq[1])

time: 47.2 us -> 47.2 us (level)
  waiting for transfers between devices: 17.2 us -> 13.9 us
  starting transfers between devices: 17.6 us -> 20.9 us
    ppermute x5, waiting for transfers between devices: 11.4 us -> 8.05 us  [chip_permute(): return lax.ppermute(array, 'cp', pairs)]
    ppermute x5, starting transfers between devices: 11.5 us -> 14.8 us  [chip_permute(): return lax.ppermute(array, 'cp', pairs)]
  transfers between devices with their start and end apart: 13 -> 13, of which waited for: 7 -> 6; matrix products, arithmetic and copies ran while one was open for 0% -> 0% of each run, Pallas kernels for 15% -> 15%
where the time goes in v9:
time: 47.2 us; the launch traced here: 47 us
  starting transfers between devices  20.9 us (44%)
  waiting for transfers between devices  13.9 us (29%)
  Pallas kernels  7.74 us (16%)
  local copies, waits for them, and re-layouts  2.58 us (5%)
  other arithmetic  1.07 us (2%)
  between operations  0.79 us (2%)
    ppermute x5, starting transfers between devices, chip_permute(): return lax.ppermute(array, 'cp', pairs)  14.8 us
    ppermute x5, waiting for transfers between devices, chip_permute(): return lax.ppermute(array, 'cp', pairs)  8.05 us
    ppermute x1, waiting for transfers between devices, hd_swap(): return lax.ppermute(array, 'hd', [(0, 1), (1, 0)])  5.06 us
    pallas_call x5, Pallas kernels, call_grads(): pl.pallas_call(kernel, out_shape=out, in_specs=[SM] + [VM] * len(args), o...  3.89 us
    ppermute x1, starting transfers between devices, hd_swap(): return lax.ppermute(array, 'hd', [(0, 1), (1, 0)])  3.28 us
    unnamed x6, local copies, waits for them, and re-layouts  2.58 us
    pallas_call x5, Pallas kernels, call_stats(): pl.pallas_call(functools.partial(stats_kernel, step, slot, groups), out_s...  2.11 us
    pallas_call x5, Pallas kernels, simple(): pl.pallas_call(kernel, out_shape=out, in_specs=[VM] * len(args), out_spec...  1.74 us
  transfers between devices with their start and end apart: 13, of which 6 were waited for; matrix products, arithmetic and copies ran while one was open for 0% of the time, Pallas kernels for 15%

profile of v9, /device:TPU:0, one launch (start us, length us, event | category | flops | bytes accessed | tf_op | source)
XLA Modules:
  0.0 47.0 jit_solution(2869243059017509760)
XLA Ops:
  0.6 1.1 %broadcast_select_fusion.refs_0_.refs_1_.refs_4_.refs_5_ = bf16[2,512,128]{2,1,0:T(8,128)(2,1)S(1)} fusion(pred[2]{0:T(512)(128)(4,1)S(1)} %iota_compare_fusion, bf16[512,128]{1,0:T(8,128)(2,1)} %param.7, bf16[512,128]{1,0:T(8,128)(2,1)} %param.6), kind=kLoop, calls=%fused_computation | loop fusion | flops 131072 | bytes 524290 | tf_op jit(solution)/shard_map/jit(_where)/select_n | solution.py:318
  1.7 0.1 collective-permute-start.1
  1.8 0.5 %collective-permute-start.2 = (bf16[512,256]{1,0:T(8,128)(2,1)}, bf16[512,256]{1,0:T(8,128)(2,1)S(1)}, u32[]{:S(2)}, u32[]{:S(2)}) collective-permute-start(bf16[512,256]{1,0:T(8,128)(2,1)} %refs_2_.1), channel_id=1, source_target_pairs={{0,2},{2,0},{4,6},{6,4},{8,10},{10,8},{12,14},{14,12},{16,18},{18,... | collective-permute-start | bytes 786440 | tf_op jit(solution)/shard_map/ppermute | solution.py:44
  2.3 1.6 %collective-permute-start = (bf16[2,512,128]{2,1,0:T(8,128)(2,1)S(1)}, bf16[2,512,128]{2,1,0:T(8,128)(2,1)S(1)}, u32[]{:S(2)}, u32[]{:S(2)}) collective-permute-start(bf16[2,512,128]{2,1,0:T(8,128)(2,1)S(1)} %broadcast_select_fusion.refs_0_.refs_1_.refs_4_.refs_5_), channel_id=1, source_target_pairs={{0,4},{2,6},{4,8},{6,10},{8,12},{10,14},{12,0},{14,2},{16,20},{18,... | collective-permute-start | bytes 786440 | tf_op jit(solution)/shard_map/ppermute | solution.py:32
  3.9 2.7 %collective-permute-start.4 = (bf16[2,512,128]{2,1,0:T(8,128)(2,1)S(1)}, bf16[2,512,128]{2,1,0:T(8,128)(2,1)S(1)}, u32[]{:S(2)}, u32[]{:S(2)}) collective-permute-start(bf16[2,512,128]{2,1,0:T(8,128)(2,1)S(1)} %broadcast_select_fusion.refs_0_.refs_1_.refs_4_.refs_5_), channel_id=1, source_target_pairs={{0,8},{2,14},{4,12},{6,2},{8,0},{10,6},{12,4},{14,10},{16,24},{18,... | collective-permute-start | bytes 786440 | tf_op jit(solution)/shard_map/ppermute | solution.py:39
  6.6 1.4 %collective-permute-start.5 = (bf16[2,512,128]{2,1,0:T(8,128)(2,1)S(1)}, bf16[2,512,128]{2,1,0:T(8,128)(2,1)S(1)}, u32[]{:S(2)}, u32[]{:S(2)}) collective-permute-start(bf16[2,512,128]{2,1,0:T(8,128)(2,1)S(1)} %broadcast_select_fusion.refs_0_.refs_1_.refs_4_.refs_5_), channel_id=1, source_target_pairs={{0,12},{2,10},{4,0},{6,14},{8,4},{10,2},{12,8},{14,6},{16,28},{18,... | collective-permute-start | bytes 786440 | tf_op jit(solution)/shard_map/ppermute | solution.py:39
  8.0 0.0 collective-permute-done.1.refs_4_.refs_5_.refs_2_.refs_7_
  8.0 0.0 collective-permute-start.3
  8.0 0.0 copy-start
  8.0 0.9 %copy-done = bf16[512,256]{1,0:T(8,128)(2,1)S(1)} copy-done((bf16[512,256]{1,0:T(8,128)(2,1)S(1)}, bf16[512,256]{1,0:T(8,128)(2,1)}, u32[]{:S(2)}) %copy-start) | copy-done | bytes 262168
  9.0 0.0 copy-start.1
  9.0 0.9 %copy-done.1 = bf16[512,256]{1,0:T(8,128)(2,1)S(1)} copy-done((bf16[512,256]{1,0:T(8,128)(2,1)S(1)}, bf16[512,256]{1,0:T(8,128)(2,1)}, u32[]{:S(2)}) %copy-start.1) | copy-done | bytes 262168
  9.9 0.0 copy-start.2
  9.9 0.7 %copy-done.2 = s32[512]{0:T(512)S(1)} copy-done((s32[512]{0:T(512)S(1)}, s32[512]{0:T(512)}, u32[]{:S(2)}) %copy-start.2) | copy-done | bytes 2072
  10.6 1.2 %stats.5 = (f32[12,512]{1,0:T(8,128)S(1)}, bf16[512,256]{1,0:T(8,128)(2,1)S(1)}, bf16[512,256]{1,0:T(8,128)(2,1)S(1)}, s32[1,512]{1,0:T(1,128)S(1)}) custom-call(s32[1]{0:T(128)} %bitcast.pos_ref, bf16[2,512,128]{2,1,0:T(8,128)(2,1)S(1)} %broadcast_select_fusion.refs_0_.refs_1_.refs_4_.refs_5_, bf16[512,256]{1,0:T(8,128)(2,1)S(1)} %copy-done, ...), custom_call_target="tpu_custom_call" | custom-call | bytes 1024 | tf_op jit(solution)/shard_map/stats/pallas_call | solution.py:268
  11.8 0.0 collective-permute-done.2.refs_6_.refs_7_.refs_3_.refs_9_
  11.8 0.0 collective-permute-done.refs_2_.refs_5_
  11.8 0.0 collective-permute-done.3.refs_8_.refs_9_.refs_11_
  11.8 0.9 %stats.6 = (f32[12,512]{1,0:T(8,128)S(1)}, f32[3,4,512,512]{3,2,1,0:T(8,128)S(1)}, f32[3,4,512,512]{3,2,1,0:T(8,128)S(1)}) custom-call(s32[1]{0:T(128)} %bitcast.pos_ref, f32[12,512]{1,0:T(8,128)S(1)} %get-tuple-element.44.refs_0_, bf16[2,512,128]{2,1,0:T(8,128)(2,1)S(1)} %broadcast_select_fusion.refs_0_.refs_1_.refs_4_.refs_5_, ...), custom_call_target="tpu_custom_call" | custom-call | bytes 1024 | tf_op jit(solution)/shard_map/stats/pallas_call | solution.py:268
  12.8 5.7 %collective-permute-done.4.refs_3_.refs_12_ = bf16[2,512,128]{2,1,0:T(8,128)(2,1)S(1)} collective-permute-done((bf16[2,512,128]{2,1,0:T(8,128)(2,1)S(1)}, bf16[2,512,128]{2,1,0:T(8,128)(2,1)S(1)}, u32[]{:S(2)}, u32[]{:S(2)}) %collective-permute-start.4) | collective-permute-done | bytes 262176 | tf_op jit(solution)/shard_map/ppermute | solution.py:39
  18.5 0.0 collective-permute-done.5.refs_3_.refs_4_.refs_13_
  18.5 0.1 collective-permute-start.6
  18.6 0.5 %collective-permute-start.7 = (f32[6,512]{1,0:T(8,128)S(1)}, f32[6,512]{1,0:T(8,128)S(1)}, u32[]{:S(2)}, u32[]{:S(2)}) collective-permute-start(f32[6,512]{1,0:T(8,128)S(1)} %get-tuple-element.60.refs_0_), channel_id=1, source_target_pairs={{0,2},{2,0},{4,6},{6,4},{8,10},{10,8},{12,14},{14,12},{16,18},{18,... | collective-permute-start | bytes 36872 | tf_op jit(solution)/shard_map/ppermute | solution.py:44
  19.1 0.7 %collective-permute-done.6.refs_1_ = f32[6,512]{1,0:T(8,128)S(1)} collective-permute-done((f32[6,512]{1,0:T(8,128)S(1)}, f32[6,512]{1,0:T(8,128)S(1)}, u32[]{:S(2)}, u32[]{:S(2)}) %collective-permute-start.6) | collective-permute-done | bytes 12320 | tf_op jit(solution)/shard_map/ppermute | solution.py:44
  19.8 0.1 collective-permute-done.7.refs_2_
  20.0 0.1 grads.6
  20.0 4.8 %collective-permute-start.9 = (bf16[2,512,128]{2,1,0:T(8,128)(2,1)S(1)}, bf16[2,512,128]{2,1,0:T(8,128)(2,1)S(1)}, u32[]{:S(2)}, u32[]{:S(2)}) collective-permute-start(bf16[2,512,128]{2,1,0:T(8,128)(2,1)S(1)} %get-tuple-element.77), channel_id=1, source_target_pairs={{0,12},{2,14},{4,8},{6,10},{8,0},{10,2},{12,4},{14,6},{16,28},{18,... | collective-permute-start | bytes 786440 | tf_op jit(solution)/shard_map/ppermute | solution.py:39
  24.8 0.3 grads.7
  25.1 1.3 %collective-permute-start.10 = (bf16[2,512,128]{2,1,0:T(8,128)(2,1)S(1)}, bf16[2,512,128]{2,1,0:T(8,128)(2,1)S(1)}, u32[]{:S(2)}, u32[]{:S(2)}) collective-permute-start(bf16[2,512,128]{2,1,0:T(8,128)(2,1)S(1)} %get-tuple-element.78), channel_id=1, source_target_pairs={{2,6},{4,0},{6,10},{8,4},{12,8},{14,2},{18,22},{20,16},{22,26},{24... | collective-permute-start | bytes 786440 | tf_op jit(solution)/shard_map/ppermute | solution.py:39
  26.4 0.2 grads.8
  26.6 4.6 %collective-permute-start.11 = (bf16[2,512,128]{2,1,0:T(8,128)(2,1)S(1)}, bf16[2,512,128]{2,1,0:T(8,128)(2,1)S(1)}, u32[]{:S(2)}, u32[]{:S(2)}) collective-permute-start(bf16[2,512,128]{2,1,0:T(8,128)(2,1)S(1)} %get-tuple-element.79), channel_id=1, source_target_pairs={{0,4},{4,8},{6,2},{10,6},{12,0},{14,10},{16,20},{20,24},{22,18},{2... | collective-permute-start | bytes 786440 | tf_op jit(solution)/shard_map/ppermute | solution.py:39
  31.2 3.3 %grads.9 = (f32[256,512]{1,0:T(8,128)S(1)}, f32[256,512]{1,0:T(8,128)S(1)}, f32[2,512,128]{2,1,0:T(8,128)S(1)}) custom-call(s32[1]{0:T(128)} %bitcast.pos_ref, f32[256,512]{1,0:T(8,128)S(1)} %get-tuple-element.69.refs_0_, f32[256,512]{1,0:T(8,128)S(1)} %get-tuple-element.70.refs_1_, f32[4,512]{1,0:T(4,128)S(1)} %get-tuple-element.65.refs_0_.refs_2_, ...), custom_call_target="tpu_custom_call" | custom-call | bytes 1024 | tf_op jit(solution)/shard_map/grads/pallas_call | solution.py:281
  34.5 0.1 collective-permute-start.8
  34.6 0.0 collective-permute-done.9.part
  34.6 0.4 collective-permute-done.10.part
  35.1 1.9 %collective-permute-done.11.part = bf16[2,512,128]{2,1,0:T(8,128)(2,1)S(1)} collective-permute-done((bf16[2,512,128]{2,1,0:T(8,128)(2,1)S(1)}, bf16[2,512,128]{2,1,0:T(8,128)(2,1)S(1)}, u32[]{:S(2)}, u32[]{:S(2)}) %collective-permute-start.11) | collective-permute-done | bytes 262176 | tf_op jit(solution)/shard_map/ppermute | solution.py:39
  37.0 0.1 shard_map.79.mine
  37.0 3.3 %collective-permute-start.12 = (bf16[2,512,128]{2,1,0:T(8,128)(2,1)S(1)}, bf16[2,512,128]{2,1,0:T(8,128)(2,1)S(1)}, u32[]{:S(2)}, u32[]{:S(2)}) collective-permute-start(bf16[2,512,128]{2,1,0:T(8,128)(2,1)S(1)} %shard_map.79.mine), channel_id=1, source_target_pairs={{0,1},{1,0},{2,3},{3,2},{4,5},{5,4},{6,7},{7,6},{8,9},{9,8},{10,11... | collective-permute-start | bytes 786440 | tf_op jit(solution)/shard_map/ppermute | solution.py:48
  40.3 0.0 collective-permute-done.8.other
  40.3 0.8 %shard_map.76 = (bf16[512,256]{1,0:T(8,128)(2,1)}, f32[8,128]{1,0:T(8,128)S(1)}) custom-call(f32[256,512]{1,0:T(8,128)S(1)} %get-tuple-element.73.mine, f32[256,512]{1,0:T(8,128)S(1)} %collective-permute-done.8.other), custom_call_target="tpu_custom_call" | custom-call | bytes 1024 | tf_op jit(solution)/shard_map/pallas_call | solution.py:248
  41.2 5.1 %collective-permute-done.12.other = bf16[2,512,128]{2,1,0:T(8,128)(2,1)S(1)} collective-permute-done((bf16[2,512,128]{2,1,0:T(8,128)(2,1)S(1)}, bf16[2,512,128]{2,1,0:T(8,128)(2,1)S(1)}, u32[]{:S(2)}, u32[]{:S(2)}) %collective-permute-start.12) | collective-permute-done | bytes 262176 | tf_op jit(solution)/shard_map/ppermute | solution.py:48
  46.2 0.7 %shard_map.80 = (bf16[512,128]{1,0:T(8,128)(2,1)}, bf16[512,128]{1,0:T(8,128)(2,1)}) custom-call(bf16[2,512,128]{2,1,0:T(8,128)(2,1)S(1)} %shard_map.79.mine, bf16[2,512,128]{2,1,0:T(8,128)(2,1)S(1)} %collective-permute-done.12.other, f32[8,128]{1,0:T(8,128)S(1)} %get-tuple-element.80._), custom_call_target="tpu_custom_call" | custom-call | bytes 1024 | tf_op jit(solution)/shard_map/pallas_call | solution.py:248
  (7 shorter events, 0.2 us)
Async XLA Ops:
  1.7 6.3 %collective-permute-start.1 = (bf16[512,256]{1,0:T(8,128)(2,1)}, bf16[512,256]{1,0:T(8,128)(2,1)S(1)}, u32[]{:S(2)}, u32[]{:S(2)}) collective-permute-start(bf16[512,256]{1,0:T(8,128)(2,1)} %refs_1_.1), channel_id=1, source_target_pairs={{0,2},{2,0},{4,6},{6,4},{8,10},{10,8},{12,14},{14,12},{16,18},{18,... | collective-permute-start | bytes 786440 | tf_op jit(solution)/shard_map/ppermute | solution.py:44
  1.8 10.0 %collective-permute-start.2 = (bf16[512,256]{1,0:T(8,128)(2,1)}, bf16[512,256]{1,0:T(8,128)(2,1)S(1)}, u32[]{:S(2)}, u32[]{:S(2)}) collective-permute-start(bf16[512,256]{1,0:T(8,128)(2,1)} %refs_2_.1), channel_id=1, source_target_pairs={{0,2},{2,0},{4,6},{6,4},{8,10},{10,8},{12,14},{14,12},{16,18},{18,... | collective-permute-start | bytes 786440 | tf_op jit(solution)/shard_map/ppermute | solution.py:44
  2.3 9.5 %collective-permute-start = (bf16[2,512,128]{2,1,0:T(8,128)(2,1)S(1)}, bf16[2,512,128]{2,1,0:T(8,128)(2,1)S(1)}, u32[]{:S(2)}, u32[]{:S(2)}) collective-permute-start(bf16[2,512,128]{2,1,0:T(8,128)(2,1)S(1)} %broadcast_select_fusion.refs_0_.refs_1_.refs_4_.refs_5_), channel_id=1, source_target_pairs={{0,4},{2,6},{4,8},{6,10},{8,12},{10,14},{12,0},{14,2},{16,20},{18,... | collective-permute-start | bytes 786440 | tf_op jit(solution)/shard_map/ppermute | solution.py:32
  3.9 14.6 %collective-permute-start.4 = (bf16[2,512,128]{2,1,0:T(8,128)(2,1)S(1)}, bf16[2,512,128]{2,1,0:T(8,128)(2,1)S(1)}, u32[]{:S(2)}, u32[]{:S(2)}) collective-permute-start(bf16[2,512,128]{2,1,0:T(8,128)(2,1)S(1)} %broadcast_select_fusion.refs_0_.refs_1_.refs_4_.refs_5_), channel_id=1, source_target_pairs={{0,8},{2,14},{4,12},{6,2},{8,0},{10,6},{12,4},{14,10},{16,24},{18,... | collective-permute-start | bytes 786440 | tf_op jit(solution)/shard_map/ppermute | solution.py:39
  6.6 11.9 %collective-permute-start.5 = (bf16[2,512,128]{2,1,0:T(8,128)(2,1)S(1)}, bf16[2,512,128]{2,1,0:T(8,128)(2,1)S(1)}, u32[]{:S(2)}, u32[]{:S(2)}) collective-permute-start(bf16[2,512,128]{2,1,0:T(8,128)(2,1)S(1)} %broadcast_select_fusion.refs_0_.refs_1_.refs_4_.refs_5_), channel_id=1, source_target_pairs={{0,12},{2,10},{4,0},{6,14},{8,4},{10,2},{12,8},{14,6},{16,28},{18,... | collective-permute-start | bytes 786440 | tf_op jit(solution)/shard_map/ppermute | solution.py:39
  8.0 3.8 %collective-permute-start.3 = (s32[1,512]{1,0:T(1,128)}, s32[1,512]{1,0:T(1,128)S(1)}, u32[]{:S(2)}, u32[]{:S(2)}) collective-permute-start(s32[1,512]{1,0:T(1,128)} %bitcast.2), channel_id=1, source_target_pairs={{0,2},{2,0},{4,6},{6,4},{8,10},{10,8},{12,14},{14,12},{16,18},{18,... | collective-permute-start | bytes 6152 | tf_op jit(solution)/shard_map/ppermute | solution.py:44
  8.0 1.0 %copy-start = (bf16[512,256]{1,0:T(8,128)(2,1)S(1)}, bf16[512,256]{1,0:T(8,128)(2,1)}, u32[]{:S(2)}) copy-start(bf16[512,256]{1,0:T(8,128)(2,1)} %refs_1_.1) | copy-start | bytes 786436
  9.0 0.9 %copy-start.1 = (bf16[512,256]{1,0:T(8,128)(2,1)S(1)}, bf16[512,256]{1,0:T(8,128)(2,1)}, u32[]{:S(2)}) copy-start(bf16[512,256]{1,0:T(8,128)(2,1)} %refs_2_.1) | copy-start | bytes 786436
  9.9 0.7 %copy-start.2 = (s32[512]{0:T(512)S(1)}, s32[512]{0:T(512)}, u32[]{:S(2)}) copy-start(s32[512]{0:T(512)} %param.9) | copy-start | bytes 6148
  18.5 1.3 %collective-permute-start.6 = (f32[6,512]{1,0:T(8,128)S(1)}, f32[6,512]{1,0:T(8,128)S(1)}, u32[]{:S(2)}, u32[]{:S(2)}) collective-permute-start(f32[6,512]{1,0:T(8,128)S(1)} %get-tuple-element.61.refs_1_), channel_id=1, source_target_pairs={{0,2},{2,0},{4,6},{6,4},{8,10},{10,8},{12,14},{14,12},{16,18},{18,... | collective-permute-start | bytes 36872 | tf_op jit(solution)/shard_map/ppermute | solution.py:44
  18.6 1.3 %collective-permute-start.7 = (f32[6,512]{1,0:T(8,128)S(1)}, f32[6,512]{1,0:T(8,128)S(1)}, u32[]{:S(2)}, u32[]{:S(2)}) collective-permute-start(f32[6,512]{1,0:T(8,128)S(1)} %get-tuple-element.60.refs_0_), channel_id=1, source_target_pairs={{0,2},{2,0},{4,6},{6,4},{8,10},{10,8},{12,14},{14,12},{16,18},{18,... | collective-permute-start | bytes 36872 | tf_op jit(solution)/shard_map/ppermute | solution.py:44
  20.0 14.5 %collective-permute-start.9 = (bf16[2,512,128]{2,1,0:T(8,128)(2,1)S(1)}, bf16[2,512,128]{2,1,0:T(8,128)(2,1)S(1)}, u32[]{:S(2)}, u32[]{:S(2)}) collective-permute-start(bf16[2,512,128]{2,1,0:T(8,128)(2,1)S(1)} %get-tuple-element.77), channel_id=1, source_target_pairs={{0,12},{2,14},{4,8},{6,10},{8,0},{10,2},{12,4},{14,6},{16,28},{18,... | collective-permute-start | bytes 786440 | tf_op jit(solution)/shard_map/ppermute | solution.py:39
  25.1 9.9 %collective-permute-start.10 = (bf16[2,512,128]{2,1,0:T(8,128)(2,1)S(1)}, bf16[2,512,128]{2,1,0:T(8,128)(2,1)S(1)}, u32[]{:S(2)}, u32[]{:S(2)}) collective-permute-start(bf16[2,512,128]{2,1,0:T(8,128)(2,1)S(1)} %get-tuple-element.78), channel_id=1, source_target_pairs={{2,6},{4,0},{6,10},{8,4},{12,8},{14,2},{18,22},{20,16},{22,26},{24... | collective-permute-start | bytes 786440 | tf_op jit(solution)/shard_map/ppermute | solution.py:39
  26.6 10.4 %collective-permute-start.11 = (bf16[2,512,128]{2,1,0:T(8,128)(2,1)S(1)}, bf16[2,512,128]{2,1,0:T(8,128)(2,1)S(1)}, u32[]{:S(2)}, u32[]{:S(2)}) collective-permute-start(bf16[2,512,128]{2,1,0:T(8,128)(2,1)S(1)} %get-tuple-element.79), channel_id=1, source_target_pairs={{0,4},{4,8},{6,2},{10,6},{12,0},{14,10},{16,20},{20,24},{22,18},{2... | collective-permute-start | bytes 786440 | tf_op jit(solution)/shard_map/ppermute | solution.py:39
  34.5 5.9 %collective-permute-start.8 = (f32[256,512]{1,0:T(8,128)S(1)}, f32[256,512]{1,0:T(8,128)S(1)}, u32[]{:S(2)}, u32[]{:S(2)}) collective-permute-start(f32[256,512]{1,0:T(8,128)S(1)} %get-tuple-element.74), channel_id=1, source_target_pairs={{0,2},{2,0},{4,6},{6,4},{8,10},{10,8},{12,14},{14,12},{16,18},{18,... | collective-permute-start | bytes 1572872 | tf_op jit(solution)/shard_map/ppermute | solution.py:44
  37.0 9.2 %collective-permute-start.12 = (bf16[2,512,128]{2,1,0:T(8,128)(2,1)S(1)}, bf16[2,512,128]{2,1,0:T(8,128)(2,1)S(1)}, u32[]{:S(2)}, u32[]{:S(2)}) collective-permute-start(bf16[2,512,128]{2,1,0:T(8,128)(2,1)S(1)} %shard_map.79.mine), channel_id=1, source_target_pairs={{0,1},{1,0},{2,3},{3,2},{4,5},{5,4},{6,7},{7,6},{8,9},{9,8},{10,11... | collective-permute-start | bytes 786440 | tf_op jit(solution)/shard_map/ppermute | solution.py:48
